TPU v7x, 32 devices: a whole 2x2x4 slice. The times are simulated.
32 devices in a mesh: section: 2 (over x), shard: 4 (over z), replica: 4 (over y, core).
Axes of the slice: x: 2, y: 2, z: 4, core: 2. Of those that a mesh axis runs over, the one named last changes fastest.
Arguments:
- tokens: bfloat16 [16384, 768], P(('shard', 'replica')), may hold values from -6 to 6
- cotangent: bfloat16 [16384, 768], P(('shard', 'replica')), may hold values from -6 to 6
- lengths: int32 [32, 4], replicated, may hold values from 0 to 512, as said below
- assignment: int32 [32], replicated, may hold values from 0 to 31, each once
- attention_gain: bfloat16 [2, 768], P('section', 'shard'), may hold values from 0.25 to 1.75
- attention_shift: bfloat16 [2, 768], P('section', 'shard'), may hold values from -2 to 2
- input_weight: bfloat16 [2, 768, 2304], P('section', 'shard'), may hold values from -0.21875 to 0.21875
- query_bias: bfloat16 [2, 768], P('section', 'shard'), may hold values from -2 to 2
- value_bias: bfloat16 [2, 768], P('section', 'shard'), may hold values from -2 to 2
- output_weight: bfloat16 [2, 768, 768], P('section', 'shard'), may hold values from -0.625 to 0.625
- output_bias: bfloat16 [2, 768], P('section', 'shard'), may hold values from -2 to 2
- feedforward_gain: bfloat16 [2, 768], P('section', 'shard'), may hold values from 0.25 to 1.75
- feedforward_shift: bfloat16 [2, 768], P('section', 'shard'), may hold values from -2 to 2
- expand_weight: bfloat16 [2, 768, 3072], P('section', 'shard'), may hold values from -0.21875 to 0.21875
- expand_bias: bfloat16 [2, 3072], P('section', 'shard'), may hold values from -2 to 2
- contract_weight: bfloat16 [2, 3072, 768], P('section', 'shard'), may hold values from -0.15625 to 0.15625
- contract_bias: bfloat16 [2, 768], P('section', 'shard'), may hold values from -2 to 2
Outputs:
- block_outputs: bfloat16 [2, 16384, 768], P('section', ('shard', 'replica'))
- input_grads: float32 [2, 16384, 768], P('section', ('shard', 'replica'))
- attention_gain_gradient: float32 [2, 768], P('section', 'shard')
- attention_shift_gradient: float32 [2, 768], P('section', 'shard')
- input_weight_gradient: float32 [2, 768, 2304], P('section', 'shard')
- query_bias_gradient: float32 [2, 768], P('section', 'shard')
- value_bias_gradient: float32 [2, 768], P('section', 'shard')
- output_weight_gradient: float32 [2, 768, 768], P('section', 'shard')
- output_bias_gradient: float32 [2, 768], P('section', 'shard')
- feedforward_gain_gradient: float32 [2, 768], P('section', 'shard')
- feedforward_shift_gradient: float32 [2, 768], P('section', 'shard')
- expand_weight_gradient: float32 [2, 768, 3072], P('section', 'shard')
- expand_bias_gradient: float32 [2, 3072], P('section', 'shard')
- contract_weight_gradient: float32 [2, 3072, 768], P('section', 'shard')
- contract_bias_gradient: float32 [2, 768], P('section', 'shard')
Inputs may be any that keep to these rules, and one draw needn't show every extreme that they name: `lengths`: row g lists the token counts of group g's 4 sequences in order, zero for an empty entry; each row sums to at most 512, and some row holds a single sequence of 512 tokens. `assignment`: every slot receives exactly one group.
All inputs are finite; a program needn't handle non-finite values.
Results may differ from a plain program's by a relative error of at most 0.022.
Values may be sent and summed in bfloat16 or wider, within the bound.
No kernel may reach another device: no remote copies, remote signals or barrier semaphores. Data moves between devices by JAX's collectives and lax.ppermute only.
A program may use at most 448 MiB of HBM per device.

v0:
```python
import jax
import jax.numpy as jnp
from jax import lax
from jax.sharding import PartitionSpec as P

HEADS = 12
ROWS = 512
MICRO = 2


EPSILON = 1e-05
MASKED_SCORE = -1e30


def from_behind(block, axis, distance):
    devices = range(lax.axis_size(axis))
    route = [(i - distance, i) for i in devices if i - distance in devices]
    return lax.ppermute(block, axis, route)


def layer_norm(hidden, norm_gain, norm_shift):
    center = hidden - jnp.mean(hidden, axis=-1, keepdims=True)
    spread = jnp.mean(center * center, axis=-1, keepdims=True)
    return center * lax.rsqrt(spread + EPSILON) * norm_gain + norm_shift


def slot_layout(counts, row_count):
    bounds = jnp.cumsum(counts, dtype=jnp.int32)
    places = jnp.arange(row_count, dtype=jnp.int32)
    segment = jnp.sum(
        (bounds[None, :] <= places[:, None]).astype(jnp.int32), axis=1, dtype=jnp.int32
    )
    living = (places < bounds[-1]).astype(jnp.float32)
    return (segment, living)


def gelu_tanh(values):
    return jax.nn.gelu(values, approximate=True)


def contract_rows(left_side, right_side):
    return lax.dot_general(
        left_side, right_side, (((0,), (0,)), ((), ())), preferred_element_type=jnp.float32
    )


def times_transpose(left_side, right_side):
    return lax.dot_general(
        left_side, right_side, (((1,), (1,)), ((), ())), preferred_element_type=jnp.float32
    )


def split_heads(joint_low):
    row_count, three_width = joint_low.shape
    model_width = three_width // 3
    shaped = joint_low.reshape(row_count, 3, HEADS, model_width // HEADS)
    return (shaped[:, 0], shaped[:, 1], shaped[:, 2])


def masked_scores(block_queries, keys_all, segment, first_row, score_scale):
    block_count = block_queries.shape[0]
    scores = (
        jnp.einsum("qhd,khd->hqk", block_queries, keys_all, preferred_element_type=jnp.float32)
        * score_scale
    )
    query_places = first_row + jnp.arange(block_count, dtype=jnp.int32)
    key_places = jnp.arange(keys_all.shape[0], dtype=jnp.int32)
    same_segment = segment[first_row : first_row + block_count, None] == segment[None, :]
    allowed = same_segment & (key_places[None, :] <= query_places[:, None])
    return jnp.where(allowed[None], scores, MASKED_SCORE)


def attend_forward(joint_low, segment):
    queries, keys_all, values = split_heads(joint_low)
    row_count, head_count, head_dim = queries.shape
    score_scale = head_dim ** (-0.5)
    scores = masked_scores(queries, keys_all, segment, 0, score_scale)
    row_max = jnp.max(scores, axis=-1, keepdims=True)
    exponent = jnp.exp(scores - row_max)
    row_total = jnp.sum(exponent, axis=-1, keepdims=True)
    probabilities = (exponent / row_total).astype(jnp.bfloat16)
    outputs = [
        jnp.einsum("hqk,khd->qhd", probabilities, values, preferred_element_type=jnp.float32)
    ]
    log_parts = [(row_max + jnp.log(row_total))[:, :, 0]]
    mixed = jnp.concatenate(outputs, axis=0).reshape(row_count, head_count * head_dim)
    return (mixed, jnp.concatenate(log_parts, axis=1))


def attend_backward(joint_low, log_sums, mixed_grad, segment):
    queries, keys_all, values = split_heads(joint_low)
    row_count, head_count, head_dim = queries.shape
    model_width = head_count * head_dim
    score_scale = head_dim ** (-0.5)
    block_rows = min(512, row_count)
    grad_heads = mixed_grad.reshape(row_count, head_count, head_dim)
    key_grad = jnp.zeros((row_count, head_count, head_dim), jnp.float32)
    value_grad = jnp.zeros((row_count, head_count, head_dim), jnp.float32)
    scores = masked_scores(queries, keys_all, segment, 0, score_scale)
    probabilities = jnp.exp(scores - log_sums[:, 0:block_rows, None])
    probs_low = probabilities.astype(jnp.bfloat16)
    value_grad = value_grad + jnp.einsum(
        "hqk,qhd->khd", probs_low, grad_heads, preferred_element_type=jnp.float32
    )
    prob_grad = jnp.einsum("qhd,khd->hqk", grad_heads, values, preferred_element_type=jnp.float32)
    centered = prob_grad - jnp.sum(prob_grad * probabilities, axis=-1, keepdims=True)
    score_grad = (probabilities * centered).astype(jnp.bfloat16)
    query_parts = [
        jnp.einsum("hqk,khd->qhd", score_grad, keys_all, preferred_element_type=jnp.float32)
        * score_scale
    ]
    key_grad = (
        key_grad
        + jnp.einsum("hqk,qhd->khd", score_grad, queries, preferred_element_type=jnp.float32)
        * score_scale
    )
    query_grad = jnp.concatenate(query_parts, axis=0).reshape(row_count, model_width)
    return jnp.concatenate(
        [
            query_grad,
            key_grad.reshape(row_count, model_width),
            value_grad.reshape(row_count, model_width),
        ],
        axis=1,
    )


def block_forward(params_here, hidden_low, segment, living):
    (
        attention_gain,
        attention_shift,
        input_weight,
        query_bias,
        value_bias,
        output_weight,
        output_bias,
        feedforward_gain,
        feedforward_shift,
        expand_weight,
        expand_bias,
        contract_weight,
        contract_bias,
    ) = params_here
    hidden = hidden_low.astype(jnp.float32)
    normed = layer_norm(hidden, attention_gain, attention_shift).astype(jnp.bfloat16)
    joint_bias = jnp.concatenate([query_bias, jnp.zeros_like(query_bias), value_bias])
    joint_low = (
        jnp.dot(normed, input_weight, preferred_element_type=jnp.float32) + joint_bias
    ).astype(jnp.bfloat16)
    mixed, log_sums = attend_forward(joint_low, segment)
    mixed_low = mixed.astype(jnp.bfloat16)
    middle = (
        hidden + jnp.dot(mixed_low, output_weight, preferred_element_type=jnp.float32) + output_bias
    )
    normed_two = layer_norm(middle, feedforward_gain, feedforward_shift).astype(jnp.bfloat16)
    expanded = jnp.dot(normed_two, expand_weight, preferred_element_type=jnp.float32) + expand_bias
    activated = gelu_tanh(expanded).astype(jnp.bfloat16)
    result = (
        middle
        + jnp.dot(activated, contract_weight, preferred_element_type=jnp.float32)
        + contract_bias
    )
    result = result * living[:, None]
    return (
        result.astype(jnp.bfloat16),
        (hidden_low, joint_low, log_sums, mixed_low, middle, expanded),
    )


def back_late(params_here, kept_state, upstream, living):
    (
        attention_gain,
        attention_shift,
        input_weight,
        query_bias,
        value_bias,
        output_weight,
        output_bias,
        feedforward_gain,
        feedforward_shift,
        expand_weight,
        expand_bias,
        contract_weight,
        contract_bias,
    ) = params_here
    hidden_low, joint_low, log_sums, mixed_low, middle, expanded = kept_state
    out_grad = upstream * living[:, None]
    contract_grad_low = out_grad.astype(jnp.bfloat16)
    activated, gelu_pull = jax.vjp(gelu_tanh, expanded)
    activated_low = activated.astype(jnp.bfloat16)
    contract_weight_grad = contract_rows(activated_low, contract_grad_low)
    contract_bias_grad = jnp.sum(contract_grad_low.astype(jnp.float32), axis=0)
    activated_grad = times_transpose(contract_grad_low, contract_weight)
    (expanded_grad,) = gelu_pull(activated_grad)
    expanded_grad_low = expanded_grad.astype(jnp.bfloat16)
    normed_two, norm_two_pull = jax.vjp(layer_norm, middle, feedforward_gain, feedforward_shift)
    expand_weight_grad = contract_rows(normed_two.astype(jnp.bfloat16), expanded_grad_low)
    expand_bias_grad = jnp.sum(expanded_grad_low.astype(jnp.float32), axis=0)
    normed_two_grad = times_transpose(expanded_grad_low, expand_weight)
    middle_norm_grad, feedforward_gain_grad, feedforward_shift_grad = norm_two_pull(normed_two_grad)
    middle_grad = out_grad + middle_norm_grad
    branch_grad_low = middle_grad.astype(jnp.bfloat16)
    output_weight_grad = contract_rows(mixed_low, branch_grad_low)
    output_bias_grad = jnp.sum(branch_grad_low.astype(jnp.float32), axis=0)
    mixed_grad_low = times_transpose(branch_grad_low, output_weight).astype(jnp.bfloat16)
    return (
        middle_grad,
        mixed_grad_low,
        (
            output_weight_grad,
            output_bias_grad,
            feedforward_gain_grad,
            feedforward_shift_grad,
            expand_weight_grad,
            expand_bias_grad,
            contract_weight_grad,
            contract_bias_grad,
        ),
    )


def back_early(params_here, kept_state, middle_grad, mixed_grad_low, segment):
    (
        attention_gain,
        attention_shift,
        input_weight,
        query_bias,
        value_bias,
        output_weight,
        output_bias,
        feedforward_gain,
        feedforward_shift,
        expand_weight,
        expand_bias,
        contract_weight,
        contract_bias,
    ) = params_here
    hidden_low, joint_low, log_sums, mixed_low, middle, expanded = kept_state
    model_width = middle.shape[1]
    joint_grad_low = attend_backward(joint_low, log_sums, mixed_grad_low, segment).astype(
        jnp.bfloat16
    )
    normed, norm_one_pull = jax.vjp(
        layer_norm, hidden_low.astype(jnp.float32), attention_gain, attention_shift
    )
    input_weight_grad = contract_rows(normed.astype(jnp.bfloat16), joint_grad_low)
    joint_sums = jnp.sum(joint_grad_low.astype(jnp.float32), axis=0)
    query_bias_grad = joint_sums[:model_width]
    value_bias_grad = joint_sums[2 * model_width :]
    normed_grad = times_transpose(joint_grad_low, input_weight)
    hidden_norm_grad, attention_gain_grad, attention_shift_grad = norm_one_pull(normed_grad)
    hidden_grad = middle_grad + hidden_norm_grad
    return (
        hidden_grad,
        (
            attention_gain_grad,
            attention_shift_grad,
            input_weight_grad,
            query_bias_grad,
            value_bias_grad,
        ),
    )


def block_backward(params_here, kept_state, upstream, segment, living):
    middle_grad, mixed_grad_low, late_grads = back_late(params_here, kept_state, upstream, living)
    hidden_grad, early_grads = back_early(
        params_here, kept_state, middle_grad, mixed_grad_low, segment
    )
    return (hidden_grad, early_grads + late_grads)


def prepare(gathered):
    return tuple(
        (member[0] if member.ndim == 3 else member[0].astype(jnp.float32) for member in gathered)
    )


def per_device(
    tokens,
    cotangent,
    lengths,
    assignment,
    attention_gain,
    attention_shift,
    input_weight,
    query_bias,
    value_bias,
    output_weight,
    output_bias,
    feedforward_gain,
    feedforward_shift,
    expand_weight,
    expand_bias,
    contract_weight,
    contract_bias,
):
    section_index = lax.axis_index("section")
    data_rank = lax.axis_index("shard") * lax.axis_size("replica") + lax.axis_index("replica")
    model_width = tokens.shape[1]
    expand_width = expand_weight.shape[2]
    gathered = (
        lax.all_gather(attention_gain, "shard", axis=1, tiled=True),
        lax.all_gather(attention_shift, "shard", axis=1, tiled=True),
        lax.all_gather(input_weight, "shard", axis=1, tiled=True),
        lax.all_gather(query_bias, "shard", axis=1, tiled=True),
        lax.all_gather(value_bias, "shard", axis=1, tiled=True),
        lax.all_gather(output_weight, "shard", axis=1, tiled=True),
        lax.all_gather(output_bias, "shard", axis=1, tiled=True),
        lax.all_gather(feedforward_gain, "shard", axis=1, tiled=True),
        lax.all_gather(feedforward_shift, "shard", axis=1, tiled=True),
        lax.all_gather(expand_weight, "shard", axis=1, tiled=True),
        lax.all_gather(expand_bias, "shard", axis=1, tiled=True),
        lax.all_gather(contract_weight, "shard", axis=1, tiled=True),
        lax.all_gather(contract_bias, "shard", axis=1, tiled=True),
    )
    params_here = prepare(gathered)
    slots_here = data_rank * MICRO + jnp.arange(MICRO, dtype=jnp.int32)
    matches = (assignment[None, :] == slots_here[:, None]).astype(jnp.int32)
    slot_counts = jnp.sum(matches[:, :, None] * lengths[None, :, :], axis=1, dtype=jnp.int32)
    segments, livings = jax.vmap(lambda counts: slot_layout(counts, ROWS))(slot_counts)

    def run_forward(hidden_low, segment, living):
        return block_forward(params_here, hidden_low, segment, living)

    def skip_forward(hidden_low, segment, living):
        return (
            jnp.zeros((ROWS, model_width), jnp.bfloat16),
            (
                jnp.zeros((ROWS, model_width), jnp.bfloat16),
                jnp.zeros((ROWS, 3 * model_width), jnp.bfloat16),
                jnp.zeros((HEADS, ROWS), jnp.float32),
                jnp.zeros((ROWS, model_width), jnp.bfloat16),
                jnp.zeros((ROWS, model_width), jnp.float32),
                jnp.zeros((ROWS, expand_width), jnp.float32),
            ),
        )

    received = jnp.zeros((ROWS, model_width), jnp.bfloat16)
    block_out = jnp.zeros((tokens.shape[0], model_width), jnp.bfloat16)
    kept_steps = []
    for step_index in range(MICRO + 1):
        micro_index = step_index - section_index
        active = (micro_index >= 0) & (micro_index < MICRO)
        position = jnp.clip(micro_index, 0, MICRO - 1)
        own_rows = lax.dynamic_slice_in_dim(tokens, position * ROWS, ROWS, 0)
        entering = jnp.where(section_index == 0, own_rows, received)
        segment = lax.dynamic_index_in_dim(segments, position, 0, keepdims=False)
        living = lax.dynamic_index_in_dim(livings, position, 0, keepdims=False)
        leaving, kept_state = lax.cond(active, run_forward, skip_forward, entering, segment, living)
        updated = lax.dynamic_update_slice_in_dim(block_out, leaving, position * ROWS, 0)
        block_out = jnp.where(active, updated, block_out)
        kept_steps.append(kept_state)
        if step_index < MICRO:
            received = from_behind(leaving, "section", 1)
    stacked = jax.tree.map(lambda *members: jnp.stack(members), *kept_steps)
    params_back = prepare(
        (
            lax.all_gather(attention_gain, "shard", axis=1, tiled=True),
            lax.all_gather(attention_shift, "shard", axis=1, tiled=True),
            lax.all_gather(input_weight, "shard", axis=1, tiled=True),
            lax.all_gather(query_bias, "shard", axis=1, tiled=True),
            lax.all_gather(value_bias, "shard", axis=1, tiled=True),
            lax.all_gather(output_weight, "shard", axis=1, tiled=True),
            lax.all_gather(output_bias, "shard", axis=1, tiled=True),
            lax.all_gather(feedforward_gain, "shard", axis=1, tiled=True),
            lax.all_gather(feedforward_shift, "shard", axis=1, tiled=True),
            lax.all_gather(expand_weight, "shard", axis=1, tiled=True),
            lax.all_gather(expand_bias, "shard", axis=1, tiled=True),
            lax.all_gather(contract_weight, "shard", axis=1, tiled=True),
            lax.all_gather(contract_bias, "shard", axis=1, tiled=True),
        )
    )

    def run_backward(kept_state, upstream, segment, living):
        return block_backward(params_back, kept_state, upstream, segment, living)

    def skip_backward(kept_state, upstream, segment, living):
        return (
            jnp.zeros((ROWS, model_width), jnp.float32),
            tuple((jnp.zeros(member.shape, jnp.float32) for member in params_back)),
        )

    full_totals = tuple((jnp.zeros(member.shape, jnp.float32) for member in params_back))
    received_grad = jnp.zeros((ROWS, model_width), jnp.bfloat16)
    grad_buffer = jnp.zeros((tokens.shape[0], model_width), jnp.float32)
    shard_totals = None
    for step_index in range(MICRO + 1):
        micro_index = step_index - 1 + section_index
        active = (micro_index >= 0) & (micro_index < MICRO)
        position = jnp.clip(micro_index, 0, MICRO - 1)
        kept_index = jnp.clip(micro_index + section_index, 0, MICRO)
        kept_state = jax.tree.map(
            lambda member: lax.dynamic_index_in_dim(member, kept_index, 0, keepdims=False), stacked
        )
        own_seed = lax.dynamic_slice_in_dim(cotangent, position * ROWS, ROWS, 0).astype(jnp.float32)
        upstream = jnp.where(section_index == 1, own_seed, received_grad.astype(jnp.float32))
        segment = lax.dynamic_index_in_dim(segments, position, 0, keepdims=False)
        living = lax.dynamic_index_in_dim(livings, position, 0, keepdims=False)
        entering_grad, step_grads = lax.cond(
            active, run_backward, skip_backward, kept_state, upstream, segment, living
        )
        full_totals = tuple((first + second for first, second in zip(full_totals, step_grads)))
        updated = lax.dynamic_update_slice_in_dim(grad_buffer, entering_grad, position * ROWS, 0)
        grad_buffer = jnp.where(active, updated, grad_buffer)
        if step_index < MICRO:
            received_grad = from_behind(entering_grad.astype(jnp.bfloat16), "section", -1)
    leading = tuple((member[None] for member in full_totals))
    shard_totals = (
        lax.psum_scatter(
            leading[0].astype(jnp.bfloat16), "shard", scatter_dimension=1, tiled=True
        ).astype(jnp.float32),
        lax.psum_scatter(
            leading[1].astype(jnp.bfloat16), "shard", scatter_dimension=1, tiled=True
        ).astype(jnp.float32),
        lax.psum_scatter(
            leading[2].astype(jnp.bfloat16), "shard", scatter_dimension=1, tiled=True
        ).astype(jnp.float32),
        lax.psum_scatter(
            leading[3].astype(jnp.bfloat16), "shard", scatter_dimension=1, tiled=True
        ).astype(jnp.float32),
        lax.psum_scatter(
            leading[4].astype(jnp.bfloat16), "shard", scatter_dimension=1, tiled=True
        ).astype(jnp.float32),
        lax.psum_scatter(
            leading[5].astype(jnp.bfloat16), "shard", scatter_dimension=1, tiled=True
        ).astype(jnp.float32),
        lax.psum_scatter(
            leading[6].astype(jnp.bfloat16), "shard", scatter_dimension=1, tiled=True
        ).astype(jnp.float32),
        lax.psum_scatter(
            leading[7].astype(jnp.bfloat16), "shard", scatter_dimension=1, tiled=True
        ).astype(jnp.float32),
        lax.psum_scatter(
            leading[8].astype(jnp.bfloat16), "shard", scatter_dimension=1, tiled=True
        ).astype(jnp.float32),
        lax.psum_scatter(
            leading[9].astype(jnp.bfloat16), "shard", scatter_dimension=1, tiled=True
        ).astype(jnp.float32),
        lax.psum_scatter(
            leading[10].astype(jnp.bfloat16), "shard", scatter_dimension=1, tiled=True
        ).astype(jnp.float32),
        lax.psum_scatter(
            leading[11].astype(jnp.bfloat16), "shard", scatter_dimension=1, tiled=True
        ).astype(jnp.float32),
        lax.psum_scatter(
            leading[12].astype(jnp.bfloat16), "shard", scatter_dimension=1, tiled=True
        ).astype(jnp.float32),
    )
    summed = (
        lax.psum(shard_totals[0].astype(jnp.bfloat16), "replica").astype(jnp.float32),
        lax.psum(shard_totals[1].astype(jnp.bfloat16), "replica").astype(jnp.float32),
        lax.psum(shard_totals[2].astype(jnp.bfloat16), "replica").astype(jnp.float32),
        lax.psum(shard_totals[3].astype(jnp.bfloat16), "replica").astype(jnp.float32),
        lax.psum(shard_totals[4].astype(jnp.bfloat16), "replica").astype(jnp.float32),
        lax.psum(shard_totals[5].astype(jnp.bfloat16), "replica").astype(jnp.float32),
        lax.psum(shard_totals[6].astype(jnp.bfloat16), "replica").astype(jnp.float32),
        lax.psum(shard_totals[7].astype(jnp.bfloat16), "replica").astype(jnp.float32),
        lax.psum(shard_totals[8].astype(jnp.bfloat16), "replica").astype(jnp.float32),
        lax.psum(shard_totals[9].astype(jnp.bfloat16), "replica").astype(jnp.float32),
        lax.psum(shard_totals[10].astype(jnp.bfloat16), "replica").astype(jnp.float32),
        lax.psum(shard_totals[11].astype(jnp.bfloat16), "replica").astype(jnp.float32),
        lax.psum(shard_totals[12].astype(jnp.bfloat16), "replica").astype(jnp.float32),
    )
    return (
        block_out[None],
        grad_buffer[None],
        summed[0],
        summed[1],
        summed[2],
        summed[3],
        summed[4],
        summed[5],
        summed[6],
        summed[7],
        summed[8],
        summed[9],
        summed[10],
        summed[11],
        summed[12],
    )


def solution(mesh):
    placed = (
        P(("shard", "replica"), None),
        P(("shard", "replica"), None),
        P(),
        P(),
        P("section", "shard"),
        P("section", "shard"),
        P("section", "shard", None),
        P("section", "shard"),
        P("section", "shard"),
        P("section", "shard", None),
        P("section", "shard"),
        P("section", "shard"),
        P("section", "shard"),
        P("section", "shard", None),
        P("section", "shard"),
        P("section", "shard", None),
        P("section", "shard"),
    )
    return jax.shard_map(
        per_device,
        mesh=mesh,
        in_specs=placed,
        out_specs=(
            P("section", ("shard", "replica"), None),
            P("section", ("shard", "replica"), None),
            P("section", "shard"),
            P("section", "shard"),
            P("section", "shard", None),
            P("section", "shard"),
            P("section", "shard"),
            P("section", "shard", None),
            P("section", "shard"),
            P("section", "shard"),
            P("section", "shard"),
            P("section", "shard", None),
            P("section", "shard"),
            P("section", "shard", None),
            P("section", "shard"),
        ),
        check_vma=False,
    )
```

profile of v0, /device:TPU:0, one launch (start us, length us, event | category | flops | bytes accessed | tf_op | source)
XLA Modules:
  0.0 1358.3 jit_solution(8355788246038441990)
XLA Ops:
  13.8 21.1 %all-reduce.10 = (bf16[768]{0:T(1024)(128)(2,1)S(1)}, bf16[768]{0:T(1024)(128)(2,1)S(1)}, bf16[768]{0:T(1024)(128)(2,1)S(1)}, bf16[768]{0:T(1024)(128)(2,1)S(1)}...) all-reduce(bf16[768]{0:T(1024)(128)(2,1)S(1)} %dynamic-update-slice, ...), channel_id=1, replica_groups=mesh['section'=2,'shard'=4,'replica'=4] {'shard'}, use_global_device_ids=true, to_apply=%add | all-reduce | flops 6144 | bytes 24576
  39.0 13.0 all_gather.57
  55.9 58.1 %all-gather.5.cloned.1.call-done = bf16[1,768,2304]{2,1,0:T(8,128)(2,1)} async-done(((bf16[1,192,2304]{2,1,0:T(8,128)(2,1)}), bf16[1,768,2304]{2,1,0:T(8,128)(2,1)}) %all-gather.5.cloned.1.call-update) | async-done | bytes 3538960 | tf_op jit(solution)/shard_map/all_gather | solution.py:305
  114.0 89.6 %all-gather.9.cloned.1.call-done = bf16[1,768,3072]{2,1,0:T(8,128)(2,1)} async-done(((bf16[1,192,3072]{2,1,0:T(8,128)(2,1)}), bf16[1,768,3072]{2,1,0:T(8,128)(2,1)}) %all-gather.9.cloned.1.call-update) | async-done | bytes 4718608 | tf_op jit(solution)/shard_map/all_gather | solution.py:312
  203.6 89.3 %all-gather.11.cloned.1.call-done = bf16[1,3072,768]{2,1,0:T(8,128)(2,1)} async-done(((bf16[1,768,768]{2,1,0:T(8,128)(2,1)}), bf16[1,3072,768]{2,1,0:T(8,128)(2,1)}) %all-gather.11.cloned.1.call-update) | async-done | bytes 4718608 | tf_op jit(solution)/shard_map/all_gather | solution.py:314
  293.1 41.6 %conditional.6 = (bf16[512,768]{1,0:T(8,128)(2,1)}, bf16[1,512,768]{2,1,0:T(8,128)(2,1)S(1)}, f32[1,12,512]{2,1,0:T(8,128)}, f32[1,512,768]{2,1,0:T(8,128)S(1)},...) conditional(s32[]{:T(128)} %convert_element_type.651, () %tuple.116, ...), branch_computations={%region_3.4_spmd, %region_4.11_spmd} | conditional | flops 8123055616 | bytes 150000224 | solution.py:350
  354.9 49.4 %conditional.7 = (bf16[512,768]{1,0:T(8,128)(2,1)}, bf16[1,512,768]{2,1,0:T(8,128)(2,1)S(1)}, f32[1,12,512]{2,1,0:T(8,128)}, f32[1,512,768]{2,1,0:T(8,128)}, f32...) conditional(s32[]{:T(128)} %convert_element_type.673, () %tuple.118, ...), branch_computations={%region_11.12_spmd, %region_12.19_spmd} | conditional | flops 8123055616 | bytes 122143056 | solution.py:350
  450.2 23.2 %conditional.9 = (f32[512,768]{1,0:T(8,128)S(1)}, f32[768]{0:T(1024)S(1)}, f32[768]{0:T(1024)S(1)}, f32[768,2304]{1,0:T(8,128)S(1)}, f32[768]{0:T(1024)S(1)}, /*...) conditional(s32[]{:T(128)} %convert_element_type.675, ...), branch_computations={%region_27.28_spmd, %region_28.46_spmd} | conditional | flops 16659373056 | bytes 343563200 | solution.py:400
  477.8 124.4 %collective-permute-done.2 = bf16[512,768]{1,0:T(8,128)(2,1)} collective-permute-done((bf16[512,768]{1,0:T(8,128)(2,1)}, bf16[512,768]{1,0:T(8,128)(2,1)}, u32[]{:S(2)}, u32[]{:S(2)}) %collective-permute-start.2) | collective-permute-done | bytes 786464 | tf_op jit(solution)/shard_map/ppermute | solution.py:18
  604.6 88.3 %conditional.10 = (f32[512,768]{1,0:T(8,128)S(1)}, f32[768]{0:T(1024)S(1)}, f32[768]{0:T(1024)S(1)}, f32[768,2304]{1,0:T(8,128)}, f32[768]{0:T(1024)S(1)}, /*ind...) conditional(s32[]{:T(128)} %convert_element_type.677, ...), branch_computations={%region_46.47_spmd, %region_47.65_spmd} | conditional | flops 16659373056 | bytes 356158464 | solution.py:400
  607.7 10.1 convert_reduce_fusion.8
  617.8 10.8 fusion.213
  695.5 19.1 %collective-permute-done.3 = bf16[512,768]{1,0:T(8,128)(2,1)} collective-permute-done((bf16[512,768]{1,0:T(8,128)(2,1)}, bf16[512,768]{1,0:T(8,128)(2,1)}, u32[]{:S(2)}, u32[]{:S(2)}) %collective-permute-start.3) | collective-permute-done | bytes 786464 | tf_op jit(solution)/shard_map/ppermute | solution.py:18
  717.0 88.3 %conditional.11 = (f32[512,768]{1,0:T(8,128)}, f32[768]{0:T(1024)}, f32[768]{0:T(1024)}, f32[768,2304]{1,0:T(8,128)}, f32[768]{0:T(1024)}, /*index=5*/f32[768]{0...) conditional(s32[]{:T(128)} %convert_element_type.681, ...), branch_computations={%region_65.66_spmd, %region_66.84_spmd} | conditional | flops 16659373056 | bytes 364378880 | solution.py:400
  720.0 10.4 convert_reduce_fusion.13
  730.4 10.8 fusion.286
  819.2 12.4 fusion.345
  831.7 12.1 fusion.346
  859.6 43.9 %reduce-scatter.32.cloned.1.call-done = bf16[1,192,2304]{2,1,0:T(8,128)(2,1)} async-done(((bf16[1,768,2304]{2,1,0:T(8,128)(2,1)}), bf16[1,192,2304]{2,1,0:T(8,128)(2,1)}) %reduce-scatter.32.cloned.1.call-update) | async-done | bytes 884752 | tf_op jit(solution)/shard_map/reduce_scatter | solution.py:416
  903.5 87.9 %reduce-scatter.36.cloned.1.call-done = bf16[1,192,3072]{2,1,0:T(8,128)(2,1)} async-done(((bf16[1,768,3072]{2,1,0:T(8,128)(2,1)}), bf16[1,192,3072]{2,1,0:T(8,128)(2,1)}) %reduce-scatter.36.cloned.1.call-update) | async-done | bytes 1179664 | tf_op jit(solution)/shard_map/reduce_scatter | solution.py:437
  991.4 88.1 %reduce-scatter.38.cloned.1.call-done = bf16[1,768,768]{2,1,0:T(8,128)(2,1)} async-done(((bf16[1,3072,768]{2,1,0:T(8,128)(2,1)}), bf16[1,768,768]{2,1,0:T(8,128)(2,1)}) %reduce-scatter.38.cloned.1.call-update) | async-done | bytes 1179664 | tf_op jit(solution)/shard_map/reduce_scatter | solution.py:443
  1088.3 14.0 %reduce-scatter.40.cloned.1.call-done = bf16[192,1]{1,0:T(8,128)(2,1)} async-done(((bf16[768,1]{1,0:T(8,128)(2,1)}), bf16[192,1]{1,0:T(8,128)(2,1)}) %reduce-scatter.40.cloned.1.call-update) | async-done | bytes 400
  1103.2 19.5 %reduce-scatter.42.cloned.1.call-done = bf16[192,1]{1,0:T(8,128)(2,1)} async-done(((bf16[768,1]{1,0:T(8,128)(2,1)}), bf16[192,1]{1,0:T(8,128)(2,1)}) %reduce-scatter.42.cloned.1.call-update) | async-done | bytes 400
  1123.5 19.5 %reduce-scatter.44.cloned.1.call-done = bf16[192,1]{1,0:T(8,128)(2,1)} async-done(((bf16[768,1]{1,0:T(8,128)(2,1)}), bf16[192,1]{1,0:T(8,128)(2,1)}) %reduce-scatter.44.cloned.1.call-update) | async-done | bytes 400
  1143.9 18.9 %reduce-scatter.46.cloned.1.call-done = bf16[192,1]{1,0:T(8,128)(2,1)} async-done(((bf16[768,1]{1,0:T(8,128)(2,1)}), bf16[192,1]{1,0:T(8,128)(2,1)}) %reduce-scatter.46.cloned.1.call-update) | async-done | bytes 400
  1163.8 19.0 %reduce-scatter.48.cloned.1.call-done = bf16[192,1]{1,0:T(8,128)(2,1)} async-done(((bf16[768,1]{1,0:T(8,128)(2,1)}), bf16[192,1]{1,0:T(8,128)(2,1)}) %reduce-scatter.48.cloned.1.call-update) | async-done | bytes 400
  1183.6 18.9 %reduce-scatter.50.cloned.1.call-done = bf16[192,1]{1,0:T(8,128)(2,1)} async-done(((bf16[768,1]{1,0:T(8,128)(2,1)}), bf16[192,1]{1,0:T(8,128)(2,1)}) %reduce-scatter.50.cloned.1.call-update) | async-done | bytes 400
  1203.4 18.8 %reduce-scatter.52.cloned.1.call-done = bf16[192,1]{1,0:T(8,128)(2,1)} async-done(((bf16[768,1]{1,0:T(8,128)(2,1)}), bf16[192,1]{1,0:T(8,128)(2,1)}) %reduce-scatter.52.cloned.1.call-update) | async-done | bytes 400
  1223.1 19.0 %reduce-scatter.56.cloned.1.call-done = bf16[192,1]{1,0:T(8,128)(2,1)} async-done(((bf16[768,1]{1,0:T(8,128)(2,1)}), bf16[192,1]{1,0:T(8,128)(2,1)}) %reduce-scatter.56.cloned.1.call-update) | async-done | bytes 400
  1243.0 23.4 %reduce-scatter.54.cloned.1.call-done = bf16[768,1]{1,0:T(8,128)(2,1)} async-done(((bf16[3072,1]{1,0:T(8,128)(2,1)}), bf16[768,1]{1,0:T(8,128)(2,1)}) %reduce-scatter.54.cloned.1.call-update) | async-done | bytes 1552
  1267.4 10.6 all-reduce.8
  1283.1 60.5 %all-reduce.13.cloned.1.call-done = (bf16[1,192,2304]{2,1,0:T(8,128)(2,1)}, bf16[1,192,768]{2,1,0:T(8,128)(2,1)}, bf16[1,192,3072]{2,1,0:T(8,128)(2,1)}, bf16[1,768,768]{2,1,0:T(8,128)(2,1)}) async-done(((bf16[1,192,2304]{2,1,0:T(8,128)(2,1)}, bf16[1,192,768]{2,1,0:T(8,128)(2,1)}, bf16[1,192,3072]{2,1,0:T(8,128)(2,1)}, bf16[1,768,768]{2,1,0:T(8,128)(2,1)}), (bf16[1,192,2304]{2,1,0:T(8,128)(2,1)}, ...) | async-done | bytes 3538960 | tf_op jit(solution)/shard_map/psum | solution.py:453
  (579 shorter events, 396.5 us)
Async XLA Ops:
  7.3 31.7 %copy-start.128 = (bf16[1,768]{1,0:T(2,128)(2,1)S(1)}, bf16[1,768]{1,0:T(2,128)(2,1)}, u32[]{:S(2)}) copy-start(bf16[1,768]{1,0:T(2,128)(2,1)} %param.43) | copy-start | bytes 4612
  7.3 46.3 %copy-start.31 = (bf16[1024,768]{1,0:T(8,128)(2,1)S(1)}, bf16[1024,768]{1,0:T(8,128)(2,1)}, u32[]{:S(2)}) copy-start(bf16[1024,768]{1,0:T(8,128)(2,1)} %param.30) | copy-start | bytes 4718596
  7.3 48.6 %all-gather.7.cloned.1.call-start = ((), (), s32[]{:S(2)}) async-start(), calls=%async_computation.14 | async-start | bytes 1474560 | tf_op jit(solution)/shard_map/all_gather | solution.py:308
  8.1 106.0 %all-gather.5.cloned.1.call-start = ((), (), s32[]{:S(2)}) async-start(), calls=%async_computation.13 | async-start | bytes 4423680 | tf_op jit(solution)/shard_map/all_gather | solution.py:305
  8.8 194.8 %all-gather.9.cloned.1.call-start = ((), (), s32[]{:S(2)}) async-start(), calls=%async_computation.15 | async-start | bytes 5898240 | tf_op jit(solution)/shard_map/all_gather | solution.py:312
  9.5 283.4 %all-gather.11.cloned.1.call-start = ((), (), s32[]{:S(2)}) async-start(), calls=%async_computation.16 | async-start | bytes 5898240 | tf_op jit(solution)/shard_map/all_gather | solution.py:314
  10.1 849.5 %reduce-scatter.34.cloned.1.call-start = ((), (), s32[]{:S(2)}) async-start(), calls=%async_computation.18 | async-start | bytes 1474560 | tf_op jit(solution)/shard_map/reduce_scatter | solution.py:425
  336.1 18.7 %collective-permute-start = (bf16[512,768]{1,0:T(8,128)(2,1)}, bf16[512,768]{1,0:T(8,128)(2,1)S(1)}, u32[]{:S(2)}, u32[]{:S(2)}) collective-permute-start(bf16[512,768]{1,0:T(8,128)(2,1)} %get-tuple-element.1161), channel_id=1, source_target_pairs={{0,16},{1,17},{2,18},{3,19},{4,20},{5,21},{6,22},{7,23},{8,24},{9,... | collective-permute-start | bytes 2359304 | tf_op jit(solution)/shard_map/ppermute | solution.py:18
  404.3 21.1 %collective-permute-start.1 = (bf16[512,768]{1,0:T(8,128)(2,1)}, bf16[512,768]{1,0:T(8,128)(2,1)S(1)}, u32[]{:S(2)}, u32[]{:S(2)}) collective-permute-start(bf16[512,768]{1,0:T(8,128)(2,1)} %get-tuple-element.1162), channel_id=1, source_target_pairs={{0,16},{1,17},{2,18},{3,19},{4,20},{5,21},{6,22},{7,23},{8,24},{9,... | collective-permute-start | bytes 2359304 | tf_op jit(solution)/shard_map/ppermute | solution.py:18
  476.5 125.7 %collective-permute-start.2 = (bf16[512,768]{1,0:T(8,128)(2,1)}, bf16[512,768]{1,0:T(8,128)(2,1)}, u32[]{:S(2)}, u32[]{:S(2)}) collective-permute-start(bf16[512,768]{1,0:T(8,128)(2,1)} %get-tuple-element.1457), channel_id=1, source_target_pairs={{16,0},{17,1},{18,2},{19,3},{20,4},{21,5},{22,6},{23,7},{24,8},{25... | collective-permute-start | bytes 2359304 | tf_op jit(solution)/shard_map/ppermute | solution.py:18
  604.7 28.5 %slice-start.2 = ((s8[4718592]{0:T(1024)(128)(4,1)}), s8[4194304]{0:T(1024)(128)(4,1)S(1)}, s32[]{:S(2)}) async-start(s8[4718592]{0:T(1024)(128)(4,1)} %bitcast.472), calls=%async_computation.33 | async-start | bytes 8388608 | tf_op jit(solution)/shard_map/cond
  607.7 33.0 %copy-start.14 = (f32[512,768]{1,0:T(8,128)}, f32[512,768]{1,0:T(8,128)S(1)}, u32[]{:S(2)}) copy-start(f32[512,768]{1,0:T(8,128)S(1)} %get-tuple-element.1393) | copy-start | bytes 4718596 | tf_op jit(solution)/shard_map/cond
  607.7 27.8 %slice-start.8 = ((s8[4718592]{0:T(1024)(128)(4,1)}), s8[4194304]{0:T(1024)(128)(4,1)S(1)}, s32[]{:S(2)}) async-start(s8[4718592]{0:T(1024)(128)(4,1)} %bitcast.574), calls=%async_computation.39 | async-start | bytes 8388608 | tf_op jit(solution)/shard_map/cond
  607.7 27.8 %slice-start.9 = ((s8[4718592]{0:T(1024)(128)(4,1)}), s8[524288]{0:T(1024)(128)(4,1)S(1)}, s32[]{:S(2)}) async-start(s8[4718592]{0:T(1024)(128)(4,1)} %bitcast.574), calls=%async_computation.40 | async-start | bytes 1048576 | tf_op jit(solution)/shard_map/cond
  694.2 20.4 %collective-permute-start.3 = (bf16[512,768]{1,0:T(8,128)(2,1)}, bf16[512,768]{1,0:T(8,128)(2,1)}, u32[]{:S(2)}, u32[]{:S(2)}) collective-permute-start(bf16[512,768]{1,0:T(8,128)(2,1)} %get-tuple-element.1452), channel_id=1, source_target_pairs={{16,0},{17,1},{18,2},{19,3},{20,4},{21,5},{22,6},{23,7},{24,8},{25... | collective-permute-start | bytes 2359304 | tf_op jit(solution)/shard_map/ppermute | solution.py:18
  717.0 28.2 %slice-start.4 = ((s8[4718592]{0:T(1024)(128)(4,1)}), s8[4194304]{0:T(1024)(128)(4,1)S(1)}, s32[]{:S(2)}) async-start(s8[4718592]{0:T(1024)(128)(4,1)} %bitcast.474), calls=%async_computation.35 | async-start | bytes 8388608 | tf_op jit(solution)/shard_map/cond
  720.0 31.4 %copy-start.16 = (f32[512,768]{1,0:T(8,128)}, f32[512,768]{1,0:T(8,128)S(1)}, u32[]{:S(2)}) copy-start(f32[512,768]{1,0:T(8,128)S(1)} %get-tuple-element.1399) | copy-start | bytes 4718596 | tf_op jit(solution)/shard_map/cond
  720.0 26.9 %slice-start.10 = ((s8[4718592]{0:T(1024)(128)(4,1)}), s8[4194304]{0:T(1024)(128)(4,1)S(1)}, s32[]{:S(2)}) async-start(s8[4718592]{0:T(1024)(128)(4,1)} %bitcast.576), calls=%async_computation.41 | async-start | bytes 8388608 | tf_op jit(solution)/shard_map/cond
  720.0 26.9 %slice-start.11 = ((s8[4718592]{0:T(1024)(128)(4,1)}), s8[524288]{0:T(1024)(128)(4,1)S(1)}, s32[]{:S(2)}) async-start(s8[4718592]{0:T(1024)(128)(4,1)} %bitcast.576), calls=%async_computation.42 | async-start | bytes 1048576 | tf_op jit(solution)/shard_map/cond
  809.0 94.5 %reduce-scatter.32.cloned.1.call-start = ((), (), s32[]{:S(2)}) async-start(), calls=%async_computation.17 | async-start | bytes 4423680 | tf_op jit(solution)/shard_map/reduce_scatter | solution.py:416
  819.2 172.2 %reduce-scatter.36.cloned.1.call-start = ((), (), s32[]{:S(2)}) async-start(), calls=%async_computation.19 | async-start | bytes 5898240 | tf_op jit(solution)/shard_map/reduce_scatter | solution.py:437
  831.6 247.9 %reduce-scatter.38.cloned.1.call-start = ((), (), s32[]{:S(2)}) async-start(), calls=%async_computation.20 | async-start | bytes 5898240 | tf_op jit(solution)/shard_map/reduce_scatter | solution.py:443
  843.9 258.3 %reduce-scatter.40.cloned.1.call-start = ((), (), s32[]{:S(2)}) async-start(), calls=%async_computation.21 | async-start | bytes 245760
  846.0 276.7 %reduce-scatter.42.cloned.1.call-start = ((), (), s32[]{:S(2)}) async-start(), calls=%async_computation.22 | async-start | bytes 245760
  847.6 295.4 %reduce-scatter.44.cloned.1.call-start = ((), (), s32[]{:S(2)}) async-start(), calls=%async_computation.23 | async-start | bytes 245760
  849.3 313.6 %reduce-scatter.46.cloned.1.call-start = ((), (), s32[]{:S(2)}) async-start(), calls=%async_computation.24 | async-start | bytes 245760
  850.9 331.8 %reduce-scatter.48.cloned.1.call-start = ((), (), s32[]{:S(2)}) async-start(), calls=%async_computation.25 | async-start | bytes 245760
  852.5 350.0 %reduce-scatter.50.cloned.1.call-start = ((), (), s32[]{:S(2)}) async-start(), calls=%async_computation.26 | async-start | bytes 245760
  854.1 368.1 %reduce-scatter.52.cloned.1.call-start = ((), (), s32[]{:S(2)}) async-start(), calls=%async_computation.27 | async-start | bytes 245760
  855.8 386.3 %reduce-scatter.56.cloned.1.call-start = ((), (), s32[]{:S(2)}) async-start(), calls=%async_computation.29 | async-start | bytes 245760
  857.4 409.0 %reduce-scatter.54.cloned.1.call-start = ((), (), s32[]{:S(2)}) async-start(), calls=%async_computation.28 | async-start | bytes 983040
  859.6 484.0 %all-reduce.13.cloned.1.call-start = ((), (), s32[]{:S(2)}) async-start(), calls=%async_computation.30 | async-start | bytes 7077888 | tf_op jit(solution)/shard_map/psum | solution.py:453
  (128 other events, 706.2 us)
Sparse Core Ops, SparseCore 0:
  9.7 33.5 all-gather.6
  44.9 69.0 all-gather.4
  115.6 87.9 all-gather.8
  205.1 87.8 all-gather.10
  809.1 27.0 reduce-scatter.33
  838.4 65.0 reduce-scatter.31
  905.8 85.5 reduce-scatter.35
  993.7 85.7 reduce-scatter.37
  1082.3 19.8 reduce-scatter.39
  1105.0 17.5 reduce-scatter.41
  1125.5 17.5 reduce-scatter.43
  1145.3 17.5 reduce-scatter.45
  1165.1 17.5 reduce-scatter.47
  1184.9 17.5 reduce-scatter.49
  1204.6 17.5 reduce-scatter.51
  1224.5 17.6 reduce-scatter.55
  1244.8 21.4 reduce-scatter.53
  1268.8 74.6 all-reduce.12
where the time goes:
time: 1360 us
  waiting for transfers between devices  840 us (62%)
  matrix products  172 us (13%)
  other arithmetic  134 us (10%)
  local copies, waits for them, and re-layouts  131 us (10%)
  blocking collectives  44.7 us (3%)
  between operations  16.1 us (1%)
    unnamed x27, waiting for transfers between devices  174 us
    ppermute x4, waiting for transfers between devices, from_behind(): return lax.ppermute(block, axis, route)  148 us
    all_gather x1, waiting for transfers between devices, per_device(): lax.all_gather(expand_weight, 'shard', axis=1, tiled=True)  89.6 us
    all_gather x1, waiting for transfers between devices, per_device(): lax.all_gather(contract_weight, 'shard', axis=1, tiled=True)  89.3 us
    reduce_scatter x1, waiting for transfers between devices, per_device(): lax.psum_scatter(leading[11].astype(jnp.bfloat16), 'shard', scatter_dimen...  88.1 us
    reduce_scatter x1, waiting for transfers between devices, per_device(): lax.psum_scatter(leading[9].astype(jnp.bfloat16), 'shard', scatter_dimens...  87.9 us
    psum x1, waiting for transfers between devices, per_device(): lax.psum(shard_totals[2].astype(jnp.bfloat16), 'replica')  60.5 us
    all_gather x1, waiting for transfers between devices, per_device(): lax.all_gather(input_weight, 'shard', axis=1, tiled=True)  58.1 us
  transfers between devices with their start and end apart: 22, of which 20 were waited for; matrix products, arithmetic and copies ran while one was open for 8% of the time, Pallas kernels for 0%

commit v1 on v0

v1 whole, which is shorter than its diff:
```python
import jax
import jax.numpy as jnp
from jax import lax
from jax.experimental import pallas as pl
from jax.experimental.pallas import tpu as pltpu
from jax.sharding import PartitionSpec as P

HEADS = 12
ROWS = 512
MICRO = 2


EPSILON = 1e-05
MASKED_SCORE = -1e30


def layer_norm(hidden, norm_gain, norm_shift):
    center = hidden - jnp.mean(hidden, axis=-1, keepdims=True)
    spread = jnp.mean(center * center, axis=-1, keepdims=True)
    return center * lax.rsqrt(spread + EPSILON) * norm_gain + norm_shift


def slot_layout(counts, row_count):
    bounds = jnp.cumsum(counts, dtype=jnp.int32)
    places = jnp.arange(row_count, dtype=jnp.int32)
    segment = jnp.sum(
        (bounds[None, :] <= places[:, None]).astype(jnp.int32), axis=1, dtype=jnp.int32
    )
    living = (places < bounds[-1]).astype(jnp.float32)
    return (segment, living)


def gelu_tanh(values):
    return jax.nn.gelu(values, approximate=True)


def contract_rows(left_side, right_side):
    return lax.dot_general(
        left_side, right_side, (((0,), (0,)), ((), ())), preferred_element_type=jnp.float32
    )


def times_transpose(left_side, right_side):
    return lax.dot_general(
        left_side, right_side, (((1,), (1,)), ((), ())), preferred_element_type=jnp.float32
    )


def split_heads(joint_low):
    row_count, three_width = joint_low.shape
    model_width = three_width // 3
    shaped = joint_low.reshape(row_count, 3, HEADS, model_width // HEADS)
    return (shaped[:, 0], shaped[:, 1], shaped[:, 2])


def masked_scores(block_queries, keys_all, segment, first_row, score_scale):
    block_count = block_queries.shape[0]
    scores = (
        jnp.einsum("qhd,khd->hqk", block_queries, keys_all, preferred_element_type=jnp.float32)
        * score_scale
    )
    query_places = first_row + jnp.arange(block_count, dtype=jnp.int32)
    key_places = jnp.arange(keys_all.shape[0], dtype=jnp.int32)
    same_segment = segment[first_row : first_row + block_count, None] == segment[None, :]
    allowed = same_segment & (key_places[None, :] <= query_places[:, None])
    return jnp.where(allowed[None], scores, MASKED_SCORE)


def attend_forward(joint_low, segment):
    queries, keys_all, values = split_heads(joint_low)
    row_count, head_count, head_dim = queries.shape
    score_scale = head_dim ** (-0.5)
    scores = masked_scores(queries, keys_all, segment, 0, score_scale)
    row_max = jnp.max(scores, axis=-1, keepdims=True)
    exponent = jnp.exp(scores - row_max)
    row_total = jnp.sum(exponent, axis=-1, keepdims=True)
    probabilities = (exponent / row_total).astype(jnp.bfloat16)
    outputs = [
        jnp.einsum("hqk,khd->qhd", probabilities, values, preferred_element_type=jnp.float32)
    ]
    log_parts = [(row_max + jnp.log(row_total))[:, :, 0]]
    mixed = jnp.concatenate(outputs, axis=0).reshape(row_count, head_count * head_dim)
    return (mixed, jnp.concatenate(log_parts, axis=1))


def attend_backward(joint_low, log_sums, mixed_grad, segment):
    queries, keys_all, values = split_heads(joint_low)
    row_count, head_count, head_dim = queries.shape
    model_width = head_count * head_dim
    score_scale = head_dim ** (-0.5)
    block_rows = min(512, row_count)
    grad_heads = mixed_grad.reshape(row_count, head_count, head_dim)
    key_grad = jnp.zeros((row_count, head_count, head_dim), jnp.float32)
    value_grad = jnp.zeros((row_count, head_count, head_dim), jnp.float32)
    scores = masked_scores(queries, keys_all, segment, 0, score_scale)
    probabilities = jnp.exp(scores - log_sums[:, 0:block_rows, None])
    probs_low = probabilities.astype(jnp.bfloat16)
    value_grad = value_grad + jnp.einsum(
        "hqk,qhd->khd", probs_low, grad_heads, preferred_element_type=jnp.float32
    )
    prob_grad = jnp.einsum("qhd,khd->hqk", grad_heads, values, preferred_element_type=jnp.float32)
    centered = prob_grad - jnp.sum(prob_grad * probabilities, axis=-1, keepdims=True)
    score_grad = (probabilities * centered).astype(jnp.bfloat16)
    query_parts = [
        jnp.einsum("hqk,khd->qhd", score_grad, keys_all, preferred_element_type=jnp.float32)
        * score_scale
    ]
    key_grad = (
        key_grad
        + jnp.einsum("hqk,qhd->khd", score_grad, queries, preferred_element_type=jnp.float32)
        * score_scale
    )
    query_grad = jnp.concatenate(query_parts, axis=0).reshape(row_count, model_width)
    return jnp.concatenate(
        [
            query_grad,
            key_grad.reshape(row_count, model_width),
            value_grad.reshape(row_count, model_width),
        ],
        axis=1,
    )


def swap(block, axis, bit):
    return lax.ppermute(block, axis, [(i, i ^ bit) for i in range(lax.axis_size(axis))])


def turn(block, axis, step):
    size = lax.axis_size(axis)
    return lax.ppermute(block, axis, [((i + step) % size, i) for i in range(size)])


def one_way(block, axis, source, target):
    return lax.ppermute(block, axis, [(source, target)])


def place_kernel(where_ref, *refs):
    pieces, whole, sems = refs[:-2], refs[-2], refs[-1]
    section, turned, core, side = (where_ref[i] for i in range(4))
    copies = []
    for half in range(2):
        rank_core = core if half == 0 else 1 - core
        plain, over_x, over_y, far_low, far_high = pieces[half * 5 : half * 5 + 5]
        parts = [(plain, 0, section, side), (over_x, 0, 1 - section, side)]
        parts += [(over_y, 0, section, 1 - side)]
        parts += [(far_low, 0, 1 - section, 1 - side), (far_high, 2, 1 - section, 1 - side)]
        for piece, first, to_section, to_side in parts:
            for i in range(piece.shape[0]):
                shard = lax.rem(turned + first + i, 4)
                copies.append(
                    pltpu.make_async_copy(
                        piece.at[i],
                        whole.at[to_section, shard, rank_core * 2 + to_side],
                        sems.at[len(copies)],
                    )
                )
    for copy in copies:
        copy.start()
    for copy in copies:
        copy.wait()


def place(pieces, where):
    rows, columns = pieces[0].shape[1:]
    whole = jax.ShapeDtypeStruct((2, 4, 4, rows, columns), pieces[0].dtype)
    return pl.pallas_call(
        place_kernel,
        out_shape=whole,
        in_specs=[pl.BlockSpec(memory_space=pltpu.SMEM)]
        + [pl.BlockSpec(memory_space=pl.ANY)] * len(pieces),
        out_specs=pl.BlockSpec(memory_space=pl.ANY),
        scratch_shapes=[pltpu.SemaphoreType.DMA((32,))],
    )(where, *pieces)


def gather_whole(own, where):
    chunks = jnp.stack([own] + [turn(own, "shard", i) for i in (1, 2, 3)])
    over_x = swap(chunks, "section", 1)
    over_y = swap(chunks, "replica", 2)
    far_low = swap(over_x[:2], "replica", 2)
    far_high = swap(over_y[2:], "section", 1)
    mine = (chunks, over_x, over_y, far_low, far_high)
    theirs = tuple(swap(piece, "replica", 1) for piece in mine)
    return place(mine + theirs, where)


def add_low(first, second):
    return (first.astype(jnp.float32) + second.astype(jnp.float32)).astype(jnp.bfloat16)


def pick(array, index, axis):
    return lax.dynamic_index_in_dim(array, index, axis, keepdims=False)


def grad_halves(left, right, core):
    row_count, width = left.shape
    split = left.reshape(row_count, 4, 2, width // 8)
    theirs = contract_rows(pick(split, 1 - core, 2).reshape(row_count, width // 2), right)
    received = swap(theirs.astype(jnp.bfloat16), "replica", 1)
    own = contract_rows(pick(split, core, 2).reshape(row_count, width // 2), right)
    own = (own + received.astype(jnp.float32)).astype(jnp.bfloat16)
    return own.reshape(4, 2, width // 16, right.shape[1])


def halve(array, index, axis):
    size = array.shape[axis] // 2
    return lax.dynamic_slice_in_dim(array, index * size, size, axis)


def plane_reduce(mine, section, side, shard):
    low, high = mine[:2], mine[2:]
    low_got = swap(halve(low, 1 - section, 3), "section", 1)
    high_got = swap(pick(high, 1 - side, 1), "replica", 2)
    low = add_low(halve(low, section, 3), low_got)
    high = add_low(pick(high, side, 1), high_got)
    low_got = swap(pick(low, 1 - side, 1), "replica", 2)
    high_got = swap(halve(high, 1 - section, 2), "section", 1)
    low = add_low(pick(low, side, 1), low_got)
    high = add_low(halve(high, section, 2), high_got)
    both = jnp.concatenate([low, high], axis=0)
    total = pick(both, shard, 0).astype(jnp.float32)
    for i in (1, 2, 3):
        total = total + turn(pick(both, (shard - i) % 4, 0), "shard", i).astype(jnp.float32)
    return total.astype(jnp.bfloat16)


def ordered(own, other, index, axis):
    first = jnp.where(index == 0, own, other)
    second = jnp.where(index == 0, other, own)
    return jnp.concatenate([first, second], axis=axis)


def spread_back(parts, section, core, side):
    keep = jnp.where(section == 0, parts[0], parts[1])
    give = jnp.where(section == 0, parts[1], parts[0])
    rows = ordered(keep, swap(give, "section", 1), section, 1)
    rows = ordered(rows, swap(rows, "replica", 2), side, 0)
    rows = ordered(rows, swap(rows, "replica", 1), core, 0)
    return rows.astype(jnp.float32)


def total_all(array):
    for axis, bits in (("replica", 1), ("section", 1), ("replica", 2), ("shard", 1), ("shard", 2)):
        array = array + swap(array, axis, bits)
    return array


def block_forward(params_here, hidden_low, segment, living):
    (
        attention_gain,
        attention_shift,
        input_weight,
        query_bias,
        value_bias,
        output_weight,
        output_bias,
        feedforward_gain,
        feedforward_shift,
        expand_weight,
        expand_bias,
        contract_weight,
        contract_bias,
    ) = params_here
    hidden = hidden_low.astype(jnp.float32)
    normed = layer_norm(hidden, attention_gain, attention_shift).astype(jnp.bfloat16)
    joint_bias = jnp.concatenate([query_bias, jnp.zeros_like(query_bias), value_bias])
    joint_low = (
        jnp.dot(normed, input_weight, preferred_element_type=jnp.float32) + joint_bias
    ).astype(jnp.bfloat16)
    mixed, log_sums = attend_forward(joint_low, segment)
    mixed_low = mixed.astype(jnp.bfloat16)
    middle = (
        hidden + jnp.dot(mixed_low, output_weight, preferred_element_type=jnp.float32) + output_bias
    )
    normed_two = layer_norm(middle, feedforward_gain, feedforward_shift).astype(jnp.bfloat16)
    expanded = jnp.dot(normed_two, expand_weight, preferred_element_type=jnp.float32) + expand_bias
    activated = gelu_tanh(expanded).astype(jnp.bfloat16)
    result = (
        middle
        + jnp.dot(activated, contract_weight, preferred_element_type=jnp.float32)
        + contract_bias
    )
    result = result * living[:, None]
    return (
        result.astype(jnp.bfloat16),
        (hidden_low, normed, joint_low, log_sums, mixed_low, middle, normed_two, expanded, activated),
    )


def block_backward(params_here, kept_state, upstream, segment, living, grad_of):
    (
        attention_gain,
        attention_shift,
        input_weight,
        query_bias,
        value_bias,
        output_weight,
        output_bias,
        feedforward_gain,
        feedforward_shift,
        expand_weight,
        expand_bias,
        contract_weight,
        contract_bias,
    ) = params_here
    (hidden_low, normed, joint_low, log_sums, mixed_low, middle, normed_two, expanded, activated) = (
        kept_state
    )
    model_width = middle.shape[1]
    out_grad = upstream * living[:, None]
    contract_grad_low = out_grad.astype(jnp.bfloat16)
    contract_weight_grad = grad_of(activated, contract_grad_low)
    contract_bias_grad = jnp.sum(contract_grad_low.astype(jnp.float32), axis=0)
    activated_grad = times_transpose(contract_grad_low, contract_weight)
    _, gelu_pull = jax.vjp(gelu_tanh, expanded)
    (expanded_grad,) = gelu_pull(activated_grad)
    expanded_grad_low = expanded_grad.astype(jnp.bfloat16)
    expand_weight_grad = grad_of(normed_two, expanded_grad_low)
    expand_bias_grad = jnp.sum(expanded_grad_low.astype(jnp.float32), axis=0)
    normed_two_grad = times_transpose(expanded_grad_low, expand_weight)
    _, norm_two_pull = jax.vjp(layer_norm, middle, feedforward_gain, feedforward_shift)
    middle_norm_grad, feedforward_gain_grad, feedforward_shift_grad = norm_two_pull(normed_two_grad)
    middle_grad = out_grad + middle_norm_grad
    branch_grad_low = middle_grad.astype(jnp.bfloat16)
    output_weight_grad = grad_of(mixed_low, branch_grad_low)
    output_bias_grad = jnp.sum(branch_grad_low.astype(jnp.float32), axis=0)
    mixed_grad_low = times_transpose(branch_grad_low, output_weight).astype(jnp.bfloat16)
    joint_grad_low = attend_backward(joint_low, log_sums, mixed_grad_low, segment).astype(
        jnp.bfloat16
    )
    input_weight_grad = grad_of(normed, joint_grad_low)
    joint_sums = jnp.sum(joint_grad_low.astype(jnp.float32), axis=0)
    query_bias_grad = joint_sums[:model_width]
    value_bias_grad = joint_sums[2 * model_width :]
    normed_grad = times_transpose(joint_grad_low, input_weight)
    _, norm_one_pull = jax.vjp(
        layer_norm, hidden_low.astype(jnp.float32), attention_gain, attention_shift
    )
    hidden_norm_grad, attention_gain_grad, attention_shift_grad = norm_one_pull(normed_grad)
    hidden_grad = middle_grad + hidden_norm_grad
    small = jnp.concatenate(
        [
            attention_gain_grad,
            attention_shift_grad,
            query_bias_grad,
            value_bias_grad,
            output_bias_grad,
            feedforward_gain_grad,
            feedforward_shift_grad,
            contract_bias_grad,
            expand_bias_grad,
        ]
    )
    large = (input_weight_grad, output_weight_grad, expand_weight_grad, contract_weight_grad)
    return (hidden_grad, small, large)


def per_device(
    tokens,
    cotangent,
    lengths,
    assignment,
    attention_gain,
    attention_shift,
    input_weight,
    query_bias,
    value_bias,
    output_weight,
    output_bias,
    feedforward_gain,
    feedforward_shift,
    expand_weight,
    expand_bias,
    contract_weight,
    contract_bias,
):
    section = lax.axis_index("section")
    shard = lax.axis_index("shard")
    replica = lax.axis_index("replica")
    shards, replicas = lax.axis_size("shard"), lax.axis_size("replica")
    core, side = replica % 2, replica // 2
    model_width = tokens.shape[1]
    cube = shards == 4 and replicas == 4
    where = jnp.stack([section, shard, core, side]).astype(jnp.int32)

    slot = (shard * replicas + replica) * MICRO + section
    matches = (assignment == slot).astype(jnp.int32)
    counts = jnp.sum(matches[:, None] * lengths, axis=0, dtype=jnp.int32)
    segment, living = slot_layout(counts, ROWS)
    entering = lax.dynamic_slice_in_dim(tokens, section * ROWS, ROWS, 0)
    seed = lax.dynamic_slice_in_dim(cotangent, section * ROWS, ROWS, 0)

    vectors = (
        attention_gain,
        attention_shift,
        query_bias,
        value_bias,
        output_bias,
        feedforward_gain,
        feedforward_shift,
        contract_bias,
        expand_bias,
    )
    small_own = jnp.concatenate([member[0] for member in vectors])
    small_rows = small_own.shape[0] // model_width

    if cube:

        def chunk(weight):
            size = weight.shape[1] // 4
            return lax.dynamic_slice_in_dim(weight[0], (core * 2 + side) * size, size, 0)

        out_chunk = chunk(output_weight)
        out_rows = out_chunk.shape[0]
        padded = jnp.zeros((16, model_width), jnp.bfloat16)
        padded = padded.at[:small_rows].set(small_own.reshape(small_rows, model_width))
        first = gather_whole(jnp.concatenate([out_chunk, padded], axis=0), where)
        small_all = first[:, :, 0, out_rows : out_rows + small_rows].reshape(2, shards, -1)
        output_all = first[:, :, :, :out_rows].reshape(2, -1, model_width)

        def whole(weight):
            return gather_whole(chunk(weight), where).reshape(2, -1, weight.shape[2])

        input_all, expand_all, contract_all = (
            whole(input_weight),
            whole(expand_weight),
            whole(contract_weight),
        )
    else:

        def whole(weight):
            held = lax.all_gather(weight, "shard", axis=1, tiled=True)
            return lax.all_gather(held, "section", axis=0, tiled=True)

        input_all, output_all, expand_all, contract_all = (
            whole(input_weight),
            whole(output_weight),
            whole(expand_weight),
            whole(contract_weight),
        )
        small_all = whole(small_own[None, None])

    pieces = []
    start = 0
    for member in vectors:
        size = member.shape[1]
        pieces.append(small_all[:, :, start : start + size].reshape(2, -1).astype(jnp.float32))
        start += size
    (gain_a, shift_a, bias_q, bias_v, bias_o, gain_f, shift_f, bias_c, bias_e) = pieces
    params_of = [
        (
            gain_a[block],
            shift_a[block],
            input_all[block],
            bias_q[block],
            bias_v[block],
            output_all[block],
            bias_o[block],
            gain_f[block],
            shift_f[block],
            expand_all[block],
            bias_e[block],
            contract_all[block],
            bias_c[block],
        )
        for block in range(2)
    ]

    middle_out, kept_first = block_forward(params_of[0], entering, segment, living)
    last_out, kept_second = block_forward(params_of[1], middle_out, segment, living)

    if cube:

        def grad_of(left, right):
            return plane_reduce(grad_halves(left, right, core), section, side, shard)
    else:

        def grad_of(left, right):
            return contract_rows(left, right).astype(jnp.bfloat16)

    second_grad, small_second, large_second = block_backward(
        params_of[1], kept_second, seed.astype(jnp.float32), segment, living, grad_of
    )
    upstream = second_grad.astype(jnp.bfloat16).astype(jnp.float32)
    first_grad, small_first, large_first = block_backward(
        params_of[0], kept_first, upstream, segment, living, grad_of
    )

    def own_block(first_value, second_value):
        first_got = one_way(first_value, "section", 1, 0)
        second_got = one_way(second_value, "section", 0, 1)
        keep = jnp.where(section == 0, first_value, second_value)
        got = jnp.where(section == 0, first_got, second_got)
        return ordered(keep, got, section, 0)

    block_out = own_block(middle_out, last_out)
    grads_low = (first_grad.astype(jnp.bfloat16), second_grad.astype(jnp.bfloat16))
    grad_out = own_block(*grads_low).astype(jnp.float32)

    small_both = jnp.stack([small_first, small_second])
    if cube:
        small_sum = total_all(small_both.reshape(2, -1, model_width))
        small_sum = small_sum.reshape(2, -1)
        large = [
            spread_back(parts, section, core, side) for parts in zip(large_first, large_second)
        ]
    else:
        small_sum = lax.psum(small_both, ("section", "shard", "replica"))
        large = []
        for parts in zip(large_first, large_second):
            held = lax.psum_scatter(
                jnp.stack(parts), "section", scatter_dimension=0, tiled=True
            )
            held = lax.psum_scatter(held[0], "shard", scatter_dimension=0, tiled=True)
            large.append(lax.psum(held, "replica").astype(jnp.float32))
    small_sum = pick(small_sum, section, 0)
    small = []
    start = 0
    for member in vectors:
        size = member.shape[1] * shards
        part = small_sum[start : start + size].reshape(shards, -1)
        small.append(pick(part, shard, 0)[None])
        start += size
    input_grad, output_grad, expand_grad, contract_grad = (member[None] for member in large)
    return (
        block_out[None],
        grad_out[None],
        small[0],
        small[1],
        input_grad,
        small[2],
        small[3],
        output_grad,
        small[4],
        small[5],
        small[6],
        expand_grad,
        small[8],
        contract_grad,
        small[7],
    )


def solution(mesh):
    placed = (
        P(("shard", "replica"), None),
        P(("shard", "replica"), None),
        P(),
        P(),
        P("section", "shard"),
        P("section", "shard"),
        P("section", "shard", None),
        P("section", "shard"),
        P("section", "shard"),
        P("section", "shard", None),
        P("section", "shard"),
        P("section", "shard"),
        P("section", "shard"),
        P("section", "shard", None),
        P("section", "shard"),
        P("section", "shard", None),
        P("section", "shard"),
    )
    return jax.shard_map(
        per_device,
        mesh=mesh,
        in_specs=placed,
        out_specs=(
            P("section", ("shard", "replica"), None),
            P("section", ("shard", "replica"), None),
            P("section", "shard"),
            P("section", "shard"),
            P("section", "shard", None),
            P("section", "shard"),
            P("section", "shard"),
            P("section", "shard", None),
            P("section", "shard"),
            P("section", "shard"),
            P("section", "shard"),
            P("section", "shard", None),
            P("section", "shard"),
            P("section", "shard", None),
            P("section", "shard"),
        ),
        check_vma=False,
    )
```

time: 1360 us -> 1700 us (1.25)
  Pallas kernels: 0 us -> 890 us
  waiting for transfers between devices: 840 us -> 214 us
  starting transfers between devices: 9.32 us -> 186 us
  other arithmetic: 134 us -> 69.4 us
  blocking collectives: 44.7 us -> 0 us
  local copies, waits for them, and re-layouts: 131 us -> 166 us
    pallas_call x0 -> x4, Pallas kernels: none -> 890 us  [place(): pl.pallas_call(place_kernel, out_shape=whole, in_specs=[pl.BlockSpec(memo...]
    all_gather x4 -> x0, waiting for transfers between devices: 237 us -> none  [the longest x1 89.6 us: per_device(): lax.all_gather(expand_weight, 'shard', axis=1, tiled=True)]
    reduce_scatter x4 -> x0, waiting for transfers between devices: 220 us -> none  [the longest x1 88.1 us: per_device(): lax.psum_scatter(leading[11].astype(jnp.bfloat16), 'shard', scatter_dimen...]
    ppermute x4 -> x133, starting transfers between devices: 8.58 us -> 186 us  [the longest x36 97.5 us: turn(): lax.ppermute(block, axis, [((i + step) % size, i) for i in range(size)])]
    unnamed x27 -> x0, waiting for transfers between devices: 174 us -> none
    ppermute x4 -> x133, waiting for transfers between devices: 148 us -> 214 us  [the longest x93 185 us: swap(): lax.ppermute(block, axis, [(i, i ^ bit) for i in range(lax.axis_size(axis...]
    psum x1 -> x0, waiting for transfers between devices: 60.5 us -> none  [per_device(): lax.psum(shard_totals[2].astype(jnp.bfloat16), 'replica')]
    convert_element_type x41 -> x45, other arithmetic: 71.1 us -> 14.6 us  [the longest x4 5.42 us: spread_back(): return rows.astype(jnp.float32)]
  transfers between devices with their start and end apart: 22 -> 133, of which waited for: 20 -> 46; matrix products, arithmetic and copies ran while one was open for 8% -> 20% of each run, Pallas kernels for 0% -> 36%
where the time goes in v1:
time: 1700 us; the launch traced here: 1690 us
  Pallas kernels  890 us (52%)
  waiting for transfers between devices  214 us (13%)
  starting transfers between devices  186 us (11%)
  local copies, waits for them, and re-layouts  166 us (10%)
  matrix products  164 us (10%)
  other arithmetic  69.4 us (4%)
    pallas_call x4, Pallas kernels, place(): pl.pallas_call(place_kernel, out_shape=whole, in_specs=[pl.BlockSpec(memo...  890 us
    ppermute x93, waiting for transfers between devices, swap(): lax.ppermute(block, axis, [(i, i ^ bit) for i in range(lax.axis_size(axis...  185 us
    ppermute x36, starting transfers between devices, turn(): lax.ppermute(block, axis, [((i + step) % size, i) for i in range(size)])  97.5 us
    ppermute x93, starting transfers between devices, swap(): lax.ppermute(block, axis, [(i, i ^ bit) for i in range(lax.axis_size(axis...  77.4 us
    unnamed x320, local copies, waits for them, and re-layouts  51.1 us
    dot_general x8, matrix products, times_transpose(): lax.dot_general(left_side, right_side, (((1,), (1,)), ((), ())), preferre...  36.2 us
    dot_general x16, matrix products, contract_rows(): lax.dot_general(left_side, right_side, (((0,), (0,)), ((), ())), preferre...  35.3 us
  transfers between devices with their start and end apart: 133, of which 46 were waited for; matrix products, arithmetic and copies ran while one was open for 20% of the time, Pallas kernels for 36%

profile of v1, /device:TPU:0, one launch (start us, length us, event | category | flops | bytes accessed | tf_op | source)
XLA Modules:
  0.0 1693.1 jit_solution(9241252145998254816)
XLA Ops:
  33.1 9.2 collective-permute-start.38
  44.7 9.8 collective-permute-start.26
  63.1 18.2 %collective-permute-start.24 = (bf16[48,3072]{1,0:T(8,128)(2,1)}, bf16[48,3072]{1,0:T(8,128)(2,1)S(1)}, u32[]{:S(2)}, u32[]{:S(2)}) collective-permute-start(bf16[48,3072]{1,0:T(8,128)(2,1)} %fusion.316), channel_id=1, source_target_pairs={{4,0},{8,4},{12,8},{0,12},{5,1},{9,5},{13,9},{1,13},{6,2},{10,6},{... | collective-permute-start | bytes 884744 | tf_op jit(solution)/shard_map/ppermute | solution.py:130
  97.8 97.3 %shard_map.280 = bf16[2,4,4,64,768]{4,3,2,1,0:T(8,128)(2,1)} custom-call(s32[4]{0:T(128)} %pad_add_fusion.where_ref, bf16[4,64,768]{2,1,0:T(8,128)(2,1)} %copy-done.47, bf16[4,64,768]{2,1,0:T(8,128)(2,1)} %copy-done.60, bf16[4,64,768]{2,1,0:T(8,128)(2,1)} %copy-done.59, bf16[2,64,768]{2,1,0:T(8,128)(2,1)} %copy-done.83, bf16[2,64,768]{2,1,0:T(8,128)(2,1)} %copy-done.82, ...), custom_call_target="tpu_custom_call" | custom-call | tf_op jit(solution)/shard_map/pallas_call | solution.py:166
  199.4 17.7 %collective-permute-done.15.refs_1_ = bf16[4,48,2304]{2,1,0:T(8,128)(2,1)} collective-permute-done((bf16[4,48,2304]{2,1,0:T(8,128)(2,1)S(1)}, bf16[4,48,2304]{2,1,0:T(8,128)(2,1)}, u32[]{:S(2)}, u32[]{:S(2)}) %collective-permute-start.15) | collective-permute-done | bytes 884768 | tf_op jit(solution)/shard_map/ppermute | solution.py:125
  247.7 216.5 %shard_map.281 = bf16[2,4,4,48,2304]{4,3,2,1,0:T(8,128)(2,1)} custom-call(s32[4]{0:T(128)} %pad_add_fusion.where_ref, bf16[4,48,2304]{2,1,0:T(8,128)(2,1)} %copy-done.36, bf16[4,48,2304]{2,1,0:T(8,128)(2,1)} %collective-permute-done.15.refs_1_, bf16[4,48,2304]{2,1,0:T(8,128)(2,1)} %collective-permute-done.16.refs_2_, ...), custom_call_target="tpu_custom_call" | custom-call | tf_op jit(solution)/shard_map/pallas_call | solution.py:166
  492.7 12.2 collective-permute-done.42.refs_4_
  509.8 287.9 %shard_map.282 = bf16[2,4,4,48,3072]{4,3,2,1,0:T(8,128)(2,1)} custom-call(s32[4]{0:T(128)} %pad_add_fusion.where_ref, bf16[4,48,3072]{2,1,0:T(8,128)(2,1)} %pad_maximum_fusion.2.refs_0_, bf16[4,48,3072]{2,1,0:T(8,128)(2,1)} %collective-permute-done.27.refs_1_, bf16[4,48,3072]{2,1,0:T(8,128)(2,1)} %collective-permute-done.28.refs_2_, ...), custom_call_target="tpu_custom_call" | custom-call | tf_op jit(solution)/shard_map/pallas_call | solution.py:166
  797.8 8.7 fusion.233
  807.3 287.9 %shard_map.283 = bf16[2,4,4,192,768]{4,3,2,1,0:T(8,128)(2,1)} custom-call(s32[4]{0:T(128)} %pad_add_fusion.where_ref, bf16[4,192,768]{2,1,0:T(8,128)(2,1)} %pad_maximum_fusion.3.refs_0_, bf16[4,192,768]{2,1,0:T(8,128)(2,1)} %collective-permute-done.39.refs_1_, bf16[4,192,768]{2,1,0:T(8,128)(2,1)} %collective-permute-done.40.refs_2_, ...), custom_call_target="tpu_custom_call" | custom-call | tf_op jit(solution)/shard_map/pallas_call | solution.py:166
  1095.3 8.5 fusion.232
  1110.2 8.3 reshape.775
  1162.7 9.2 convert_reduce_fusion
  1182.0 8.1 fusion.56
  1190.1 9.8 multiply_reduce_fusion.1
  1228.4 9.2 convert_reduce_fusion.1
  1251.9 10.1 multiply_reduce_fusion
  1280.1 9.1 constant_dynamic-slice_fusion.11
  1289.2 8.3 copy.188
  1299.5 8.4 reshape.778
  1321.4 9.1 constant_dynamic-slice_fusion.6
  1356.1 8.2 copy.194
  1379.1 8.3 copy.193
  1410.4 8.0 collective-permute-done.85
  1473.7 9.9 collective-permute-done.68
  1484.0 11.2 collective-permute-done.66
  1496.3 9.7 collective-permute-done.60
  1506.4 9.9 collective-permute-done.58
  1551.3 19.0 %collective-permute-done.73 = bf16[48,1152]{1,0:T(8,128)(2,1)S(1)} collective-permute-done((bf16[48,1152]{1,0:T(8,128)(2,1)S(1)}, bf16[48,1152]{1,0:T(8,128)(2,1)S(1)}, u32[]{:S(2)}, u32[]{:S(2)}) %collective-permute-start.73) | collective-permute-done | bytes 110624 | tf_op jit(solution)/shard_map/ppermute | solution.py:125
  1581.9 12.8 collective-permute-done.98
  1599.1 8.0 collective-permute-done.117
  1646.4 13.2 collective-permute-start.128
  (883 shorter events, 507.5 us)
Async XLA Ops:
  42.3 39.0 %collective-permute-start.36 = (bf16[192,768]{1,0:T(8,128)(2,1)}, bf16[192,768]{1,0:T(8,128)(2,1)}, u32[]{:S(2)}, u32[]{:S(2)}) collective-permute-start(bf16[192,768]{1,0:T(8,128)(2,1)} %fusion.315), channel_id=1, source_target_pairs={{4,0},{8,4},{12,8},{0,12},{5,1},{9,5},{13,9},{1,13},{6,2},{10,6},{... | collective-permute-start | bytes 884744 | tf_op jit(solution)/shard_map/ppermute | solution.py:130
  44.7 37.1 %collective-permute-start.26 = (bf16[48,3072]{1,0:T(8,128)(2,1)}, bf16[48,3072]{1,0:T(8,128)(2,1)}, u32[]{:S(2)}, u32[]{:S(2)}) collective-permute-start(bf16[48,3072]{1,0:T(8,128)(2,1)} %fusion.316), channel_id=1, source_target_pairs={{12,0},{0,4},{4,8},{8,12},{13,1},{1,5},{5,9},{9,13},{14,2},{2,6},{... | collective-permute-start | bytes 884744 | tf_op jit(solution)/shard_map/ppermute | solution.py:130
  54.5 33.3 %collective-permute-start.7 = (bf16[4,64,768]{2,1,0:T(8,128)(2,1)S(1)}, bf16[4,64,768]{2,1,0:T(8,128)(2,1)}, u32[]{:S(2)}, u32[]{:S(2)}) collective-permute-start(bf16[4,64,768]{2,1,0:T(8,128)(2,1)S(1)} %pad_maximum_fusion.8.refs_0_), channel_id=1, source_target_pairs={{0,1},{1,0},{2,3},{3,2},{4,5},{5,4},{6,7},{7,6},{8,9},{9,8},{10,11... | collective-permute-start | bytes 1179656 | tf_op jit(solution)/shard_map/ppermute | solution.py:125
  85.5 110.7 %collective-permute-start.16 = (bf16[4,48,2304]{2,1,0:T(8,128)(2,1)S(1)}, bf16[4,48,2304]{2,1,0:T(8,128)(2,1)}, u32[]{:S(2)}, u32[]{:S(2)}) collective-permute-start(bf16[4,48,2304]{2,1,0:T(8,128)(2,1)S(1)} %pad_maximum_fusion.4.refs_0_), channel_id=1, source_target_pairs={{0,2},{1,3},{2,0},{3,1},{4,6},{5,7},{6,4},{7,5},{8,10},{9,11},{10,... | collective-permute-start | bytes 2654216 | tf_op jit(solution)/shard_map/ppermute | solution.py:125
  93.4 125.6 %collective-permute-start.28 = (bf16[4,48,3072]{2,1,0:T(8,128)(2,1)}, bf16[4,48,3072]{2,1,0:T(8,128)(2,1)}, u32[]{:S(2)}, u32[]{:S(2)}) collective-permute-start(bf16[4,48,3072]{2,1,0:T(8,128)(2,1)} %pad_maximum_fusion.2.refs_0_), channel_id=1, source_target_pairs={{0,2},{1,3},{2,0},{3,1},{4,6},{5,7},{6,4},{7,5},{8,10},{9,11},{10,... | collective-permute-start | bytes 3538952 | tf_op jit(solution)/shard_map/ppermute | solution.py:125
  95.0 125.1 %collective-permute-start.27 = (bf16[4,48,3072]{2,1,0:T(8,128)(2,1)}, bf16[4,48,3072]{2,1,0:T(8,128)(2,1)}, u32[]{:S(2)}, u32[]{:S(2)}) collective-permute-start(bf16[4,48,3072]{2,1,0:T(8,128)(2,1)} %pad_maximum_fusion.2.refs_0_), channel_id=1, source_target_pairs={{0,16},{16,0},{1,17},{17,1},{2,18},{18,2},{3,19},{19,3},{4,20},{20... | collective-permute-start | bytes 3538952 | tf_op jit(solution)/shard_map/ppermute | solution.py:125
  95.1 125.9 %collective-permute-start.40 = (bf16[4,192,768]{2,1,0:T(8,128)(2,1)}, bf16[4,192,768]{2,1,0:T(8,128)(2,1)}, u32[]{:S(2)}, u32[]{:S(2)}) collective-permute-start(bf16[4,192,768]{2,1,0:T(8,128)(2,1)} %pad_maximum_fusion.3.refs_0_), channel_id=1, source_target_pairs={{0,2},{1,3},{2,0},{3,1},{4,6},{5,7},{6,4},{7,5},{8,10},{9,11},{10,... | collective-permute-start | bytes 3538952 | tf_op jit(solution)/shard_map/ppermute | solution.py:125
  97.0 124.0 %collective-permute-start.39 = (bf16[4,192,768]{2,1,0:T(8,128)(2,1)}, bf16[4,192,768]{2,1,0:T(8,128)(2,1)}, u32[]{:S(2)}, u32[]{:S(2)}) collective-permute-start(bf16[4,192,768]{2,1,0:T(8,128)(2,1)} %pad_maximum_fusion.3.refs_0_), channel_id=1, source_target_pairs={{0,16},{16,0},{1,17},{17,1},{2,18},{18,2},{3,19},{19,3},{4,20},{20... | collective-permute-start | bytes 3538952 | tf_op jit(solution)/shard_map/ppermute | solution.py:125
  244.7 244.8 %collective-permute-start.31 = (bf16[4,48,3072]{2,1,0:T(8,128)(2,1)}, bf16[4,48,3072]{2,1,0:T(8,128)(2,1)}, u32[]{:S(2)}, u32[]{:S(2)}) collective-permute-start(bf16[4,48,3072]{2,1,0:T(8,128)(2,1)} %pad_maximum_fusion.2.refs_0_), channel_id=1, source_target_pairs={{0,1},{1,0},{2,3},{3,2},{4,5},{5,4},{6,7},{7,6},{8,9},{9,8},{10,11... | collective-permute-start | bytes 3538952 | tf_op jit(solution)/shard_map/ppermute | solution.py:125
  245.2 246.0 %collective-permute-start.30 = (bf16[2,48,3072]{2,1,0:T(8,128)(2,1)}, bf16[2,48,3072]{2,1,0:T(8,128)(2,1)}, u32[]{:S(2)}, u32[]{:S(2)}) collective-permute-start(bf16[2,48,3072]{2,1,0:T(8,128)(2,1)} %slice.470), channel_id=1, source_target_pairs={{0,16},{16,0},{1,17},{17,1},{2,18},{18,2},{3,19},{19,3},{4,20},{20... | collective-permute-start | bytes 1769480 | tf_op jit(solution)/shard_map/ppermute | solution.py:125
  246.1 246.4 %collective-permute-start.29 = (bf16[2,48,3072]{2,1,0:T(8,128)(2,1)}, bf16[2,48,3072]{2,1,0:T(8,128)(2,1)}, u32[]{:S(2)}, u32[]{:S(2)}) collective-permute-start(bf16[2,48,3072]{2,1,0:T(8,128)(2,1)} %slice.469), channel_id=1, source_target_pairs={{0,2},{1,3},{2,0},{3,1},{4,6},{5,7},{6,4},{7,5},{8,10},{9,11},{10,... | collective-permute-start | bytes 1769480 | tf_op jit(solution)/shard_map/ppermute | solution.py:125
  247.2 259.0 %collective-permute-start.33 = (bf16[4,48,3072]{2,1,0:T(8,128)(2,1)}, bf16[4,48,3072]{2,1,0:T(8,128)(2,1)}, u32[]{:S(2)}, u32[]{:S(2)}) collective-permute-start(bf16[4,48,3072]{2,1,0:T(8,128)(2,1)} %collective-permute-done.28.refs_2_), channel_id=1, source_target_pairs={{0,1},{1,0},{2,3},{3,2},{4,5},{5,4},{6,7},{7,6},{8,9},{9,8},{10,11... | collective-permute-start | bytes 3538952 | tf_op jit(solution)/shard_map/ppermute | solution.py:125
  247.2 259.5 %collective-permute-start.32 = (bf16[4,48,3072]{2,1,0:T(8,128)(2,1)}, bf16[4,48,3072]{2,1,0:T(8,128)(2,1)}, u32[]{:S(2)}, u32[]{:S(2)}) collective-permute-start(bf16[4,48,3072]{2,1,0:T(8,128)(2,1)} %collective-permute-done.27.refs_1_), channel_id=1, source_target_pairs={{0,1},{1,0},{2,3},{3,2},{4,5},{5,4},{6,7},{7,6},{8,9},{9,8},{10,11... | collective-permute-start | bytes 3538952 | tf_op jit(solution)/shard_map/ppermute | solution.py:125
  506.2 300.3 %collective-permute-start.43 = (bf16[4,192,768]{2,1,0:T(8,128)(2,1)}, bf16[4,192,768]{2,1,0:T(8,128)(2,1)}, u32[]{:S(2)}, u32[]{:S(2)}) collective-permute-start(bf16[4,192,768]{2,1,0:T(8,128)(2,1)} %pad_maximum_fusion.3.refs_0_), channel_id=1, source_target_pairs={{0,1},{1,0},{2,3},{3,2},{4,5},{5,4},{6,7},{7,6},{8,9},{9,8},{10,11... | collective-permute-start | bytes 3538952 | tf_op jit(solution)/shard_map/ppermute | solution.py:125
  506.2 300.3 %collective-permute-start.45 = (bf16[4,192,768]{2,1,0:T(8,128)(2,1)}, bf16[4,192,768]{2,1,0:T(8,128)(2,1)}, u32[]{:S(2)}, u32[]{:S(2)}) collective-permute-start(bf16[4,192,768]{2,1,0:T(8,128)(2,1)} %collective-permute-done.40.refs_2_), channel_id=1, source_target_pairs={{0,1},{1,0},{2,3},{3,2},{4,5},{5,4},{6,7},{7,6},{8,9},{9,8},{10,11... | collective-permute-start | bytes 3538952 | tf_op jit(solution)/shard_map/ppermute | solution.py:125
  506.7 299.8 %collective-permute-start.44 = (bf16[4,192,768]{2,1,0:T(8,128)(2,1)}, bf16[4,192,768]{2,1,0:T(8,128)(2,1)}, u32[]{:S(2)}, u32[]{:S(2)}) collective-permute-start(bf16[4,192,768]{2,1,0:T(8,128)(2,1)} %collective-permute-done.39.refs_1_), channel_id=1, source_target_pairs={{0,1},{1,0},{2,3},{3,2},{4,5},{5,4},{6,7},{7,6},{8,9},{9,8},{10,11... | collective-permute-start | bytes 3538952 | tf_op jit(solution)/shard_map/ppermute | solution.py:125
  509.3 297.2 %collective-permute-start.47 = (bf16[2,192,768]{2,1,0:T(8,128)(2,1)}, bf16[2,192,768]{2,1,0:T(8,128)(2,1)S(1)}, u32[]{:S(2)}, u32[]{:S(2)}) collective-permute-start(bf16[2,192,768]{2,1,0:T(8,128)(2,1)} %copy-done.67), channel_id=1, source_target_pairs={{0,1},{1,0},{2,3},{3,2},{4,5},{5,4},{6,7},{7,6},{8,9},{9,8},{10,11... | collective-permute-start | bytes 1769480 | tf_op jit(solution)/shard_map/ppermute | solution.py:125
  509.6 297.0 %collective-permute-start.46 = (bf16[2,192,768]{2,1,0:T(8,128)(2,1)}, bf16[2,192,768]{2,1,0:T(8,128)(2,1)}, u32[]{:S(2)}, u32[]{:S(2)}) collective-permute-start(bf16[2,192,768]{2,1,0:T(8,128)(2,1)} %copy-done.68), channel_id=1, source_target_pairs={{0,1},{1,0},{2,3},{3,2},{4,5},{5,4},{6,7},{7,6},{8,9},{9,8},{10,11... | collective-permute-start | bytes 1769480 | tf_op jit(solution)/shard_map/ppermute | solution.py:125
  1125.3 317.5 %collective-permute-start.48 = (bf16[512,768]{1,0:T(8,128)(2,1)}, bf16[512,768]{1,0:T(8,128)(2,1)}, u32[]{:S(2)}, u32[]{:S(2)}) collective-permute-start(bf16[512,768]{1,0:T(8,128)(2,1)} %get-tuple-element.217), channel_id=1, source_target_pairs={{16,0},{17,1},{18,2},{19,3},{20,4},{21,5},{22,6},{23,7},{24,8},{25... | collective-permute-start | bytes 2359304 | tf_op jit(solution)/shard_map/ppermute | solution.py:134
  1222.0 234.9 %collective-permute-start.51 = (bf16[512,768]{1,0:T(8,128)(2,1)S(1)}, bf16[512,768]{1,0:T(8,128)(2,1)}, u32[]{:S(2)}, u32[]{:S(2)}) collective-permute-start(bf16[512,768]{1,0:T(8,128)(2,1)S(1)} %get-tuple-element.65), channel_id=1, source_target_pairs={{0,16},{1,17},{2,18},{3,19},{4,20},{5,21},{6,22},{7,23},{8,24},{9,... | collective-permute-start | bytes 2359304 | tf_op jit(solution)/shard_map/ppermute | solution.py:134
  1316.2 77.3 %collective-permute-start.84 = (bf16[384,768]{1,0:T(8,128)(2,1)}, bf16[384,768]{1,0:T(8,128)(2,1)}, u32[]{:S(2)}, u32[]{:S(2)}) collective-permute-start(bf16[384,768]{1,0:T(8,128)(2,1)} %convolution_convert_fusion.8), channel_id=1, source_target_pairs={{0,1},{1,0},{2,3},{3,2},{4,5},{5,4},{6,7},{7,6},{8,9},{9,8},{10,11... | collective-permute-start | bytes 1769480 | tf_op jit(solution)/shard_map/ppermute | solution.py:125
  1316.2 128.7 %collective-permute-start.49 = (bf16[512,768]{1,0:T(8,128)(2,1)}, bf16[512,768]{1,0:T(8,128)(2,1)}, u32[]{:S(2)}, u32[]{:S(2)}) collective-permute-start(bf16[512,768]{1,0:T(8,128)(2,1)} %multiply_convert_fusion.8), channel_id=1, source_target_pairs={{0,16},{1,17},{2,18},{3,19},{4,20},{5,21},{6,22},{7,23},{8,24},{9,... | collective-permute-start | bytes 2359304 | tf_op jit(solution)/shard_map/ppermute | solution.py:134
  1393.4 64.1 %collective-permute-start.50 = (bf16[512,768]{1,0:T(8,128)(2,1)S(1)}, bf16[512,768]{1,0:T(8,128)(2,1)S(1)}, u32[]{:S(2)}, u32[]{:S(2)}) collective-permute-start(bf16[512,768]{1,0:T(8,128)(2,1)S(1)} %copy-done.40), channel_id=1, source_target_pairs={{16,0},{17,1},{18,2},{19,3},{20,4},{21,5},{22,6},{23,7},{24,8},{25... | collective-permute-start | bytes 2359304 | tf_op jit(solution)/shard_map/ppermute | solution.py:134
  1452.9 63.9 %collective-permute-start.103 = (bf16[384,3072]{1,0:T(8,128)(2,1)S(1)}, bf16[384,3072]{1,0:T(8,128)(2,1)S(1)}, u32[]{:S(2)}, u32[]{:S(2)}) collective-permute-start(bf16[384,3072]{1,0:T(8,128)(2,1)S(1)} %copy-done.119), channel_id=1, source_target_pairs={{0,1},{1,0},{2,3},{3,2},{4,5},{5,4},{6,7},{7,6},{8,9},{9,8},{10,11... | collective-permute-start | bytes 7077896 | tf_op jit(solution)/shard_map/ppermute | solution.py:125
  1453.7 65.8 %collective-permute-start.122 = (bf16[1536,768]{1,0:T(8,128)(2,1)S(1)}, bf16[1536,768]{1,0:T(8,128)(2,1)S(1)}, u32[]{:S(2)}, u32[]{:S(2)}) collective-permute-start(bf16[1536,768]{1,0:T(8,128)(2,1)S(1)} %copy-done.121), channel_id=1, source_target_pairs={{0,1},{1,0},{2,3},{3,2},{4,5},{5,4},{6,7},{7,6},{8,9},{9,8},{10,11... | collective-permute-start | bytes 7077896 | tf_op jit(solution)/shard_map/ppermute | solution.py:125
  1456.9 66.5 %collective-permute-start.95 = (bf16[384,3072]{1,0:T(8,128)(2,1)S(1)}, bf16[384,3072]{1,0:T(8,128)(2,1)S(1)}, u32[]{:S(2)}, u32[]{:S(2)}) collective-permute-start(bf16[384,3072]{1,0:T(8,128)(2,1)S(1)} %copy-done.118), channel_id=1, source_target_pairs={{0,1},{1,0},{2,3},{3,2},{4,5},{5,4},{6,7},{7,6},{8,9},{9,8},{10,11... | collective-permute-start | bytes 7077896 | tf_op jit(solution)/shard_map/ppermute | solution.py:125
  1468.8 58.0 %collective-permute-start.114 = (bf16[1536,768]{1,0:T(8,128)(2,1)S(1)}, bf16[1536,768]{1,0:T(8,128)(2,1)S(1)}, u32[]{:S(2)}, u32[]{:S(2)}) collective-permute-start(bf16[1536,768]{1,0:T(8,128)(2,1)S(1)} %copy-done.120), channel_id=1, source_target_pairs={{0,1},{1,0},{2,3},{3,2},{4,5},{5,4},{6,7},{7,6},{8,9},{9,8},{10,11... | collective-permute-start | bytes 7077896 | tf_op jit(solution)/shard_map/ppermute | solution.py:125
  1545.1 34.8 %collective-permute-start.106 = (bf16[2,48,3072]{2,1,0:T(8,128)(2,1)S(1)}, bf16[2,48,3072]{2,1,0:T(8,128)(2,1)S(1)}, u32[]{:S(2)}, u32[]{:S(2)}) collective-permute-start(bf16[2,48,3072]{2,1,0:T(8,128)(2,1)S(1)} %dynamic-slice_bitcast_fusion.2), channel_id=1, source_target_pairs={{0,2},{1,3},{2,0},{3,1},{4,6},{5,7},{6,4},{7,5},{8,10},{9,11},{10,... | collective-permute-start | bytes 1769480 | tf_op jit(solution)/shard_map/ppermute | solution.py:125
  1546.2 51.9 %collective-permute-start.104 = (bf16[2,2,48,1536]{3,2,0,1:T(8,128)(2,1)S(1)}, bf16[2,2,48,1536]{3,2,0,1:T(8,128)(2,1)S(1)}, u32[]{:S(2)}, u32[]{:S(2)}) collective-permute-start(bf16[2,2,48,1536]{3,2,0,1:T(8,128)(2,1)S(1)} %copy.186), channel_id=1, source_target_pairs={{0,16},{16,0},{1,17},{17,1},{2,18},{18,2},{3,19},{19,3},{4,20},{20... | collective-permute-start | bytes 1769480 | tf_op jit(solution)/shard_map/ppermute | solution.py:125
  1547.9 48.3 %collective-permute-start.125 = (bf16[2,192,768]{2,1,0:T(8,128)(2,1)S(1)}, bf16[2,192,768]{2,1,0:T(8,128)(2,1)S(1)}, u32[]{:S(2)}, u32[]{:S(2)}) collective-permute-start(bf16[2,192,768]{2,1,0:T(8,128)(2,1)S(1)} %dynamic-slice_bitcast_fusion), channel_id=1, source_target_pairs={{0,2},{1,3},{2,0},{3,1},{4,6},{5,7},{6,4},{7,5},{8,10},{9,11},{10,... | collective-permute-start | bytes 1769480 | tf_op jit(solution)/shard_map/ppermute | solution.py:125
  1548.8 49.6 %collective-permute-start.123 = (bf16[2,2,192,384]{3,2,0,1:T(8,128)(2,1)S(1)}, bf16[2,2,192,384]{3,2,0,1:T(8,128)(2,1)S(1)}, u32[]{:S(2)}, u32[]{:S(2)}) collective-permute-start(bf16[2,2,192,384]{3,2,0,1:T(8,128)(2,1)S(1)} %copy.196), channel_id=1, source_target_pairs={{0,16},{16,0},{1,17},{17,1},{2,18},{18,2},{3,19},{19,3},{4,20},{20... | collective-permute-start | bytes 1769480 | tf_op jit(solution)/shard_map/ppermute | solution.py:125
  1598.2 41.0 %collective-permute-start.75 = (bf16[96,2304]{1,0:T(8,128)(2,1)S(1)}, bf16[96,2304]{1,0:T(8,128)(2,1)S(1)}, u32[]{:S(2)}, u32[]{:S(2)}) collective-permute-start(bf16[96,2304]{1,0:T(8,128)(2,1)S(1)} %pad_maximum_fusion.7), channel_id=1, source_target_pairs={{0,1},{1,0},{2,3},{3,2},{4,5},{5,4},{6,7},{7,6},{8,9},{9,8},{10,11... | collective-permute-start | bytes 1327112 | tf_op jit(solution)/shard_map/ppermute | solution.py:125
  (246 other events, 3900.9 us)

commit v2 on v1

v2 whole, which is shorter than its diff:
```python
import functools

import jax
import jax.numpy as jnp
from jax import lax
from jax.experimental import pallas as pl
from jax.experimental.pallas import tpu as pltpu
from jax.sharding import PartitionSpec as P

HEADS = 12
ROWS = 512
MICRO = 2


EPSILON = 1e-05
MASKED_SCORE = -1e30


def layer_norm(hidden, norm_gain, norm_shift):
    center = hidden - jnp.mean(hidden, axis=-1, keepdims=True)
    spread = jnp.mean(center * center, axis=-1, keepdims=True)
    return center * lax.rsqrt(spread + EPSILON) * norm_gain + norm_shift


def slot_layout(counts, row_count):
    bounds = jnp.cumsum(counts, dtype=jnp.int32)
    places = jnp.arange(row_count, dtype=jnp.int32)
    segment = jnp.sum(
        (bounds[None, :] <= places[:, None]).astype(jnp.int32), axis=1, dtype=jnp.int32
    )
    living = (places < bounds[-1]).astype(jnp.float32)
    return (segment, living)


def gelu_tanh(values):
    return jax.nn.gelu(values, approximate=True)


def contract_rows(left_side, right_side):
    return lax.dot_general(
        left_side, right_side, (((0,), (0,)), ((), ())), preferred_element_type=jnp.float32
    )


def times_transpose(left_side, right_side):
    return lax.dot_general(
        left_side, right_side, (((1,), (1,)), ((), ())), preferred_element_type=jnp.float32
    )


def masked_bias(segment_column, segment_row):
    row_count = segment_column.shape[0]
    query_places = lax.broadcasted_iota(jnp.int32, (row_count, row_count), 0)
    key_places = lax.broadcasted_iota(jnp.int32, (row_count, row_count), 1)
    allowed = (segment_column == segment_row) & (key_places <= query_places)
    return jnp.where(allowed, 0.0, MASKED_SCORE)


def head_lanes(block, head):
    half = block.shape[1] // 2
    lanes = lax.broadcasted_iota(jnp.int32, block.shape, 1)
    return jnp.where((lanes < half) == (head == 0), block, jnp.zeros_like(block))


def attend_kernel(column_ref, row_ref, q_ref, k_ref, v_ref, mixed_ref, log_ref, bias_ref):
    @pl.when(pl.program_id(0) == 0)
    def _():
        bias_ref[...] = masked_bias(column_ref[...], row_ref[...])

    row_count, width = q_ref.shape
    tall = row_count // 2
    scale = (width // 2) ** (-0.5)
    first_lanes = lax.broadcasted_iota(jnp.int32, (tall, width), 1) < width // 2
    for start in (0, tall):
        stop = start + tall
        queries = q_ref[start:stop] * jnp.asarray(scale, q_ref.dtype)
        outs, logs = [], []
        for head in range(2):
            scores = times_transpose(head_lanes(queries, head), k_ref[:stop])
            scores = scores + bias_ref[start:stop, :stop]
            row_max = jnp.max(scores, axis=1, keepdims=True)
            exponent = jnp.exp(scores - row_max)
            row_total = jnp.sum(exponent, axis=1, keepdims=True)
            probs = (exponent * (1.0 / row_total)).astype(jnp.bfloat16)
            outs.append(jnp.dot(probs, v_ref[:stop], preferred_element_type=jnp.float32))
            logs.append(jnp.broadcast_to(row_max + jnp.log(row_total), (tall, width)))
        mixed_ref[start:stop] = jnp.where(first_lanes, *outs).astype(jnp.bfloat16)
        log_ref[start:stop] = jnp.where(first_lanes, *logs)


def attend_back_kernel(
    column_ref, row_ref, q_ref, k_ref, v_ref, grad_ref, log_ref, dq_ref, dk_ref, dv_ref, bias_ref
):
    @pl.when(pl.program_id(0) == 0)
    def _():
        bias_ref[...] = masked_bias(column_ref[...], row_ref[...])

    row_count, width = q_ref.shape
    tall = row_count // 2
    scale = (width // 2) ** (-0.5)
    first_lanes = lax.broadcasted_iota(jnp.int32, (tall, width), 1) < width // 2
    key_parts, value_parts = [], []
    for start in (0, tall):
        stop = start + tall
        queries = q_ref[start:stop] * jnp.asarray(scale, q_ref.dtype)
        query_parts = []
        key_grad = value_grad = 0.0
        for head in range(2):
            mine = head_lanes(queries, head)
            grad = head_lanes(grad_ref[start:stop], head)
            lane = head * (width // 2)
            scores = times_transpose(mine, k_ref[:stop]) + bias_ref[start:stop, :stop]
            probs = jnp.exp(scores - log_ref[start:stop, lane : lane + 1])
            prob_grad = times_transpose(grad, v_ref[:stop])
            center = jnp.sum(prob_grad * probs, axis=1, keepdims=True)
            score_grad = (probs * (prob_grad - center)).astype(jnp.bfloat16)
            query_parts.append(
                jnp.dot(score_grad, k_ref[:stop], preferred_element_type=jnp.float32)
            )
            key_grad = key_grad + contract_rows(score_grad, mine)
            value_grad = value_grad + contract_rows(probs.astype(jnp.bfloat16), grad)
        dq_ref[start:stop] = (jnp.where(first_lanes, *query_parts) * scale).astype(jnp.bfloat16)
        key_parts.append(key_grad)
        value_parts.append(value_grad)
    for parts, target in ((key_parts, dk_ref), (value_parts, dv_ref)):
        target[:tall] = (parts[0] + parts[1][:tall]).astype(jnp.bfloat16)
        target[tall:] = parts[1][tall:].astype(jnp.bfloat16)


def attention_call(kernel, segment, blocks, outs, flops):
    row_count = segment.shape[0]
    pairs = HEADS // 2
    model_width = blocks[0][0].shape[1] // 3
    lanes = model_width // pairs

    def spec(first):
        return pl.BlockSpec((row_count, lanes), lambda pair: (0, first + pair))

    return pl.pallas_call(
        kernel,
        grid=(pairs,),
        out_shape=[jax.ShapeDtypeStruct((row_count, model_width), kind) for kind in outs],
        in_specs=[
            pl.BlockSpec((row_count, 1), lambda pair: (0, 0)),
            pl.BlockSpec((1, row_count), lambda pair: (0, 0)),
        ]
        + [spec(first) for _, first in blocks],
        out_specs=[spec(0) for _ in outs],
        scratch_shapes=[pltpu.VMEM((row_count, row_count), jnp.float32)],
        compiler_params=pltpu.CompilerParams(vmem_limit_bytes=48 * 1024 * 1024),
        cost_estimate=pl.CostEstimate(
            flops=flops * row_count * row_count * model_width,
            bytes_accessed=row_count * model_width * 16,
            transcendentals=HEADS * row_count * row_count,
        ),
    )(segment[:, None], segment[None, :], *(array for array, _ in blocks))


def attend_forward(joint_low, segment):
    pairs = HEADS // 2
    blocks = [(joint_low, first * pairs) for first in range(3)]
    return attention_call(attend_kernel, segment, blocks, (jnp.bfloat16, jnp.float32), 8)


def attend_backward(joint_low, log_sums, mixed_grad, segment):
    pairs = HEADS // 2
    blocks = [(joint_low, first * pairs) for first in range(3)]
    blocks += [(mixed_grad, 0), (log_sums, 0)]
    parts = attention_call(attend_back_kernel, segment, blocks, (jnp.bfloat16,) * 3, 20)
    return jnp.concatenate(parts, axis=1)


def swap(block, axis, bit):
    return lax.ppermute(block, axis, [(i, i ^ bit) for i in range(lax.axis_size(axis))])


def turn(block, axis, step):
    size = lax.axis_size(axis)
    return lax.ppermute(block, axis, [((i + step) % size, i) for i in range(size)])


def one_way(block, axis, source, target):
    return lax.ppermute(block, axis, [(source, target)])


def place_kernel(rows, extra, where_ref, *refs):
    pieces, outs, held, in_sems, out_sems = refs[:10], refs[10:-3], refs[-3], refs[-2], refs[-1]
    section, turned, core, side = (where_ref[i] for i in range(4))

    def run(same, other):
        steps = []
        for half in range(2):
            rank_core = core if half == 0 else 1 - core
            plain, over_x, over_y, far_low, far_high = pieces[half * 5 : half * 5 + 5]
            parts = [(plain, 0, same, side), (over_x, 0, other, side), (over_y, 0, same, 1 - side)]
            parts += [(far_low, 0, other, 1 - side), (far_high, 2, other, 1 - side)]
            for place_index, (piece, first, block, to_side) in enumerate(parts):
                for i in range(piece.shape[0]):
                    shard = lax.rem(turned + first + i, 4)
                    slot = held.at[len(steps)]
                    load = pltpu.make_async_copy(piece.at[i], slot, in_sems.at[len(steps)])
                    load.start()
                    target = outs[block].at[shard, rank_core * 2 + to_side]
                    stores = [(slot.at[:rows], target)]
                    if extra and half == 0 and place_index < 2:
                        stores.append((slot.at[rows:], outs[2 + block].at[shard]))
                    steps.append((load, stores))
        begun = []
        for load, stores in steps:
            load.wait()
            for source, target in stores:
                store = pltpu.make_async_copy(source, target, out_sems.at[len(begun)])
                store.start()
                begun.append(store)
        for store in begun:
            store.wait()

    @pl.when(section == 0)
    def _():
        run(0, 1)

    @pl.when(section == 1)
    def _():
        run(1, 0)


def place(pieces, where, extra=0):
    rows, columns = pieces[0].shape[1:]
    kind = pieces[0].dtype
    keep = rows - extra
    shapes = [jax.ShapeDtypeStruct((4, 4, keep, columns), kind)] * 2
    if extra:
        shapes += [jax.ShapeDtypeStruct((4, extra, columns), kind)] * 2
    return pl.pallas_call(
        functools.partial(place_kernel, keep, extra),
        out_shape=shapes,
        in_specs=[pl.BlockSpec(memory_space=pltpu.SMEM)]
        + [pl.BlockSpec(memory_space=pl.ANY)] * len(pieces),
        out_specs=[pl.BlockSpec(memory_space=pl.ANY)] * len(shapes),
        scratch_shapes=[
            pltpu.VMEM((32, rows, columns), kind),
            pltpu.SemaphoreType.DMA((32,)),
            pltpu.SemaphoreType.DMA((40,)),
        ],
        compiler_params=pltpu.CompilerParams(vmem_limit_bytes=32 * 1024 * 1024),
    )(where, *pieces)


def gather_along(own):
    return jnp.stack([own] + [turn(own, "shard", i) for i in (1, 2, 3)])


def gather_across(chunks):
    return (chunks, swap(chunks, "section", 1), swap(chunks, "replica", 2))


def gather_far(chunks, over_x, over_y):
    far_low = swap(over_x[:2], "replica", 2)
    far_high = swap(over_y[2:], "section", 1)
    return (chunks, over_x, over_y, far_low, far_high)


def gather_mate(*mine):
    return mine + tuple(swap(piece, "replica", 1) for piece in mine)


def gather_all(chunks):
    steps = (gather_along, gather_across, gather_far, gather_mate)
    states = [(chunk,) for chunk in chunks]
    for turn_index in range(len(chunks) + len(steps) - 1):
        states = lax.optimization_barrier(states)
        for index in range(len(chunks)):
            step = turn_index - index
            if 0 <= step < len(steps):
                result = steps[step](*states[index])
                states[index] = result if isinstance(result, tuple) else (result,)
    return states


def add_low(first, second):
    return (first.astype(jnp.float32) + second.astype(jnp.float32)).astype(jnp.bfloat16)


def pick(array, index, axis):
    return lax.dynamic_index_in_dim(array, index, axis, keepdims=False)


def grad_share(left, right, core):
    whole = contract_rows(left, right).astype(jnp.bfloat16)
    rows, columns = whole.shape
    halves = whole.reshape(4, 2, rows // 8, columns)
    received = swap(pick(halves, 1 - core, 1), "replica", 1)
    return add_low(pick(halves, core, 1), received).reshape(4, 2, rows // 16, columns)


def halve(array, index, axis):
    size = array.shape[axis] // 2
    return lax.dynamic_slice_in_dim(array, index * size, size, axis)


def reduce_steps(section, side, shard):
    def across(mine):
        low, high = mine[:2], mine[2:]
        low_got = swap(halve(low, 1 - section, 3), "section", 1)
        high_got = swap(pick(high, 1 - side, 1), "replica", 2)
        return (halve(low, section, 3), pick(high, side, 1), low_got, high_got)

    def along(low, high, low_got, high_got):
        low, high = add_low(low, low_got), add_low(high, high_got)
        low_got = swap(pick(low, 1 - side, 1), "replica", 2)
        high_got = swap(halve(high, 1 - section, 2), "section", 1)
        return (pick(low, side, 1), halve(high, section, 2), low_got, high_got)

    def over_shards(low, high, low_got, high_got):
        both = jnp.concatenate([add_low(low, low_got), add_low(high, high_got)], axis=0)
        got = [turn(pick(both, (shard - i) % 4, 0), "shard", i) for i in (1, 2, 3)]
        return (pick(both, shard, 0), *got)

    def finish(own, *got):
        total = own.astype(jnp.float32)
        for member in got:
            total = total + member.astype(jnp.float32)
        return (total.astype(jnp.bfloat16),)

    return (across, along, over_shards, finish)


def spread_steps(section, core, side):
    def back(first, second):
        keep = jnp.where(section == 0, first, second)
        give = jnp.where(section == 0, second, first)
        return (keep, swap(give, "section", 1))

    def sides(keep, got):
        rows = ordered(keep, got, section, 1)
        return (rows, swap(rows, "replica", 2))

    def cores(own, got):
        rows = ordered(own, got, side, 0)
        return (rows, swap(rows, "replica", 1))

    def finish(own, got):
        return (ordered(own, got, core, 0).astype(jnp.float32),)

    return (back, sides, cores, finish)


class Flows:
    def __init__(self, reduce_steps, spread_steps):
        self.reduce_steps = reduce_steps
        self.spread_steps = spread_steps
        self.left = {}
        self.states = {}

    def add(self, name, mine):
        self.left[name] = list(self.reduce_steps)
        self.states[name] = (mine,)

    def join(self):
        for name in [name for name in self.left if name.startswith("first_")]:
            whole, other = name[len("first_") :], "second_" + name[len("first_") :]
            if not self.left[name] and not self.left[other] and whole not in self.left:
                self.left[whole] = list(self.spread_steps)
                self.states[whole] = self.states[name] + self.states[other]

    def busy(self):
        return [name for name in self.left if self.left[name]]

    def stage(self, compute, *inputs):
        self.join()
        names = self.busy()
        states = [self.states[name] for name in names]
        inputs, states = lax.optimization_barrier((inputs, states))
        moved = [self.left[name].pop(0)(*state) for name, state in zip(names, states)]
        results, moved = lax.optimization_barrier((compute(*inputs), moved))
        self.states.update(zip(names, moved))
        self.join()
        return results


def ordered(own, other, index, axis):
    first = jnp.where(index == 0, own, other)
    second = jnp.where(index == 0, other, own)
    return jnp.concatenate([first, second], axis=axis)


def total_all(array):
    for axis, bits in (("replica", 1), ("section", 1), ("replica", 2), ("shard", 1), ("shard", 2)):
        array = array + swap(array, axis, bits)
    return array


def block_forward(params_here, hidden_low, segment, living):
    (
        attention_gain,
        attention_shift,
        input_weight,
        query_bias,
        value_bias,
        output_weight,
        output_bias,
        feedforward_gain,
        feedforward_shift,
        expand_weight,
        expand_bias,
        contract_weight,
        contract_bias,
    ) = params_here
    hidden = hidden_low.astype(jnp.float32)
    normed = layer_norm(hidden, attention_gain, attention_shift).astype(jnp.bfloat16)
    joint_bias = jnp.concatenate([query_bias, jnp.zeros_like(query_bias), value_bias])
    joint_low = (
        jnp.dot(normed, input_weight, preferred_element_type=jnp.float32) + joint_bias
    ).astype(jnp.bfloat16)
    mixed_low, log_sums = attend_forward(joint_low, segment)
    middle = (
        hidden + jnp.dot(mixed_low, output_weight, preferred_element_type=jnp.float32) + output_bias
    )
    normed_two = layer_norm(middle, feedforward_gain, feedforward_shift).astype(jnp.bfloat16)
    expanded = jnp.dot(normed_two, expand_weight, preferred_element_type=jnp.float32) + expand_bias
    activated = gelu_tanh(expanded).astype(jnp.bfloat16)
    result = (
        middle
        + jnp.dot(activated, contract_weight, preferred_element_type=jnp.float32)
        + contract_bias
    )
    result = result * living[:, None]
    return (
        result.astype(jnp.bfloat16),
        (hidden_low, normed, joint_low, log_sums, mixed_low, middle, normed_two, expanded, activated),
    )


def block_backward(params_here, kept_state, upstream, segment, living, flow, tag, core):
    (
        attention_gain,
        attention_shift,
        input_weight,
        query_bias,
        value_bias,
        output_weight,
        output_bias,
        feedforward_gain,
        feedforward_shift,
        expand_weight,
        expand_bias,
        contract_weight,
        contract_bias,
    ) = params_here
    (hidden_low, normed, joint_low, log_sums, mixed_low, middle, normed_two, expanded, activated) = (
        kept_state
    )
    model_width = middle.shape[1]

    def contract_part(upstream, activated):
        out_grad = upstream * living[:, None]
        low = out_grad.astype(jnp.bfloat16)
        return (out_grad, low, grad_share(activated, low, core))

    out_grad, contract_grad_low, contract_mine = flow.stage(contract_part, upstream, activated)
    flow.add(tag + "contract", contract_mine)

    def expand_part(contract_grad_low, expanded):
        activated_grad = times_transpose(contract_grad_low, contract_weight)
        _, gelu_pull = jax.vjp(gelu_tanh, expanded)
        (expanded_grad,) = gelu_pull(activated_grad)
        return expanded_grad.astype(jnp.bfloat16)

    expanded_grad_low = flow.stage(expand_part, contract_grad_low, expanded)

    def expand_grad_part(expanded_grad_low, normed_two):
        return grad_share(normed_two, expanded_grad_low, core)

    expand_mine = flow.stage(expand_grad_part, expanded_grad_low, normed_two)

    def norm_part(expanded_grad_low, out_grad, middle, mixed_low):
        normed_two_grad = times_transpose(expanded_grad_low, expand_weight)
        _, pull = jax.vjp(layer_norm, middle, feedforward_gain, feedforward_shift)
        middle_norm_grad, gain_grad, shift_grad = pull(normed_two_grad)
        middle_grad = out_grad + middle_norm_grad
        branch_grad_low = middle_grad.astype(jnp.bfloat16)
        mixed_grad_low = times_transpose(branch_grad_low, output_weight).astype(jnp.bfloat16)
        own = grad_share(mixed_low, branch_grad_low, core)
        return (middle_grad, branch_grad_low, mixed_grad_low, gain_grad, shift_grad, own)

    (
        middle_grad,
        branch_grad_low,
        mixed_grad_low,
        feedforward_gain_grad,
        feedforward_shift_grad,
        output_mine,
    ) = flow.stage(norm_part, expanded_grad_low, out_grad, middle, mixed_low)
    flow.add(tag + "expand", jnp.concatenate([expand_mine, output_mine], axis=3))

    def attention_part(joint_low, log_sums, mixed_grad_low):
        return attend_backward(joint_low, log_sums, mixed_grad_low, segment)

    joint_grad_low = flow.stage(attention_part, joint_low, log_sums, mixed_grad_low)

    def input_part(normed, joint_grad_low):
        return grad_share(normed, joint_grad_low, core)

    input_mine = flow.stage(input_part, normed, joint_grad_low)
    flow.add(tag + "input", input_mine)

    def last_part(joint_grad_low, middle_grad, hidden_low):
        normed_grad = times_transpose(joint_grad_low, input_weight)
        _, pull = jax.vjp(
            layer_norm, hidden_low.astype(jnp.float32), attention_gain, attention_shift
        )
        hidden_norm_grad, gain_grad, shift_grad = pull(normed_grad)
        return (middle_grad + hidden_norm_grad, gain_grad, shift_grad)

    hidden_grad, attention_gain_grad, attention_shift_grad = flow.stage(
        last_part, joint_grad_low, middle_grad, hidden_low
    )

    joint_sums = jnp.sum(joint_grad_low.astype(jnp.float32), axis=0)
    small = jnp.concatenate(
        [
            attention_gain_grad,
            attention_shift_grad,
            joint_sums[:model_width],
            joint_sums[2 * model_width :],
            jnp.sum(branch_grad_low.astype(jnp.float32), axis=0),
            feedforward_gain_grad,
            feedforward_shift_grad,
            jnp.sum(contract_grad_low.astype(jnp.float32), axis=0),
            jnp.sum(expanded_grad_low.astype(jnp.float32), axis=0),
        ]
    )
    return (hidden_grad, small)


def core_whole(mine, core):
    shards, sides, rows, columns = mine.shape
    own = mine.reshape(shards, 1, sides * rows, columns)
    both = jnp.concatenate([jnp.where(core == 0, own, 0), jnp.where(core == 0, 0, own)], axis=1)
    return both.reshape(shards * 2 * sides * rows, columns)


def per_device(
    tokens,
    cotangent,
    lengths,
    assignment,
    attention_gain,
    attention_shift,
    input_weight,
    query_bias,
    value_bias,
    output_weight,
    output_bias,
    feedforward_gain,
    feedforward_shift,
    expand_weight,
    expand_bias,
    contract_weight,
    contract_bias,
):
    section = lax.axis_index("section")
    shard = lax.axis_index("shard")
    replica = lax.axis_index("replica")
    shards, replicas = lax.axis_size("shard"), lax.axis_size("replica")
    core, side = replica % 2, replica // 2
    model_width = tokens.shape[1]
    cube = shards == 4 and replicas == 4
    where = jnp.stack([section, shard, core, side]).astype(jnp.int32)

    slot = (shard * replicas + replica) * MICRO + section
    matches = (assignment == slot).astype(jnp.int32)
    counts = jnp.sum(matches[:, None] * lengths, axis=0, dtype=jnp.int32)
    segment, living = slot_layout(counts, ROWS)
    entering = lax.dynamic_slice_in_dim(tokens, section * ROWS, ROWS, 0)
    seed = lax.dynamic_slice_in_dim(cotangent, section * ROWS, ROWS, 0)

    vectors = (
        attention_gain,
        attention_shift,
        query_bias,
        value_bias,
        output_bias,
        feedforward_gain,
        feedforward_shift,
        contract_bias,
        expand_bias,
    )
    small_own = jnp.concatenate([member[0] for member in vectors])
    small_rows = small_own.shape[0] // model_width

    if cube:

        def chunk(weight):
            size = weight.shape[1] // 4
            return lax.dynamic_slice_in_dim(weight[0], (core * 2 + side) * size, size, 0)

        out_chunk = chunk(output_weight)
        padded = jnp.zeros((16, model_width), jnp.bfloat16)
        padded = padded.at[:small_rows].set(small_own.reshape(small_rows, model_width))
        packed = jnp.concatenate([out_chunk, padded], axis=0)
        out_pieces, in_pieces, expand_pieces, contract_pieces = gather_all(
            [packed, chunk(input_weight), chunk(expand_weight), chunk(contract_weight)]
        )

        def joined(members):
            return [member.reshape(-1, member.shape[-1]) for member in members]

        *output_all, small_first, small_second = place(out_pieces, where, 16)
        small_all = jnp.stack([small_first, small_second])[:, :, :small_rows]
        small_all = small_all.reshape(2, shards, -1)
        output_all = joined(output_all)
        input_all = joined(place(in_pieces, where))
        expand_all = joined(place(expand_pieces, where))
        contract_all = joined(place(contract_pieces, where))
    else:

        def whole(weight):
            held = lax.all_gather(weight, "shard", axis=1, tiled=True)
            return lax.all_gather(held, "section", axis=0, tiled=True)

        input_all, output_all, expand_all, contract_all = (
            whole(input_weight),
            whole(output_weight),
            whole(expand_weight),
            whole(contract_weight),
        )
        small_all = whole(small_own[None, None])

    pieces = []
    start = 0
    for member in vectors:
        size = member.shape[1]
        pieces.append(small_all[:, :, start : start + size].reshape(2, -1).astype(jnp.float32))
        start += size
    (gain_a, shift_a, bias_q, bias_v, bias_o, gain_f, shift_f, bias_c, bias_e) = pieces
    params_of = [
        (
            gain_a[block],
            shift_a[block],
            input_all[block],
            bias_q[block],
            bias_v[block],
            output_all[block],
            bias_o[block],
            gain_f[block],
            shift_f[block],
            expand_all[block],
            bias_e[block],
            contract_all[block],
            bias_c[block],
        )
        for block in range(2)
    ]

    middle_out, kept_first = block_forward(params_of[0], entering, segment, living)
    last_out, kept_second = block_forward(params_of[1], middle_out, segment, living)

    flow = Flows(
        reduce_steps(section, side, shard) if cube else (),
        spread_steps(section, core, side) if cube else (),
    )
    second_grad, small_second = block_backward(
        params_of[1], kept_second, seed.astype(jnp.float32), segment, living, flow, "second_", core
    )
    upstream = second_grad.astype(jnp.bfloat16).astype(jnp.float32)
    first_grad, small_first = block_backward(
        params_of[0], kept_first, upstream, segment, living, flow, "first_", core
    )
    while flow.busy():
        flow.stage(lambda: ())

    def own_block(first_value, second_value):
        first_got = one_way(first_value, "section", 1, 0)
        second_got = one_way(second_value, "section", 0, 1)
        keep = jnp.where(section == 0, first_value, second_value)
        got = jnp.where(section == 0, first_got, second_got)
        return ordered(keep, got, section, 0)

    block_out = own_block(middle_out, last_out)
    grads_low = (first_grad.astype(jnp.bfloat16), second_grad.astype(jnp.bfloat16))
    grad_out = own_block(*grads_low).astype(jnp.float32)

    small_both = jnp.stack([small_first, small_second])
    if cube:
        small_sum = total_all(small_both.reshape(2, -1, model_width))
        small_sum = small_sum.reshape(2, -1)
        large = [flow.states[name][0] for name in ("input", "expand", "contract")]
    else:
        small_sum = lax.psum(small_both, ("section", "shard", "replica"))
        large = []
        for name in ("input", "expand", "contract"):
            wide = jnp.stack([core_whole(member, core) for member in flow.states[name]])
            held = lax.psum_scatter(wide, "section", scatter_dimension=0, tiled=True)
            held = lax.psum_scatter(held[0], "shard", scatter_dimension=0, tiled=True)
            large.append(lax.psum(held, "replica").astype(jnp.float32))
    small_sum = pick(small_sum, section, 0)
    small = []
    start = 0
    for member in vectors:
        size = member.shape[1] * shards
        part = small_sum[start : start + size].reshape(shards, -1)
        small.append(pick(part, shard, 0)[None])
        start += size
    input_grad, expand_both, contract_grad = (member[None] for member in large)
    expand_width = expand_weight.shape[2]
    expand_grad, output_grad = expand_both[:, :, :expand_width], expand_both[:, :, expand_width:]
    return (
        block_out[None],
        grad_out[None],
        small[0],
        small[1],
        input_grad,
        small[2],
        small[3],
        output_grad,
        small[4],
        small[5],
        small[6],
        expand_grad,
        small[8],
        contract_grad,
        small[7],
    )


def solution(mesh):
    placed = (
        P(("shard", "replica"), None),
        P(("shard", "replica"), None),
        P(),
        P(),
        P("section", "shard"),
        P("section", "shard"),
        P("section", "shard", None),
        P("section", "shard"),
        P("section", "shard"),
        P("section", "shard", None),
        P("section", "shard"),
        P("section", "shard"),
        P("section", "shard"),
        P("section", "shard", None),
        P("section", "shard"),
        P("section", "shard", None),
        P("section", "shard"),
    )
    return jax.shard_map(
        per_device,
        mesh=mesh,
        in_specs=placed,
        out_specs=(
            P("section", ("shard", "replica"), None),
            P("section", ("shard", "replica"), None),
            P("section", "shard"),
            P("section", "shard"),
            P("section", "shard", None),
            P("section", "shard"),
            P("section", "shard"),
            P("section", "shard", None),
            P("section", "shard"),
            P("section", "shard"),
            P("section", "shard"),
            P("section", "shard", None),
            P("section", "shard"),
            P("section", "shard", None),
            P("section", "shard"),
        ),
        check_vma=False,
    )
```

time: 1700 us -> 707 us (0.42)
  Pallas kernels: 890 us -> 85.6 us
  matrix products: 164 us -> 77.7 us
  local copies, waits for them, and re-layouts: 166 us -> 81.5 us
  starting transfers between devices: 186 us -> 122 us
  waiting for transfers between devices: 214 us -> 254 us
    pallas_call x4 -> x8, Pallas kernels: 890 us -> 85.6 us  [the longest x4 52.7 us: attention_call(): pl.pallas_call(kernel, grid=(pairs,), out_shape=[jax.ShapeDtypeStruct((ro...]
    ppermute x36 -> x30, waiting for transfers between devices: 29.1 us -> 97.8 us  [turn(): lax.ppermute(block, axis, [((i + step) % size, i) for i in range(size)])]
    dot_general x12 -> x0, matrix products: 52.1 us -> none  [the longest x2 20 us: attend_backward(): jnp.einsum('qhd,khd->hqk', grad_heads, values, preferred_element_type=jnp...]
    ppermute x36 -> x30, starting transfers between devices: 97.5 us -> 50.4 us  [turn(): lax.ppermute(block, axis, [((i + step) % size, i) for i in range(size)])]
    slice x21 -> x16, local copies, waits for them, and re-layouts: 39 us -> 8.02 us  [the longest x4 2.35 us: gather_far(): far_low = swap(over_x[:2], 'replica', 2)]
    ppermute x93 -> x82, waiting for transfers between devices: 185 us -> 157 us  [swap(): lax.ppermute(block, axis, [(i, i ^ bit) for i in range(lax.axis_size(axis...]
    dynamic_slice x17 -> x9, local copies, waits for them, and re-layouts: 29.2 us -> 5.12 us  [pick(): return lax.dynamic_index_in_dim(array, index, axis, keepdims=False)]
    unnamed x320 -> x356, local copies, waits for them, and re-layouts: 51.1 us -> 32 us
  transfers between devices with their start and end apart: 133 -> 116, of which waited for: 46 -> 54; matrix products, arithmetic and copies ran while one was open for 20% -> 15% of each run, Pallas kernels for 36% -> 5%
where the time goes in v2:
time: 707 us; the launch traced here: 698 us
  waiting for transfers between devices  254 us (36%)
  starting transfers between devices  122 us (17%)
  Pallas kernels  85.6 us (12%)
  local copies, waits for them, and re-layouts  81.5 us (12%)
  matrix products  77.7 us (11%)
  other arithmetic  73.5 us (10%)
    ppermute x82, waiting for transfers between devices, swap(): lax.ppermute(block, axis, [(i, i ^ bit) for i in range(lax.axis_size(axis...  157 us
    ppermute x30, waiting for transfers between devices, turn(): lax.ppermute(block, axis, [((i + step) % size, i) for i in range(size)])  97.8 us
    ppermute x82, starting transfers between devices, swap(): lax.ppermute(block, axis, [(i, i ^ bit) for i in range(lax.axis_size(axis...  58.5 us
    pallas_call x4, Pallas kernels, attention_call(): pl.pallas_call(kernel, grid=(pairs,), out_shape=[jax.ShapeDtypeStruct((ro...  52.7 us
    ppermute x30, starting transfers between devices, turn(): lax.ppermute(block, axis, [((i + step) % size, i) for i in range(size)])  50.4 us
    pallas_call x4, Pallas kernels, place(): pl.pallas_call(functools.partial(place_kernel, keep, extra), out_shape=sh...  32.9 us
    dot_general x8, matrix products, times_transpose(): lax.dot_general(left_side, right_side, (((1,), (1,)), ((), ())), preferre...  32.7 us
    unnamed x356, local copies, waits for them, and re-layouts  32 us
  transfers between devices with their start and end apart: 116, of which 54 were waited for; matrix products, arithmetic and copies ran while one was open for 15% of the time, Pallas kernels for 5%

profile of v2, /device:TPU:0, one launch (start us, length us, event | category | flops | bytes accessed | tf_op | source)
XLA Modules:
  0.0 698.4 jit_solution(14289063439697215923)
XLA Ops:
  32.8 8.4 %collective-permute-done.6 = bf16[48,2304]{1,0:T(8,128)(2,1)S(1)} collective-permute-done((bf16[48,2304]{1,0:T(8,128)(2,1)S(1)}, bf16[48,2304]{1,0:T(8,128)(2,1)S(1)}, u32[]{:S(2)}, u32[]{:S(2)}) %collective-permute-start.6) | collective-permute-done | bytes 221216 | tf_op jit(solution)/shard_map/ppermute | solution.py:179
  52.0 6.5 collective-permute-done.14
  59.0 10.3 %collective-permute-done.13 = bf16[48,3072]{1,0:T(8,128)(2,1)S(1)} collective-permute-done((bf16[48,3072]{1,0:T(8,128)(2,1)S(1)}, bf16[48,3072]{1,0:T(8,128)(2,1)S(1)}, u32[]{:S(2)}, u32[]{:S(2)}) %collective-permute-start.13) | collective-permute-done | bytes 294944 | tf_op jit(solution)/shard_map/ppermute | solution.py:179
  70.1 6.0 collective-permute-done.9.refs_4_
  92.3 11.8 %collective-permute-done.25 = bf16[192,768]{1,0:T(8,128)(2,1)S(1)} collective-permute-done((bf16[192,768]{1,0:T(8,128)(2,1)S(1)}, bf16[192,768]{1,0:T(8,128)(2,1)S(1)}, u32[]{:S(2)}, u32[]{:S(2)}) %collective-permute-start.25) | collective-permute-done | bytes 294944 | tf_op jit(solution)/shard_map/ppermute | solution.py:179
  106.2 6.8 collective-permute-done.24
  133.9 9.7 %collective-permute-done.32.refs_3_ = bf16[2,48,3072]{2,1,0:T(8,128)(2,1)} collective-permute-done((bf16[2,48,3072]{2,1,0:T(8,128)(2,1)S(1)}, bf16[2,48,3072]{2,1,0:T(8,128)(2,1)}, u32[]{:S(2)}, u32[]{:S(2)}) %collective-permute-start.32) | collective-permute-done | bytes 589856 | tf_op jit(solution)/shard_map/ppermute | solution.py:174
  147.7 21.0 %collective-permute-done.34.refs_1_ = bf16[4,192,768]{2,1,0:T(8,128)(2,1)} collective-permute-done((bf16[4,192,768]{2,1,0:T(8,128)(2,1)S(1)}, bf16[4,192,768]{2,1,0:T(8,128)(2,1)}, u32[]{:S(2)}, u32[]{:S(2)}) %collective-permute-start.34) | collective-permute-done | bytes 1179680 | tf_op jit(solution)/shard_map/ppermute | solution.py:174
  181.2 11.7 %collective-permute-done.41.refs_3_ = bf16[2,192,768]{2,1,0:T(8,128)(2,1)S(1)} collective-permute-done((bf16[2,192,768]{2,1,0:T(8,128)(2,1)S(1)}, bf16[2,192,768]{2,1,0:T(8,128)(2,1)S(1)}, u32[]{:S(2)}, u32[]{:S(2)}) %collective-permute-start.41) | collective-permute-done | bytes 589856 | tf_op jit(solution)/shard_map/ppermute | solution.py:174
  194.4 8.8 %shard_map.280 = (bf16[4,4,48,768]{3,2,1,0:T(8,128)(2,1)S(1)}, bf16[4,4,48,768]{3,2,1,0:T(8,128)(2,1)S(1)}, bf16[4,16,768]{2,1,0:T(8,128)(2,1)S(1)}, bf16[4,16,768]{2,1,0:T(8,128)(2,1)S(1)}) custom-call(s32[4]{0:T(128)S(1)} %pad_add_fusion.where_ref, bf16[4,64,768]{2,1,0:T(8,128)(2,1)S(1)} %copy-done.9, bf16[4,64,768]{2,1,0:T(8,128)(2,1)S(1)} %copy-done.11, ...), custom_call_target="tpu_custom_call" | custom-call | tf_op jit(solution)/shard_map/pallas_call | solution.py:234
  227.6 14.1 %shard_map.281 = (bf16[4,4,48,2304]{3,2,1,0:T(8,128)(2,1)S(1)}, bf16[4,4,48,2304]{3,2,1,0:T(8,128)(2,1)S(1)}) custom-call(s32[4]{0:T(128)S(1)} %pad_add_fusion.where_ref, bf16[4,48,2304]{2,1,0:T(8,128)(2,1)S(1)} %pad_maximum_fusion.6.refs_0_, bf16[4,48,2304]{2,1,0:T(8,128)(2,1)} %collective-permute-done.10.refs_1_, ...), custom_call_target="tpu_custom_call" | custom-call | tf_op jit(solution)/shard_map/pallas_call | solution.py:234
  244.6 11.7 %shard_map.282 = (bf16[512,768]{1,0:T(8,128)(2,1)S(1)}, f32[512,768]{1,0:T(8,128)S(1)}) custom-call(s32[512,1]{1,0:T(8,128)S(1)} %copy.36.column_ref, s32[1,512]{1,0:T(1,128)S(1)} %bitcast.258, bf16[512,2304]{1,0:T(8,128)(2,1)S(1)} %fusion.34.q_ref.k_ref.v_ref, bf16[512,2304]{1,0:T(8,128)(2,1)S(1)} %fusion.34.q_ref.k_ref.v_ref, ...), custom_call_target="tpu_custom_call" | custom-call | flops 1610612736 | bytes 6291456 | tf_op jit(solution)/shard_map/pallas_call | solution.py:139
  268.5 5.9 fusion.21
  287.9 11.7 %shard_map.285 = (bf16[512,768]{1,0:T(8,128)(2,1)S(1)}, f32[512,768]{1,0:T(8,128)S(1)}) custom-call(s32[512,1]{1,0:T(8,128)S(1)} %copy.36.column_ref, s32[1,512]{1,0:T(1,128)S(1)} %bitcast.259, bf16[512,2304]{1,0:T(8,128)(2,1)S(1)} %fusion.35.q_ref.k_ref.v_ref, bf16[512,2304]{1,0:T(8,128)(2,1)S(1)} %fusion.35.q_ref.k_ref.v_ref, ...), custom_call_target="tpu_custom_call" | custom-call | flops 1610612736 | bytes 6291456 | tf_op jit(solution)/shard_map/pallas_call | solution.py:139
  301.7 6.0 fusion.29
  317.4 7.4 %multiply_convert_fusion = bf16[512,768]{1,0:T(8,128)(2,1)} fusion(f32[512,768]{1,0:T(8,128)} %copy-done.60, bf16[512,3072]{1,0:T(8,128)(2,1)} %copy-done.158, bf16[3072,768]{1,0:T(8,128)(2,1)} %bitcast.270, f32[768]{0:T(1024)S(1)} %add.659, f32[512]{0:T(512)S(1)} %copy-done.138), kind=kOutput, calls=%fused_computation.134 | convolution fusion | flops 2417491968 | bytes 10228736 | tf_op jit(solution)/shard_map/dot_general | solution.py:424
  324.7 6.5 collective-permute-start.49
  336.8 8.0 %fusion.6 = bf16[512,3072]{1,0:T(8,128)(2,1)S(1)} fusion(f32[512,3072]{1,0:T(8,128)} %get-tuple-element.540, bf16[512,768]{1,0:T(8,128)(2,1)S(1)} %copy-done.77, bf16[3072,768]{1,0:T(8,128)(2,1)S(1)} %bitcast.273), kind=kOutput, calls=%fused_computation.12 | convolution fusion | flops 2447376384 | bytes 14942208 | tf_op jit(solution)/shard_map/dot_general | solution.py:46
  344.8 15.7 %collective-permute-done.51 = bf16[2,2,192,384]{3,2,1,0:T(8,128)(2,1)S(1)} collective-permute-done((bf16[2,2,192,384]{3,2,1,0:T(8,128)(2,1)S(1)}, bf16[2,2,192,384]{3,2,1,0:T(8,128)(2,1)S(1)}, u32[]{:S(2)}, u32[]{:S(2)}) %collective-permute-start.51) | collective-permute-done | bytes 589856 | tf_op jit(solution)/shard_map/ppermute | solution.py:174
  386.5 6.3 multiply_reduce_fusion.3
  404.8 8.7 %collective-permute-done.58 = bf16[192,384]{1,0:T(8,128)(2,1)S(1)} collective-permute-done((bf16[192,384]{1,0:T(8,128)(2,1)S(1)}, bf16[192,384]{1,0:T(8,128)(2,1)S(1)}, u32[]{:S(2)}, u32[]{:S(2)}) %collective-permute-start.58) | collective-permute-done | bytes 147488 | tf_op jit(solution)/shard_map/ppermute | solution.py:179
  418.8 14.6 %shard_map.286 = (bf16[512,768]{1,0:T(8,128)(2,1)S(1)}, bf16[512,768]{1,0:T(8,128)(2,1)S(1)}, bf16[512,768]{1,0:T(8,128)(2,1)S(1)}) custom-call(s32[512,1]{1,0:T(8,128)S(1)} %copy.36.column_ref, s32[1,512]{1,0:T(1,128)S(1)} %bitcast.260, bf16[512,2304]{1,0:T(8,128)(2,1)} %copy-done.3, bf16[512,2304]{1,0:T(8,128)(2,1)} %copy-done.3, ...), custom_call_target="tpu_custom_call" | custom-call | flops 4026531840 | bytes 6291456 | tf_op jit(solution)/shard_map/pallas_call | solution.py:139
  441.8 7.2 %collective-permute-done.63 = bf16[2,48,1920]{2,1,0:T(8,128)(2,1)S(1)} collective-permute-done((bf16[2,48,1920]{2,1,0:T(8,128)(2,1)S(1)}, bf16[2,48,1920]{2,1,0:T(8,128)(2,1)S(1)}, u32[]{:S(2)}, u32[]{:S(2)}) %collective-permute-start.63) | collective-permute-done | bytes 368672 | tf_op jit(solution)/shard_map/ppermute | solution.py:174
  462.6 11.4 %collective-permute-done.66 = bf16[48,1920]{1,0:T(8,128)(2,1)S(1)} collective-permute-done((bf16[48,1920]{1,0:T(8,128)(2,1)S(1)}, bf16[48,1920]{1,0:T(8,128)(2,1)S(1)}, u32[]{:S(2)}, u32[]{:S(2)}) %collective-permute-start.66) | collective-permute-done | bytes 184352 | tf_op jit(solution)/shard_map/ppermute | solution.py:179
  494.1 6.2 fusion.13
  525.9 6.2 multiply_reduce_fusion
  543.7 9.8 %collective-permute-done.83 = bf16[192,384]{1,0:T(8,128)(2,1)S(1)} collective-permute-done((bf16[192,384]{1,0:T(8,128)(2,1)S(1)}, bf16[192,384]{1,0:T(8,128)(2,1)S(1)}, u32[]{:S(2)}, u32[]{:S(2)}) %collective-permute-start.83) | collective-permute-done | bytes 147488 | tf_op jit(solution)/shard_map/ppermute | solution.py:179
  556.7 14.7 %shard_map.287 = (bf16[512,768]{1,0:T(8,128)(2,1)S(1)}, bf16[512,768]{1,0:T(8,128)(2,1)S(1)}, bf16[512,768]{1,0:T(8,128)(2,1)S(1)}) custom-call(s32[512,1]{1,0:T(8,128)S(1)} %copy.36.column_ref, s32[1,512]{1,0:T(1,128)S(1)} %bitcast.261, bf16[512,2304]{1,0:T(8,128)(2,1)} %copy-done.2, bf16[512,2304]{1,0:T(8,128)(2,1)} %copy-done.2, ...), custom_call_target="tpu_custom_call" | custom-call | flops 4026531840 | bytes 6291456 | tf_op jit(solution)/shard_map/pallas_call | solution.py:139
  580.2 10.8 %collective-permute-done.90 = bf16[192,384]{1,0:T(8,128)(2,1)S(1)} collective-permute-done((bf16[192,384]{1,0:T(8,128)(2,1)S(1)}, bf16[192,384]{1,0:T(8,128)(2,1)S(1)}, u32[]{:S(2)}, u32[]{:S(2)}) %collective-permute-start.90) | collective-permute-done | bytes 147488 | tf_op jit(solution)/shard_map/ppermute | solution.py:174
  606.6 7.8 %collective-permute-done.92 = bf16[48,1920]{1,0:T(8,128)(2,1)S(1)} collective-permute-done((bf16[48,1920]{1,0:T(8,128)(2,1)S(1)}, bf16[48,1920]{1,0:T(8,128)(2,1)S(1)}, u32[]{:S(2)}, u32[]{:S(2)}) %collective-permute-start.92) | collective-permute-done | bytes 184352 | tf_op jit(solution)/shard_map/ppermute | solution.py:179
  625.0 10.0 %collective-permute-done.100 = f32[2,12,768]{2,1,0:T(8,128)S(1)} collective-permute-done((f32[2,12,768]{2,1,0:T(8,128)S(1)}, f32[2,12,768]{2,1,0:T(8,128)S(1)}, u32[]{:S(2)}, u32[]{:S(2)}) %collective-permute-start.100) | collective-permute-done | bytes 73760 | tf_op jit(solution)/shard_map/ppermute | solution.py:174
  645.7 5.9 collective-permute-done.103
  (860 shorter events, 386.5 us)
Async XLA Ops:
  41.3 34.8 %collective-permute-start.10 = (bf16[4,48,2304]{2,1,0:T(8,128)(2,1)S(1)}, bf16[4,48,2304]{2,1,0:T(8,128)(2,1)}, u32[]{:S(2)}, u32[]{:S(2)}) collective-permute-start(bf16[4,48,2304]{2,1,0:T(8,128)(2,1)S(1)} %pad_maximum_fusion.6.refs_0_), channel_id=1, source_target_pairs={{0,16},{16,0},{1,17},{17,1},{2,18},{18,2},{3,19},{19,3},{4,20},{20... | collective-permute-start | bytes 2654216 | tf_op jit(solution)/shard_map/ppermute | solution.py:174
  42.9 33.2 %collective-permute-start.11 = (bf16[4,48,2304]{2,1,0:T(8,128)(2,1)S(1)}, bf16[4,48,2304]{2,1,0:T(8,128)(2,1)}, u32[]{:S(2)}, u32[]{:S(2)}) collective-permute-start(bf16[4,48,2304]{2,1,0:T(8,128)(2,1)S(1)} %pad_maximum_fusion.6.refs_0_), channel_id=1, source_target_pairs={{0,2},{1,3},{2,0},{3,1},{4,6},{5,7},{6,4},{7,5},{8,10},{9,11},{10,... | collective-permute-start | bytes 2654216 | tf_op jit(solution)/shard_map/ppermute | solution.py:174
  49.6 19.8 %collective-permute-start.13 = (bf16[48,3072]{1,0:T(8,128)(2,1)S(1)}, bf16[48,3072]{1,0:T(8,128)(2,1)S(1)}, u32[]{:S(2)}, u32[]{:S(2)}) collective-permute-start(bf16[48,3072]{1,0:T(8,128)(2,1)S(1)} %dynamic-slice_bitcast_fusion.29), channel_id=1, source_target_pairs={{8,0},{12,4},{0,8},{4,12},{9,1},{13,5},{1,9},{5,13},{10,2},{14,6},... | collective-permute-start | bytes 884744 | tf_op jit(solution)/shard_map/ppermute | solution.py:179
  51.0 18.9 %collective-permute-start.12 = (bf16[48,3072]{1,0:T(8,128)(2,1)S(1)}, bf16[48,3072]{1,0:T(8,128)(2,1)S(1)}, u32[]{:S(2)}, u32[]{:S(2)}) collective-permute-start(bf16[48,3072]{1,0:T(8,128)(2,1)S(1)} %dynamic-slice_bitcast_fusion.29), channel_id=1, source_target_pairs={{4,0},{8,4},{12,8},{0,12},{5,1},{9,5},{13,9},{1,13},{6,2},{10,6},{... | collective-permute-start | bytes 884744 | tf_op jit(solution)/shard_map/ppermute | solution.py:179
  76.2 50.1 %collective-permute-start.22 = (bf16[4,48,3072]{2,1,0:T(8,128)(2,1)S(1)}, bf16[4,48,3072]{2,1,0:T(8,128)(2,1)S(1)}, u32[]{:S(2)}, u32[]{:S(2)}) collective-permute-start(bf16[4,48,3072]{2,1,0:T(8,128)(2,1)S(1)} %pad_maximum_fusion.4.refs_0_), channel_id=1, source_target_pairs={{0,16},{16,0},{1,17},{17,1},{2,18},{18,2},{3,19},{19,3},{4,20},{20... | collective-permute-start | bytes 3538952 | tf_op jit(solution)/shard_map/ppermute | solution.py:174
  76.8 49.5 %collective-permute-start.23 = (bf16[4,48,3072]{2,1,0:T(8,128)(2,1)S(1)}, bf16[4,48,3072]{2,1,0:T(8,128)(2,1)S(1)}, u32[]{:S(2)}, u32[]{:S(2)}) collective-permute-start(bf16[4,48,3072]{2,1,0:T(8,128)(2,1)S(1)} %pad_maximum_fusion.4.refs_0_), channel_id=1, source_target_pairs={{0,2},{1,3},{2,0},{3,1},{4,6},{5,7},{6,4},{7,5},{8,10},{9,11},{10,... | collective-permute-start | bytes 3538952 | tf_op jit(solution)/shard_map/ppermute | solution.py:174
  81.6 22.5 %collective-permute-start.25 = (bf16[192,768]{1,0:T(8,128)(2,1)S(1)}, bf16[192,768]{1,0:T(8,128)(2,1)S(1)}, u32[]{:S(2)}, u32[]{:S(2)}) collective-permute-start(bf16[192,768]{1,0:T(8,128)(2,1)S(1)} %dynamic-slice_bitcast_fusion.28), channel_id=1, source_target_pairs={{8,0},{12,4},{0,8},{4,12},{9,1},{13,5},{1,9},{5,13},{10,2},{14,6},... | collective-permute-start | bytes 884744 | tf_op jit(solution)/shard_map/ppermute | solution.py:179
  87.8 26.8 %collective-permute-start.15 = (bf16[4,64,768]{2,1,0:T(8,128)(2,1)S(1)}, bf16[4,64,768]{2,1,0:T(8,128)(2,1)S(1)}, u32[]{:S(2)}, u32[]{:S(2)}) collective-permute-start(bf16[4,64,768]{2,1,0:T(8,128)(2,1)S(1)} %pad_maximum_fusion.10.refs_0_), channel_id=1, source_target_pairs={{0,1},{1,0},{2,3},{3,2},{4,5},{5,4},{6,7},{7,6},{8,9},{9,8},{10,11... | collective-permute-start | bytes 1179656 | tf_op jit(solution)/shard_map/ppermute | solution.py:174
  92.3 24.5 %collective-permute-start.16 = (bf16[4,64,768]{2,1,0:T(8,128)(2,1)S(1)}, bf16[4,64,768]{2,1,0:T(8,128)(2,1)S(1)}, u32[]{:S(2)}, u32[]{:S(2)}) collective-permute-start(bf16[4,64,768]{2,1,0:T(8,128)(2,1)S(1)} %collective-permute-done.3.refs_1_), channel_id=1, source_target_pairs={{0,1},{1,0},{2,3},{3,2},{4,5},{5,4},{6,7},{7,6},{8,9},{9,8},{10,11... | collective-permute-start | bytes 1179656 | tf_op jit(solution)/shard_map/ppermute | solution.py:174
  130.2 38.4 %collective-permute-start.34 = (bf16[4,192,768]{2,1,0:T(8,128)(2,1)S(1)}, bf16[4,192,768]{2,1,0:T(8,128)(2,1)}, u32[]{:S(2)}, u32[]{:S(2)}) collective-permute-start(bf16[4,192,768]{2,1,0:T(8,128)(2,1)S(1)} %pad_maximum_fusion.5.refs_0_), channel_id=1, source_target_pairs={{0,16},{16,0},{1,17},{17,1},{2,18},{18,2},{3,19},{19,3},{4,20},{20... | collective-permute-start | bytes 3538952 | tf_op jit(solution)/shard_map/ppermute | solution.py:174
  131.6 37.1 %collective-permute-start.35 = (bf16[4,192,768]{2,1,0:T(8,128)(2,1)S(1)}, bf16[4,192,768]{2,1,0:T(8,128)(2,1)}, u32[]{:S(2)}, u32[]{:S(2)}) collective-permute-start(bf16[4,192,768]{2,1,0:T(8,128)(2,1)S(1)} %pad_maximum_fusion.5.refs_0_), channel_id=1, source_target_pairs={{0,2},{1,3},{2,0},{3,1},{4,6},{5,7},{6,4},{7,5},{8,10},{9,11},{10,... | collective-permute-start | bytes 3538952 | tf_op jit(solution)/shard_map/ppermute | solution.py:174
  168.7 25.6 %collective-permute-start.36 = (bf16[4,48,3072]{2,1,0:T(8,128)(2,1)S(1)}, bf16[4,48,3072]{2,1,0:T(8,128)(2,1)}, u32[]{:S(2)}, u32[]{:S(2)}) collective-permute-start(bf16[4,48,3072]{2,1,0:T(8,128)(2,1)S(1)} %pad_maximum_fusion.4.refs_0_), channel_id=1, source_target_pairs={{0,1},{1,0},{2,3},{3,2},{4,5},{5,4},{6,7},{7,6},{8,9},{9,8},{10,11... | collective-permute-start | bytes 3538952 | tf_op jit(solution)/shard_map/ppermute | solution.py:174
  168.7 25.6 %collective-permute-start.37 = (bf16[4,48,3072]{2,1,0:T(8,128)(2,1)}, bf16[4,48,3072]{2,1,0:T(8,128)(2,1)}, u32[]{:S(2)}, u32[]{:S(2)}) collective-permute-start(bf16[4,48,3072]{2,1,0:T(8,128)(2,1)} %copy-done.4), channel_id=1, source_target_pairs={{0,1},{1,0},{2,3},{3,2},{4,5},{5,4},{6,7},{7,6},{8,9},{9,8},{10,11... | collective-permute-start | bytes 3538952 | tf_op jit(solution)/shard_map/ppermute | solution.py:174
  169.2 25.1 %collective-permute-start.38 = (bf16[4,48,3072]{2,1,0:T(8,128)(2,1)}, bf16[4,48,3072]{2,1,0:T(8,128)(2,1)}, u32[]{:S(2)}, u32[]{:S(2)}) collective-permute-start(bf16[4,48,3072]{2,1,0:T(8,128)(2,1)} %copy-done.6), channel_id=1, source_target_pairs={{0,1},{1,0},{2,3},{3,2},{4,5},{5,4},{6,7},{7,6},{8,9},{9,8},{10,11... | collective-permute-start | bytes 3538952 | tf_op jit(solution)/shard_map/ppermute | solution.py:174
  316.1 50.3 %collective-permute-start.48 = (bf16[512,768]{1,0:T(8,128)(2,1)S(1)}, bf16[512,768]{1,0:T(8,128)(2,1)}, u32[]{:S(2)}, u32[]{:S(2)}) collective-permute-start(bf16[512,768]{1,0:T(8,128)(2,1)S(1)} %get-tuple-element.603), channel_id=1, source_target_pairs={{16,0},{17,1},{18,2},{19,3},{20,4},{21,5},{22,6},{23,7},{24,8},{25... | collective-permute-start | bytes 2359304 | tf_op jit(solution)/shard_map/ppermute | solution.py:183
  324.7 41.7 %collective-permute-start.49 = (bf16[512,768]{1,0:T(8,128)(2,1)}, bf16[512,768]{1,0:T(8,128)(2,1)}, u32[]{:S(2)}, u32[]{:S(2)}) collective-permute-start(bf16[512,768]{1,0:T(8,128)(2,1)} %multiply_convert_fusion), channel_id=1, source_target_pairs={{0,16},{1,17},{2,18},{3,19},{4,20},{5,21},{6,22},{7,23},{8,24},{9,... | collective-permute-start | bytes 2359304 | tf_op jit(solution)/shard_map/ppermute | solution.py:183
  334.9 25.6 %collective-permute-start.51 = (bf16[2,2,192,384]{3,2,1,0:T(8,128)(2,1)S(1)}, bf16[2,2,192,384]{3,2,1,0:T(8,128)(2,1)S(1)}, u32[]{:S(2)}, u32[]{:S(2)}) collective-permute-start(bf16[2,2,192,384]{3,2,1,0:T(8,128)(2,1)S(1)} %get-tuple-element.875), channel_id=1, source_target_pairs={{0,16},{16,0},{1,17},{17,1},{2,18},{18,2},{3,19},{19,3},{4,20},{20... | collective-permute-start | bytes 1769480 | tf_op jit(solution)/shard_map/ppermute | solution.py:174
  335.9 24.7 %collective-permute-start.52 = (bf16[2,192,768]{2,1,0:T(8,128)(2,1)S(1)}, bf16[2,192,768]{2,1,0:T(8,128)(2,1)S(1)}, u32[]{:S(2)}, u32[]{:S(2)}) collective-permute-start(bf16[2,192,768]{2,1,0:T(8,128)(2,1)S(1)} %get-tuple-element.873), channel_id=1, source_target_pairs={{0,2},{1,3},{2,0},{3,1},{4,6},{5,7},{6,4},{7,5},{8,10},{9,11},{10,... | collective-permute-start | bytes 1769480 | tf_op jit(solution)/shard_map/ppermute | solution.py:174
  415.0 18.6 %collective-permute-start.60 = (bf16[2,2,48,1920]{3,2,1,0:T(8,128)(2,1)S(1)}, bf16[2,2,48,1920]{3,2,1,0:T(8,128)(2,1)S(1)}, u32[]{:S(2)}, u32[]{:S(2)}) collective-permute-start(bf16[2,2,48,1920]{3,2,1,0:T(8,128)(2,1)S(1)} %get-tuple-element.865), channel_id=1, source_target_pairs={{0,16},{16,0},{1,17},{17,1},{2,18},{18,2},{3,19},{19,3},{4,20},{20... | collective-permute-start | bytes 2211848 | tf_op jit(solution)/shard_map/ppermute | solution.py:174
  416.8 17.8 %collective-permute-start.61 = (bf16[2,48,3840]{2,1,0:T(8,128)(2,1)}, bf16[2,48,3840]{2,1,0:T(8,128)(2,1)S(1)}, u32[]{:S(2)}, u32[]{:S(2)}) collective-permute-start(bf16[2,48,3840]{2,1,0:T(8,128)(2,1)} %get-tuple-element.863), channel_id=1, source_target_pairs={{0,2},{1,3},{2,0},{3,1},{4,6},{5,7},{6,4},{7,5},{8,10},{9,11},{10,... | collective-permute-start | bytes 2211848 | tf_op jit(solution)/shard_map/ppermute | solution.py:174
  450.7 23.3 %collective-permute-start.68 = (bf16[2,2,48,1152]{3,2,1,0:T(8,128)(2,1)S(1)}, bf16[2,2,48,1152]{3,2,1,0:T(8,128)(2,1)S(1)}, u32[]{:S(2)}, u32[]{:S(2)}) collective-permute-start(bf16[2,2,48,1152]{3,2,1,0:T(8,128)(2,1)S(1)} %get-tuple-element.885), channel_id=1, source_target_pairs={{0,16},{16,0},{1,17},{17,1},{2,18},{18,2},{3,19},{19,3},{4,20},{20... | collective-permute-start | bytes 1327112 | tf_op jit(solution)/shard_map/ppermute | solution.py:174
  451.1 22.9 %collective-permute-start.69 = (bf16[2,48,2304]{2,1,0:T(8,128)(2,1)S(1)}, bf16[2,48,2304]{2,1,0:T(8,128)(2,1)S(1)}, u32[]{:S(2)}, u32[]{:S(2)}) collective-permute-start(bf16[2,48,2304]{2,1,0:T(8,128)(2,1)S(1)} %get-tuple-element.883), channel_id=1, source_target_pairs={{0,2},{1,3},{2,0},{3,1},{4,6},{5,7},{6,4},{7,5},{8,10},{9,11},{10,... | collective-permute-start | bytes 1327112 | tf_op jit(solution)/shard_map/ppermute | solution.py:174
  456.7 17.3 %collective-permute-start.66 = (bf16[48,1920]{1,0:T(8,128)(2,1)S(1)}, bf16[48,1920]{1,0:T(8,128)(2,1)S(1)}, u32[]{:S(2)}, u32[]{:S(2)}) collective-permute-start(bf16[48,1920]{1,0:T(8,128)(2,1)S(1)} %get-tuple-element.900), channel_id=1, source_target_pairs={{8,0},{12,4},{0,8},{4,12},{9,1},{13,5},{1,9},{5,13},{10,2},{14,6},... | collective-permute-start | bytes 552968 | tf_op jit(solution)/shard_map/ppermute | solution.py:179
  554.1 18.1 %collective-permute-start.85 = (bf16[2,2,48,1920]{3,2,1,0:T(8,128)(2,1)S(1)}, bf16[2,2,48,1920]{3,2,1,0:T(8,128)(2,1)S(1)}, u32[]{:S(2)}, u32[]{:S(2)}) collective-permute-start(bf16[2,2,48,1920]{3,2,1,0:T(8,128)(2,1)S(1)} %get-tuple-element.861), channel_id=1, source_target_pairs={{0,16},{16,0},{1,17},{17,1},{2,18},{18,2},{3,19},{19,3},{4,20},{20... | collective-permute-start | bytes 2211848 | tf_op jit(solution)/shard_map/ppermute | solution.py:174
  555.5 17.8 %collective-permute-start.86 = (bf16[2,48,3840]{2,1,0:T(8,128)(2,1)S(1)}, bf16[2,48,3840]{2,1,0:T(8,128)(2,1)S(1)}, u32[]{:S(2)}, u32[]{:S(2)}) collective-permute-start(bf16[2,48,3840]{2,1,0:T(8,128)(2,1)S(1)} %get-tuple-element.859), channel_id=1, source_target_pairs={{0,2},{1,3},{2,0},{3,1},{4,6},{5,7},{6,4},{7,5},{8,10},{9,11},{10,... | collective-permute-start | bytes 2211848 | tf_op jit(solution)/shard_map/ppermute | solution.py:174
  596.2 18.3 %collective-permute-start.92 = (bf16[48,1920]{1,0:T(8,128)(2,1)S(1)}, bf16[48,1920]{1,0:T(8,128)(2,1)S(1)}, u32[]{:S(2)}, u32[]{:S(2)}) collective-permute-start(bf16[48,1920]{1,0:T(8,128)(2,1)S(1)} %get-tuple-element.892), channel_id=1, source_target_pairs={{8,0},{12,4},{0,8},{4,12},{9,1},{13,5},{1,9},{5,13},{10,2},{14,6},... | collective-permute-start | bytes 552968 | tf_op jit(solution)/shard_map/ppermute | solution.py:179
  598.4 19.6 %collective-permute-start.93 = (bf16[48,1920]{1,0:T(8,128)(2,1)S(1)}, bf16[48,1920]{1,0:T(8,128)(2,1)S(1)}, u32[]{:S(2)}, u32[]{:S(2)}) collective-permute-start(bf16[48,1920]{1,0:T(8,128)(2,1)S(1)} %get-tuple-element.889), channel_id=1, source_target_pairs={{12,0},{0,4},{4,8},{8,12},{13,1},{1,5},{5,9},{9,13},{14,2},{2,6},{... | collective-permute-start | bytes 552968 | tf_op jit(solution)/shard_map/ppermute | solution.py:179
  602.5 17.4 %collective-permute-start.95 = (bf16[2,2,48,1152]{3,2,1,0:T(8,128)(2,1)S(1)}, bf16[2,2,48,1152]{3,2,1,0:T(8,128)(2,1)S(1)}, u32[]{:S(2)}, u32[]{:S(2)}) collective-permute-start(bf16[2,2,48,1152]{3,2,1,0:T(8,128)(2,1)S(1)} %get-tuple-element.881), channel_id=1, source_target_pairs={{0,16},{16,0},{1,17},{17,1},{2,18},{18,2},{3,19},{19,3},{4,20},{20... | collective-permute-start | bytes 1327112 | tf_op jit(solution)/shard_map/ppermute | solution.py:174
  603.3 16.7 %collective-permute-start.96 = (bf16[2,48,2304]{2,1,0:T(8,128)(2,1)S(1)}, bf16[2,48,2304]{2,1,0:T(8,128)(2,1)S(1)}, u32[]{:S(2)}, u32[]{:S(2)}) collective-permute-start(bf16[2,48,2304]{2,1,0:T(8,128)(2,1)S(1)} %get-tuple-element.879), channel_id=1, source_target_pairs={{0,2},{1,3},{2,0},{3,1},{4,6},{5,7},{6,4},{7,5},{8,10},{9,11},{10,... | collective-permute-start | bytes 1327112 | tf_op jit(solution)/shard_map/ppermute | solution.py:174
  614.5 77.1 %collective-permute-start.98 = (bf16[512,768]{1,0:T(8,128)(2,1)S(1)}, bf16[512,768]{1,0:T(8,128)(2,1)}, u32[]{:S(2)}, u32[]{:S(2)}) collective-permute-start(bf16[512,768]{1,0:T(8,128)(2,1)S(1)} %copy-done.68), channel_id=1, source_target_pairs={{0,16},{1,17},{2,18},{3,19},{4,20},{5,21},{6,22},{7,23},{8,24},{9,... | collective-permute-start | bytes 2359304 | tf_op jit(solution)/shard_map/ppermute | solution.py:183
  622.9 32.9 %collective-permute-start.104 = (bf16[384,768]{1,0:T(8,128)(2,1)S(1)}, bf16[384,768]{1,0:T(8,128)(2,1)}, u32[]{:S(2)}, u32[]{:S(2)}) collective-permute-start(bf16[384,768]{1,0:T(8,128)(2,1)S(1)} %pad_maximum_fusion.8), channel_id=1, source_target_pairs={{0,1},{1,0},{2,3},{3,2},{4,5},{5,4},{6,7},{7,6},{8,9},{9,8},{10,11... | collective-permute-start | bytes 1769480 | tf_op jit(solution)/shard_map/ppermute | solution.py:174
  665.1 26.5 %collective-permute-start.97 = (bf16[512,768]{1,0:T(8,128)(2,1)S(1)}, bf16[512,768]{1,0:T(8,128)(2,1)S(1)}, u32[]{:S(2)}, u32[]{:S(2)}) collective-permute-start(bf16[512,768]{1,0:T(8,128)(2,1)S(1)} %add_add_fusion.4), channel_id=1, source_target_pairs={{16,0},{17,1},{18,2},{19,3},{20,4},{21,5},{22,6},{23,7},{24,8},{25... | collective-permute-start | bytes 2359304 | tf_op jit(solution)/shard_map/ppermute | solution.py:183
  (253 other events, 2248.3 us)

commit v3 on v2

v3 whole, which is shorter than its diff:
```python
import functools

import jax
import jax.numpy as jnp
from jax import lax
from jax.experimental import pallas as pl
from jax.experimental.pallas import tpu as pltpu
from jax.sharding import PartitionSpec as P

HEADS = 12
ROWS = 512
MICRO = 2


EPSILON = 1e-05
MASKED_SCORE = -1e30

SHORT = pl.CostEstimate(flops=1, bytes_accessed=1, transcendentals=0)


def layer_norm(hidden, norm_gain, norm_shift):
    center = hidden - jnp.mean(hidden, axis=-1, keepdims=True)
    spread = jnp.mean(center * center, axis=-1, keepdims=True)
    return center * lax.rsqrt(spread + EPSILON) * norm_gain + norm_shift


def slot_layout(counts, row_count):
    bounds = jnp.cumsum(counts, dtype=jnp.int32)
    places = jnp.arange(row_count, dtype=jnp.int32)
    segment = jnp.sum(
        (bounds[None, :] <= places[:, None]).astype(jnp.int32), axis=1, dtype=jnp.int32
    )
    living = (places < bounds[-1]).astype(jnp.float32)
    return (segment, living)


def gelu_tanh(values):
    return jax.nn.gelu(values, approximate=True)


def contract_rows(left_side, right_side):
    return lax.dot_general(
        left_side, right_side, (((0,), (0,)), ((), ())), preferred_element_type=jnp.float32
    )


def times_transpose(left_side, right_side):
    return lax.dot_general(
        left_side, right_side, (((1,), (1,)), ((), ())), preferred_element_type=jnp.float32
    )


def masked_bias(segment_column, segment_row):
    row_count = segment_column.shape[0]
    query_places = lax.broadcasted_iota(jnp.int32, (row_count, row_count), 0)
    key_places = lax.broadcasted_iota(jnp.int32, (row_count, row_count), 1)
    allowed = (segment_column == segment_row) & (key_places <= query_places)
    return jnp.where(allowed, 0.0, MASKED_SCORE)


def head_lanes(block, head):
    half = block.shape[1] // 2
    lanes = lax.broadcasted_iota(jnp.int32, block.shape, 1)
    return jnp.where((lanes < half) == (head == 0), block, jnp.zeros_like(block))


def attend_kernel(column_ref, row_ref, q_ref, k_ref, v_ref, mixed_ref, log_ref, bias_ref):
    @pl.when(pl.program_id(0) == 0)
    def _():
        bias_ref[...] = masked_bias(column_ref[...], row_ref[...])

    row_count, width = q_ref.shape
    tall = row_count // 2
    scale = (width // 2) ** (-0.5)
    first_lanes = lax.broadcasted_iota(jnp.int32, (tall, width), 1) < width // 2
    for start in (0, tall):
        stop = start + tall
        queries = q_ref[start:stop] * jnp.asarray(scale, q_ref.dtype)
        outs, logs = [], []
        for head in range(2):
            scores = times_transpose(head_lanes(queries, head), k_ref[:stop])
            scores = scores + bias_ref[start:stop, :stop]
            row_max = jnp.max(scores, axis=1, keepdims=True)
            exponent = jnp.exp(scores - row_max)
            row_total = jnp.sum(exponent, axis=1, keepdims=True)
            probs = (exponent * (1.0 / row_total)).astype(jnp.bfloat16)
            outs.append(jnp.dot(probs, v_ref[:stop], preferred_element_type=jnp.float32))
            logs.append(jnp.broadcast_to(row_max + jnp.log(row_total), (tall, width)))
        mixed_ref[start:stop] = jnp.where(first_lanes, *outs).astype(jnp.bfloat16)
        log_ref[start:stop] = jnp.where(first_lanes, *logs)


def attend_back_kernel(
    column_ref, row_ref, q_ref, k_ref, v_ref, grad_ref, log_ref, dq_ref, dk_ref, dv_ref, bias_ref
):
    @pl.when(pl.program_id(0) == 0)
    def _():
        bias_ref[...] = masked_bias(column_ref[...], row_ref[...])

    row_count, width = q_ref.shape
    tall = row_count // 2
    scale = (width // 2) ** (-0.5)
    first_lanes = lax.broadcasted_iota(jnp.int32, (tall, width), 1) < width // 2
    key_parts, value_parts = [], []
    for start in (0, tall):
        stop = start + tall
        queries = q_ref[start:stop] * jnp.asarray(scale, q_ref.dtype)
        query_parts = []
        key_grad = value_grad = 0.0
        for head in range(2):
            mine = head_lanes(queries, head)
            grad = head_lanes(grad_ref[start:stop], head)
            lane = head * (width // 2)
            scores = times_transpose(mine, k_ref[:stop]) + bias_ref[start:stop, :stop]
            probs = jnp.exp(scores - log_ref[start:stop, lane : lane + 1])
            prob_grad = times_transpose(grad, v_ref[:stop])
            center = jnp.sum(prob_grad * probs, axis=1, keepdims=True)
            score_grad = (probs * (prob_grad - center)).astype(jnp.bfloat16)
            query_parts.append(
                jnp.dot(score_grad, k_ref[:stop], preferred_element_type=jnp.float32)
            )
            key_grad = key_grad + contract_rows(score_grad, mine)
            value_grad = value_grad + contract_rows(probs.astype(jnp.bfloat16), grad)
        dq_ref[start:stop] = (jnp.where(first_lanes, *query_parts) * scale).astype(jnp.bfloat16)
        key_parts.append(key_grad)
        value_parts.append(value_grad)
    for parts, target in ((key_parts, dk_ref), (value_parts, dv_ref)):
        target[:tall] = (parts[0] + parts[1][:tall]).astype(jnp.bfloat16)
        target[tall:] = parts[1][tall:].astype(jnp.bfloat16)


def attention_call(kernel, segment, blocks, outs):
    row_count = segment.shape[0]
    pairs = HEADS // 2
    model_width = blocks[0][0].shape[1] // 3
    lanes = model_width // pairs

    def spec(first):
        return pl.BlockSpec((row_count, lanes), lambda pair: (0, first + pair))

    return pl.pallas_call(
        kernel,
        grid=(pairs,),
        out_shape=[jax.ShapeDtypeStruct((row_count, model_width), kind) for kind in outs],
        in_specs=[
            pl.BlockSpec((row_count, 1), lambda pair: (0, 0)),
            pl.BlockSpec((1, row_count), lambda pair: (0, 0)),
        ]
        + [spec(first) for _, first in blocks],
        out_specs=[spec(0) for _ in outs],
        scratch_shapes=[pltpu.VMEM((row_count, row_count), jnp.float32)],
        compiler_params=pltpu.CompilerParams(vmem_limit_bytes=48 * 1024 * 1024),
        cost_estimate=SHORT,
    )(segment[:, None], segment[None, :], *(array for array, _ in blocks))


def attend_forward(joint_low, segment):
    pairs = HEADS // 2
    blocks = [(joint_low, first * pairs) for first in range(3)]
    return attention_call(attend_kernel, segment, blocks, (jnp.bfloat16, jnp.float32))


def attend_backward(joint_low, log_sums, mixed_grad, segment):
    pairs = HEADS // 2
    blocks = [(joint_low, first * pairs) for first in range(3)]
    blocks += [(mixed_grad, 0), (log_sums, 0)]
    parts = attention_call(attend_back_kernel, segment, blocks, (jnp.bfloat16,) * 3)
    return jnp.concatenate(parts, axis=1)


def swap(block, axis, bit):
    return lax.ppermute(block, axis, [(i, i ^ bit) for i in range(lax.axis_size(axis))])


def turn(block, axis, step):
    size = lax.axis_size(axis)
    return lax.ppermute(block, axis, [((i + step) % size, i) for i in range(size)])


def one_way(block, axis, source, target):
    return lax.ppermute(block, axis, [(source, target)])


def place_kernel(widths, where_ref, mine, theirs, *refs):
    outs, held, in_sems, out_sems = refs[:-3], refs[-3], refs[-2], refs[-1]
    section, core, side = (where_ref[i] for i in range(3))

    def run(same, other):
        steps = []
        for rank_core, pieces in ((core, mine), (1 - core, theirs)):
            for i in range(16):
                block = (same, other, same, other)[i // 4]
                to_side = (side, side, 1 - side, 1 - side)[i // 4]
                slot = held.at[len(steps)]
                load = pltpu.make_async_copy(pieces.at[i], slot, in_sems.at[len(steps)])
                load.start()
                stores, start = [], 0
                for index, width in enumerate(widths):
                    target = outs[block * len(widths) + index].at[i % 4, rank_core * 2 + to_side]
                    stores.append((slot.at[:, start : start + width], target))
                    start += width
                steps.append((load, stores))
        begun = []
        for load, stores in steps:
            load.wait()
            for source, target in stores:
                store = pltpu.make_async_copy(source, target, out_sems.at[len(begun)])
                store.start()
                begun.append(store)
        for store in begun:
            store.wait()

    @pl.when(section == 0)
    def _():
        run(0, 1)

    @pl.when(section == 1)
    def _():
        run(1, 0)


def place(pieces, where, widths=None):
    rows, columns = pieces[0].shape[1:]
    kind = pieces[0].dtype
    widths = widths or (columns,)
    shapes = [jax.ShapeDtypeStruct((4, 4, rows, width), kind) for width in widths] * 2
    return pl.pallas_call(
        functools.partial(place_kernel, widths),
        out_shape=shapes,
        in_specs=[pl.BlockSpec(memory_space=pltpu.SMEM)]
        + [pl.BlockSpec(memory_space=pl.ANY)] * len(pieces),
        out_specs=[pl.BlockSpec(memory_space=pl.ANY)] * len(shapes),
        scratch_shapes=[
            pltpu.VMEM((32, rows, columns), kind),
            pltpu.SemaphoreType.DMA((32,)),
            pltpu.SemaphoreType.DMA((32 * len(widths),)),
        ],
        compiler_params=pltpu.CompilerParams(vmem_limit_bytes=32 * 1024 * 1024),
        cost_estimate=SHORT,
    )(where, *pieces)


def add_low(first, second):
    return (first.astype(jnp.float32) + second.astype(jnp.float32)).astype(jnp.bfloat16)


def pick(array, index, axis):
    return lax.dynamic_index_in_dim(array, index, axis, keepdims=False)


def local_call(kernel, where, arrays, outs, scratch=(), steps=1, kind=jnp.bfloat16):
    def spec(shape, first):
        if first is None:
            return pl.BlockSpec(shape, lambda i: (0,) * len(shape))
        block = (1, *shape[1:])
        return pl.BlockSpec(block, lambda i: (first + i,) + (0,) * (len(shape) - 1))

    pairs = [item if isinstance(item, tuple) else (item, None) for item in arrays]
    return pl.pallas_call(
        kernel,
        grid=(steps,),
        out_shape=[jax.ShapeDtypeStruct(shape, kind) for shape in outs],
        in_specs=[pl.BlockSpec(memory_space=pltpu.SMEM)]
        + [spec(array.shape, first) for array, first in pairs],
        out_specs=[spec(shape, None if steps == 1 else 0) for shape in outs],
        scratch_shapes=list(scratch),
        compiler_params=pltpu.CompilerParams(vmem_limit_bytes=48 * 1024 * 1024),
        cost_estimate=SHORT,
    )(where, *(array for array, _ in pairs))


def across_kernel(where_ref, own, got, own_high, got_high, *outs):
    low_keep, low_send, high_keep, high_send = outs
    section, side = where_ref[0], where_ref[2]
    rows, half = low_keep.shape[2:]

    def total(first, second, to_side, start, width):
        place = (
            0,
            pl.ds(pl.multiple_of(to_side * rows, 16), rows),
            pl.ds(pl.multiple_of(start, 128), width),
        )
        return add_low(first[place], second[place])

    for to_side in range(2):
        low_keep[0, to_side] = total(own, got, to_side, section * half, half)
        low_send[0, to_side] = total(own, got, to_side, (1 - section) * half, half)
    high_keep[0] = total(own_high, got_high, side, 0, 2 * half)
    high_send[0] = total(own_high, got_high, 1 - side, 0, 2 * half)


def along_kernel(
    where_ref, low, high, low_got, high_got, low_keep, low_send, high_keep, high_send
):
    section, side = where_ref[0], where_ref[2]
    half = low_keep.shape[2]
    for to_side, target in ((side, low_keep), (1 - side, low_send)):
        target[0] = add_low(low[0, to_side], low_got[0, to_side])
    for to_section, target in ((section, high_keep), (1 - section, high_send)):
        columns = pl.ds(pl.multiple_of(to_section * half, 128), half)
        target[0] = add_low(high[0, :, columns], high_got[0, :, columns])


def shards_kernel(where_ref, low, high, low_got, high_got, own, *rest):
    sends, both = rest[:3], rest[3]
    here = where_ref[3]
    for shard in range(2):
        both[shard] = add_low(low[shard], low_got[shard])
        both[2 + shard] = add_low(high[shard], high_got[shard])
    own[...] = both[here]
    for i, target in enumerate(sends):
        target[...] = both[lax.rem(here + 3 - i, 4)]


def back_kernel(where_ref, *refs):
    keep, give = refs[-2:]

    def put(first, second):
        start = 0
        for member in range(len(refs) // 8):
            width = refs[member * 8].shape[1]
            for block, target in enumerate((first, second)):
                terms = refs[member * 8 + block * 4 : member * 8 + block * 4 + 4]
                total = sum(term[...].astype(jnp.float32) for term in terms)
                target[:, start : start + width] = total.astype(jnp.bfloat16)
            start += width

    @pl.when(where_ref[0] == 0)
    def _():
        put(keep, give)

    @pl.when(where_ref[0] == 1)
    def _():
        put(give, keep)


def grad_kernel(kinds, where_ref, *refs):
    count = len(kinds)
    lefts, rights = refs[:count], refs[count : 2 * count]
    own, send, sums, total = refs[2 * count :]
    core = where_ref[1]
    step = pl.program_id(0)

    def run(left, right):
        total[...] = contract_rows(left[...], right[...])
        sums[...] = jnp.sum(right[...].astype(jnp.float32), axis=0, keepdims=True)
        parts, rows = own.shape[:2]
        for part in range(parts):
            for to_core, target in ((core, own), (1 - core, send)):
                start = pl.multiple_of((2 * part + to_core) * rows, 32)
                target[part] = total[pl.ds(start, rows), :].astype(jnp.bfloat16)

    first = 0
    for kind, left, right in zip(kinds, lefts, rights):

        @pl.when((step >= first) & (step < first + kind))
        def _(left=left, right=right):
            run(left, right)

        first += kind


def grad_call(where, pairs, deep=False):
    width = 768
    row_count = pairs[0][0].shape[0]
    lefts, rights = [left for left, _ in pairs], [right for _, right in pairs]
    kinds = [max(left.shape[1], right.shape[1]) // width for left, right in pairs]
    steps = sum(kinds)
    firsts = [sum(kinds[:index]) for index in range(len(kinds))]

    def spec(wide, first, kind):
        if not wide:
            return pl.BlockSpec((row_count, width), lambda j: (0, 0))
        return pl.BlockSpec((row_count, width), lambda j: (0, jnp.clip(j - first, 0, kind - 1)))

    in_specs = [pl.BlockSpec(memory_space=pltpu.SMEM)]
    for arrays in (lefts, rights):
        for array, first, kind in zip(arrays, firsts, kinds):
            in_specs.append(spec(array.shape[1] > width, first, kind))
    if deep:
        shape, block = (4, lefts[0].shape[1] // 8, width), (1, lefts[0].shape[1] // 8, width)
        out_spec = pl.BlockSpec(block, lambda j: (j, 0, 0))
        sums_shape, sums_spec = (1, width), pl.BlockSpec((1, width), lambda j: (0, 0))
    else:
        shape, block = (4, width // 8, steps * width), (4, width // 8, width)
        out_spec = pl.BlockSpec(block, lambda j: (0, 0, j))
        sums_shape, sums_spec = (1, steps * width), pl.BlockSpec((1, width), lambda j: (0, j))
    return pl.pallas_call(
        functools.partial(grad_kernel, kinds),
        grid=(steps,),
        out_shape=[jax.ShapeDtypeStruct(shape, jnp.bfloat16)] * 2
        + [jax.ShapeDtypeStruct(sums_shape, jnp.float32)],
        in_specs=in_specs,
        out_specs=[out_spec, out_spec, sums_spec],
        scratch_shapes=[pltpu.VMEM((width, width), jnp.float32)],
        compiler_params=pltpu.CompilerParams(vmem_limit_bytes=40 * 1024 * 1024),
        cost_estimate=SHORT,
    )(where, *lefts, *rights)


GELU_SCALE = 0.7978845608028654
GELU_CUBE = 0.044715


def expand_kernel(normed_ref, weight_ref, bias_ref, active_ref, slope_ref):
    values = jnp.dot(normed_ref[...], weight_ref[...], preferred_element_type=jnp.float32)
    values = values + bias_ref[...]
    square = values * values
    bent = jnp.tanh(GELU_SCALE * values * (1.0 + GELU_CUBE * square))
    half = 0.5 * (1.0 + bent)
    active_ref[...] = (values * half).astype(jnp.bfloat16)
    inner = GELU_SCALE * (1.0 + 3.0 * GELU_CUBE * square)
    slope_ref[...] = (half + 0.5 * values * (1.0 - bent * bent) * inner).astype(jnp.bfloat16)


def expand_call(normed, weight, bias):
    row_count, depth = normed.shape
    columns = weight.shape[1]
    width = depth
    out_spec = pl.BlockSpec((row_count, width), lambda j: (0, j))
    return pl.pallas_call(
        expand_kernel,
        grid=(columns // width,),
        out_shape=[jax.ShapeDtypeStruct((row_count, columns), jnp.bfloat16)] * 2,
        in_specs=[
            pl.BlockSpec((row_count, depth), lambda j: (0, 0)),
            pl.BlockSpec((depth, width), lambda j: (0, j)),
            pl.BlockSpec((1, width), lambda j: (0, j)),
        ],
        out_specs=[out_spec, out_spec],
        compiler_params=pltpu.CompilerParams(vmem_limit_bytes=40 * 1024 * 1024),
        cost_estimate=SHORT,
    )(normed, weight, bias[None])


def ordered(own, other, index, axis):
    first = jnp.where(index == 0, own, other)
    second = jnp.where(index == 0, other, own)
    return jnp.concatenate([first, second], axis=axis)


class Moves:
    def __init__(self, where):
        self.where = where

    over_x = staticmethod(lambda array: swap(array, "section", 1))
    over_y = staticmethod(lambda array: swap(array, "replica", 2))
    to_mate = staticmethod(lambda array: swap(array, "replica", 1))

    def gather(self):
        def along(own):
            return ((), [(own, lambda array: lax.all_gather(array, "shard", axis=0))])

        along.late = 1

        def across(chunks):
            return ((chunks,), [(chunks, self.over_x), (chunks, self.over_y)])

        def beyond(*arrays):
            _, over_x, over_y = arrays
            return (arrays, [(over_x[:2], self.over_y), (over_y[2:], self.over_x)])

        return [along, across, beyond]

    def laid(self, state, widths=None):
        mine = jnp.concatenate(state, axis=0)
        return place((mine, self.to_mate(mine)), self.where, widths)

    def reduce(self):
        def mates(own, send):
            return ((own,), [(send, self.to_mate)])

        def across(own, got):
            shards, rows, columns = own.shape
            low = (2, 2, rows // 2, columns // 2)
            high = (2, rows // 2, columns)
            result = local_call(
                across_kernel,
                self.where,
                ((own, 0), (got, 0), (own, 2), (got, 2)),
                (low, low, high, high),
                steps=2,
            )
            low_keep, low_send, high_keep, high_send = result
            return ((low_keep, high_keep), [(low_send, self.over_x), (high_send, self.over_y)])

        def along(*state):
            shape = (2, *state[0].shape[2:])
            result = local_call(
                along_kernel, self.where, [(array, 0) for array in state], (shape,) * 4, steps=2
            )
            low_keep, low_send, high_keep, high_send = result
            return ((low_keep, high_keep), [(low_send, self.over_y), (high_send, self.over_x)])

        def shards(*state):
            shape = state[0].shape[1:]
            scratch = [pltpu.VMEM((4, *shape), jnp.bfloat16)]
            result = local_call(shards_kernel, self.where, state, (shape,) * 4, scratch)
            turns = [functools.partial(turn, axis="shard", step=i) for i in (1, 2, 3)]
            return ((result[0],), list(zip(result[1:], turns)))

        return [mates, across, along, shards]

    def spread(self):
        def back(*pairs):
            terms = [term for pair in pairs for state in pair for term in state]
            rows = terms[0].shape[0]
            shape = (rows, sum(pair[0][0].shape[1] for pair in pairs))
            keep, give = local_call(back_kernel, self.where, terms, (shape, shape))
            return ((keep,), [(give, self.over_x)])

        def around(keep, got):
            rows = jnp.stack([keep, got])

            def corner(array):
                over_y = self.over_y(array)
                return (over_y, self.to_mate(over_y))

            return ((rows,), [(rows, self.to_mate), (rows, corner)])

        return [back, around]

    @staticmethod
    def exchange(late):
        def step(section, first, second):
            give = jnp.where(section == 0, second, first)
            if not late:
                return ((), [(give, Moves.over_x)])
            return ((), [(give, lambda array: lax.all_gather(array, "section", axis=0))])

        step.late = late
        return [step]

    @staticmethod
    def total():
        def step_of(axis, bit):
            def step(*terms):
                array = sum(terms[1:], terms[0])
                return ((array,), [(array, lambda array: swap(array, axis, bit))])

            return step

        pairs = (("replica", 1), ("section", 1), ("replica", 2), ("shard", 1), ("shard", 2))
        return [step_of(*pair) for pair in pairs]


class Flows:
    def __init__(self):
        self.left = {}
        self.states = {}
        self.open = {}

    def start(self, name, steps, *state):
        self.left[name] = list(steps)
        self.states[name] = state

    def extend(self, name, steps):
        self.left[name] += steps

    def stage(self, compute=lambda: (), *inputs):
        names = [name for name in self.left if self.left[name]]
        steps = [self.left[name].pop(0) for name in names]
        states = [self.states[name] for name in names]
        inputs, states = lax.optimization_barrier((inputs, states))
        ready = [step(*state) for step, state in zip(steps, states)]
        kept = [keep for keep, _ in ready]
        sent = [[array for array, _ in sends] for _, sends in ready]
        inputs, kept, sent = lax.optimization_barrier((inputs, kept, sent))
        got = [
            [move(array) for array, (_, move) in zip(arrays, sends)]
            for arrays, (_, sends) in zip(sent, ready)
        ]
        late = [getattr(step, "late", 0) for step in steps]
        waited = [result for result, slow in zip(got, late) if not slow]
        due = [name for name in self.open if self.open[name] == 1]
        closing = [self.states[name] for name in due]
        results, waited, closing = lax.optimization_barrier((compute(*inputs), waited, closing))
        self.states.update(zip(due, closing))
        self.open = {name: left - 1 for name, left in self.open.items() if left > 1}
        self.open.update({name: slow for name, slow in zip(names, late) if slow})
        waited = iter(waited)
        for name, keep, result, slow in zip(names, kept, got, late):
            self.states[name] = (*keep, *(result if slow else next(waited)))
        return results


def close_kernel(where_ref, *refs):
    section, core, side = (where_ref[i] for i in range(3))
    wide_pieces, last_pieces = refs[:4], refs[4:8]
    input_out, expand_out, output_out, contract_out = refs[8:]
    input_half = input_out.shape[1] // 2
    contract_half = contract_out.shape[1] // 2
    split = expand_out.shape[1] - (wide_pieces[0].shape[2] - input_half)

    def one(far_core, far_side, far_section):
        at_section = section if far_section == 0 else 1 - section
        at_side = side if far_side == 0 else 1 - side
        at_core = core if far_core == 0 else 1 - core
        rank = at_core * 2 + at_side
        wide = wide_pieces[far_core * 2 + far_side][far_section].astype(jnp.float32)
        rows = pl.ds(pl.multiple_of(rank * wide.shape[0], 16), wide.shape[0])
        columns = pl.ds(pl.multiple_of(at_section * input_half, 128), input_half)
        input_out[rows, columns] = wide[:, :input_half]
        wide = wide[:, input_half:]

        @pl.when(at_section == 0)
        def _():
            expand_out[rows, : wide.shape[1]] = wide

        @pl.when(at_section == 1)
        def _():
            expand_out[rows, wide.shape[1] :] = wide[:, :split]
            output_out[rows, :] = wide[:, split:]

        last = last_pieces[far_core * 2 + far_side][far_section].astype(jnp.float32)
        rows = pl.ds(pl.multiple_of(rank * last.shape[0], 16), last.shape[0])
        columns = pl.ds(pl.multiple_of(at_section * contract_half, 128), contract_half)
        contract_out[rows, columns] = last

    for far_core in range(2):
        for far_side in range(2):
            for far_section in range(2):
                one(far_core, far_side, far_section)


def close(where, wide, contract, shapes):
    def pieces(state):
        own, mate, (over_y, mate_y) = state
        return (own, over_y, mate, mate_y)

    arrays = (*pieces(wide), *pieces(contract))
    return local_call(close_kernel, where, arrays, shapes, kind=jnp.float32)

VECTORS = ("gain_a", "shift_a", "bias_q", "bias_v", "bias_o", "gain_f", "shift_f", "bias_c")


def forward_attention(params, hidden_low, segment):
    hidden = hidden_low.astype(jnp.float32)
    normed = layer_norm(hidden, params["gain_a"], params["shift_a"]).astype(jnp.bfloat16)
    zeros = jnp.zeros_like(params["bias_q"])
    joint_bias = jnp.concatenate([params["bias_q"], zeros, params["bias_v"]])
    joint_low = (
        jnp.dot(normed, params["input"], preferred_element_type=jnp.float32) + joint_bias
    ).astype(jnp.bfloat16)
    mixed_low, log_sums = attend_forward(joint_low, segment)
    middle = (
        hidden
        + jnp.dot(mixed_low, params["output"], preferred_element_type=jnp.float32)
        + params["bias_o"]
    )
    return dict(
        hidden_low=hidden_low,
        normed=normed,
        joint_low=joint_low,
        log_sums=log_sums,
        mixed_low=mixed_low,
        middle=middle,
    )


def forward_expand(params, middle):
    normed_two = layer_norm(middle, params["gain_f"], params["shift_f"]).astype(jnp.bfloat16)
    activated, slope = expand_call(normed_two, params["expand"], params["bias_e"])
    return dict(normed_two=normed_two, slope=slope, activated=activated)


def forward_contract(params, middle, activated, living):
    result = (
        middle
        + jnp.dot(activated, params["contract"], preferred_element_type=jnp.float32)
        + params["bias_c"]
    )
    return (result * living[:, None]).astype(jnp.bfloat16)


class Backward:
    def __init__(self, params, kept, segment, living, where, upstream):
        self.params, self.segment, self.living, self.where = params, segment, living, where
        self.held = dict(kept, upstream=upstream)

    def run(self, flow, part):
        function, names = {
            "expand": (self.expand, ("upstream", "activated", "slope")),
            "norm": (
                self.norm,
                ("expand_low", "normed_two", "out_grad", "middle", "mixed_low"),
            ),
            "attention": (self.attention, ("joint_low", "log_sums", "mixed_grad")),
            "input": (self.input, ("normed", "joint_grad")),
            "last": (self.last, ("joint_grad", "middle_grad", "hidden_low")),
            "both": (self.both, ("normed", "joint_grad", "middle_grad", "hidden_low")),
        }[part]
        self.held.update(flow.stage(function, *(self.held[name] for name in names)))

    def grads(self, name, *pairs, deep=False):
        if self.where is not None:
            own, send, sums = grad_call(self.where, pairs, deep)
            return {name + "_own": own, name + "_send": send, name + "_sums": sums[0]}
        whole = jnp.concatenate([contract_rows(*pair).astype(jnp.bfloat16) for pair in pairs], axis=1)
        sums = [jnp.sum(right.astype(jnp.float32), axis=0) for _, right in pairs]
        return {name + "_own": whole, name + "_sums": jnp.concatenate(sums)}

    def expand(self, upstream, activated, slope):
        out_grad = upstream.astype(jnp.float32) * self.living[:, None]
        low = out_grad.astype(jnp.bfloat16)
        found = self.grads("contract", (activated, low), deep=True)
        activated_grad = times_transpose(low, self.params["contract"])
        expand_low = (activated_grad * slope.astype(jnp.float32)).astype(jnp.bfloat16)
        return dict(found, out_grad=out_grad, expand_low=expand_low)

    def norm(self, expand_low, normed_two, out_grad, middle, mixed_low):
        normed_grad = times_transpose(expand_low, self.params["expand"])
        _, pull = jax.vjp(layer_norm, middle, self.params["gain_f"], self.params["shift_f"])
        norm_grad, gain_grad, shift_grad = pull(normed_grad)
        middle_grad = out_grad + norm_grad
        branch_low = middle_grad.astype(jnp.bfloat16)
        mixed_grad = times_transpose(branch_low, self.params["output"]).astype(jnp.bfloat16)
        found = self.grads("expand", (normed_two, expand_low), (mixed_low, branch_low))
        return dict(
            found, middle_grad=middle_grad, mixed_grad=mixed_grad, gain_f=gain_grad, shift_f=shift_grad
        )

    def attention(self, joint_low, log_sums, mixed_grad):
        return dict(joint_grad=attend_backward(joint_low, log_sums, mixed_grad, self.segment))

    def input(self, normed, joint_grad):
        return self.grads("input", (normed, joint_grad))

    def last(self, joint_grad, middle_grad, hidden_low):
        normed_grad = times_transpose(joint_grad, self.params["input"])
        _, pull = jax.vjp(
            layer_norm,
            hidden_low.astype(jnp.float32),
            self.params["gain_a"],
            self.params["shift_a"],
        )
        norm_grad, gain_grad, shift_grad = pull(normed_grad)
        grad = middle_grad + norm_grad
        return dict(grad_low=grad.astype(jnp.bfloat16), gain_a=gain_grad, shift_a=shift_grad)

    def both(self, normed, joint_grad, middle_grad, hidden_low):
        found = self.input(normed, joint_grad)
        return dict(found, **self.last(joint_grad, middle_grad, hidden_low))

    def small(self):
        held = self.held
        width = held["gain_a"].shape[0]
        split = held["expand_sums"].shape[0] - width
        held = dict(
            held,
            bias_q=held["input_sums"][:width],
            bias_v=held["input_sums"][2 * width :],
            bias_o=held["expand_sums"][split:],
            bias_c=held["contract_sums"],
        )
        vectors = [held[name] for name in VECTORS] + [held["expand_sums"][:split]]
        return jnp.concatenate(vectors).reshape(-1, width)


def per_device(
    tokens,
    cotangent,
    lengths,
    assignment,
    attention_gain,
    attention_shift,
    input_weight,
    query_bias,
    value_bias,
    output_weight,
    output_bias,
    feedforward_gain,
    feedforward_shift,
    expand_weight,
    expand_bias,
    contract_weight,
    contract_bias,
):
    section = lax.axis_index("section")
    shard = lax.axis_index("shard")
    replica = lax.axis_index("replica")
    shards, replicas = lax.axis_size("shard"), lax.axis_size("replica")
    core, side = replica % 2, replica // 2
    model_width = tokens.shape[1]
    cube = shards == 4 and replicas == 4
    where = jnp.stack([section, core, side, shard]).astype(jnp.int32)

    slot = (shard * replicas + replica) * MICRO + section
    matches = (assignment == slot).astype(jnp.int32)
    counts = jnp.sum(matches[:, None] * lengths, axis=0, dtype=jnp.int32)
    segment, living = slot_layout(counts, ROWS)
    entering = lax.dynamic_slice_in_dim(tokens, section * ROWS, ROWS, 0)
    seed = lax.dynamic_slice_in_dim(cotangent, section * ROWS, ROWS, 0)

    vectors = (
        attention_gain,
        attention_shift,
        query_bias,
        value_bias,
        output_bias,
        feedforward_gain,
        feedforward_shift,
        contract_bias,
        expand_bias,
    )
    small_own = jnp.concatenate(vectors, axis=1)
    expand_width = expand_weight.shape[2]
    flow = Flows()
    moves = Moves(where)

    def joined(members):
        return [member.reshape(-1, member.shape[-1]) for member in members]

    def named(small_all, **pairs):
        count = len(VECTORS)
        split = small_all.shape[2] - expand_bias.shape[1]
        lines = small_all[:, :, :split].reshape(2, shards, count, split // count)
        lines = lines.transpose(0, 2, 1, 3).reshape(2, count, model_width).astype(jnp.float32)
        bias_e = small_all[:, :, split:].reshape(2, expand_width).astype(jnp.float32)
        found = []
        for block in range(2):
            params = {name: lines[block, index] for index, name in enumerate(VECTORS)}
            params["bias_e"] = bias_e[block]
            params.update({name: pair[block] for name, pair in pairs.items()})
            found.append(params)
        return found

    if cube:

        def chunk(weight):
            size = weight.shape[1] // 4
            return lax.dynamic_slice_in_dim(weight[0], (core * 2 + side) * size, size, 0)

        input_chunk, output_chunk = chunk(input_weight), chunk(output_weight)
        small_rows = small_own.shape[1] // 128
        short = input_chunk.shape[0] - small_rows
        padded = jnp.pad(small_own.reshape(small_rows, 128), ((0, short), (0, 0)))
        opening = jnp.concatenate([input_chunk, output_chunk, padded], axis=1)
        widths = (input_chunk.shape[1], output_chunk.shape[1], 128)
        flow.start("gather_open", moves.gather(), opening)
        flow.stage()
        flow.start("gather_expand", moves.gather(), chunk(expand_weight))
        flow.stage()
        flow.start("gather_contract", moves.gather(), chunk(contract_weight))
        flow.stage()

        def open_part(state, hidden_low):
            laid = moves.laid(state, widths)
            small_all = jnp.stack(laid[2::3])[:, :, 0, :small_rows].reshape(2, shards, -1)
            found = named(small_all, input=joined(laid[0::3]), output=joined(laid[1::3]))
            return (found, forward_attention(found[0], hidden_low, segment))

        (params, kept_first) = flow.stage(open_part, flow.states["gather_open"], entering)

        def middle_part(state, middle):
            expand_all = joined(moves.laid(state))
            held = forward_expand(dict(params[0], expand=expand_all[0]), middle)
            return (expand_all, held)

        expand_all, held = flow.stage(
            middle_part, flow.states["gather_expand"], kept_first["middle"]
        )
        kept_first.update(held)
        contract_all = joined(moves.laid(flow.states["gather_contract"]))
        for block in range(2):
            params[block].update(expand=expand_all[block], contract=contract_all[block])
    else:

        def whole(weight):
            held = lax.all_gather(weight, "shard", axis=1, tiled=True)
            return lax.all_gather(held, "section", axis=0, tiled=True)

        params = named(
            whole(small_own[None]),
            input=whole(input_weight),
            output=whole(output_weight),
            expand=whole(expand_weight),
            contract=whole(contract_weight),
        )
        kept_first = forward_attention(params[0], entering, segment)
        kept_first.update(forward_expand(params[0], kept_first["middle"]))

    middle_out = forward_contract(
        params[0], kept_first["middle"], kept_first["activated"], living
    )

    def second_forward(hidden_low):
        kept = forward_attention(params[1], hidden_low, segment)
        kept.update(forward_expand(params[1], kept["middle"]))
        return (kept, forward_contract(params[1], kept["middle"], kept["activated"], living))

    kept_second, last_out = second_forward(middle_out)

    def begin(block, name):
        tag = ("first_" if block is first else "second_") + name
        if cube:
            flow.start(tag, moves.reduce(), block.held[name + "_own"], block.held[name + "_send"])

    def spread(name, *members):
        if cube:
            pairs = [(flow.states["first_" + m], flow.states["second_" + m]) for m in members]
            flow.start(name, moves.spread(), *pairs)

    first = None
    second = Backward(params[1], kept_second, segment, living, where if cube else None, seed)
    flow.start("out", moves.exchange(0), section, middle_out, last_out)
    second.run(flow, "expand")
    begin(second, "contract")
    second.run(flow, "norm")
    begin(second, "expand")
    second.run(flow, "attention")
    second.run(flow, "both")
    begin(second, "input")

    first = Backward(params[0], kept_first, segment, living, where if cube else None, second.held["grad_low"])
    first.run(flow, "expand")
    begin(first, "contract")
    first.run(flow, "norm")
    begin(first, "expand")
    first.run(flow, "attention")
    first.run(flow, "input")
    begin(first, "input")
    first.run(flow, "last")
    small_both = jnp.stack([first.small(), second.small()])
    flow.start("small", moves.total() if cube else [], small_both)
    flow.start("grad", moves.exchange(4), section, first.held["grad_low"], second.held["grad_low"])
    flow.stage()
    flow.stage()
    flow.stage()
    spread("wide", "input", "expand")
    spread("contract", "contract")
    flow.stage()
    flow.stage()

    def own_block(name, first_value, second_value):
        keep = jnp.where(section == 0, first_value, second_value)
        got = flow.states[name][0]
        got = pick(got, 1 - section, 0) if got.ndim == 3 else got
        return ordered(keep, got, section, 0)

    block_out = own_block("out", middle_out, last_out)
    grad_out = own_block("grad", first.held["grad_low"], second.held["grad_low"])
    grad_out = grad_out.astype(jnp.float32)

    if cube:
        small_sum = flow.states["small"][0] + flow.states["small"][1]
        shapes = [
            weight.shape[1:] for weight in (input_weight, expand_weight, output_weight, contract_weight)
        ]
        large = close(where, flow.states["wide"], flow.states["contract"], shapes)
    else:
        small_sum = lax.psum(small_both, ("section", "shard", "replica"))
        large = []
        for name in ("input_own", "expand_own", "contract_own"):
            wide = jnp.stack([block.held[name] for block in (first, second)])
            held = lax.psum_scatter(wide, "section", scatter_dimension=0, tiled=True)
            held = lax.psum_scatter(held[0], "shard", scatter_dimension=0, tiled=True)
            large.append(lax.psum(held, "replica").astype(jnp.float32))
        large[1:2] = [large[1][:, :expand_width], large[1][:, expand_width:]]
    small_sum = pick(small_sum, section, 0)
    lines = small_sum[: len(VECTORS)].reshape(len(VECTORS), shards, -1)
    lines = pick(lines, shard, 1)
    small = {name: lines[index][None] for index, name in enumerate(VECTORS)}
    bias_e_grad = pick(small_sum[len(VECTORS) :].reshape(shards, -1), shard, 0)[None]
    input_grad, expand_grad, output_grad, contract_grad = (member[None] for member in large)
    return (
        block_out[None],
        grad_out[None],
        small["gain_a"],
        small["shift_a"],
        input_grad,
        small["bias_q"],
        small["bias_v"],
        output_grad,
        small["bias_o"],
        small["gain_f"],
        small["shift_f"],
        expand_grad,
        bias_e_grad,
        contract_grad,
        small["bias_c"],
    )


def solution(mesh):
    placed = (
        P(("shard", "replica"), None),
        P(("shard", "replica"), None),
        P(),
        P(),
        P("section", "shard"),
        P("section", "shard"),
        P("section", "shard", None),
        P("section", "shard"),
        P("section", "shard"),
        P("section", "shard", None),
        P("section", "shard"),
        P("section", "shard"),
        P("section", "shard"),
        P("section", "shard", None),
        P("section", "shard"),
        P("section", "shard", None),
        P("section", "shard"),
    )
    return jax.shard_map(
        per_device,
        mesh=mesh,
        in_specs=placed,
        out_specs=(
            P("section", ("shard", "replica"), None),
            P("section", ("shard", "replica"), None),
            P("section", "shard"),
            P("section", "shard"),
            P("section", "shard", None),
            P("section", "shard"),
            P("section", "shard"),
            P("section", "shard", None),
            P("section", "shard"),
            P("section", "shard"),
            P("section", "shard"),
            P("section", "shard", None),
            P("section", "shard"),
            P("section", "shard", None),
            P("section", "shard"),
        ),
        check_vma=False,
    )
```

time: 707 us -> 660 us (0.934)
  Pallas kernels: 85.6 us -> 153 us
  starting transfers between devices: 122 us -> 67.4 us
  waiting for transfers between devices: 254 us -> 216 us
  other arithmetic: 73.5 us -> 41.8 us
  matrix products: 77.7 us -> 57.3 us
  local copies, waits for them, and re-layouts: 81.5 us -> 98.7 us
  between operations: 4.09 us -> 16.6 us
    pallas_call x4 -> x32, Pallas kernels: 32.9 us -> 99.7 us  [the longest x21 36.7 us: local_call(): pl.pallas_call(kernel, grid=(steps,), out_shape=[jax.ShapeDtypeStruct(sha...]
    ppermute x30 -> x18, waiting for transfers between devices: 97.8 us -> 45 us  [turn(): lax.ppermute(block, axis, [((i + step) % size, i) for i in range(size)])]
    unnamed x356 -> x406, local copies, waits for them, and re-layouts: 32 us -> 72.6 us
    all_gather x0 -> x4, waiting for transfers between devices: none -> 34.3 us  [the longest x3 34.3 us: along(): return ((), [(own, lambda array: lax.all_gather(array, 'shard', axis=0))])]
    ppermute x30 -> x18, starting transfers between devices: 50.4 us -> 19 us  [turn(): lax.ppermute(block, axis, [((i + step) % size, i) for i in range(size)])]
    convert_element_type x54 -> x11, other arithmetic: 38.3 us -> 8.09 us  [the longest x2 2.83 us: norm(): branch_low = middle_grad.astype(jnp.bfloat16)]
    dot_general x16 -> x6, matrix products: 45.1 us -> 16.5 us  [the longest x2 6.78 us: forward_contract(): jnp.dot(activated, params['contract'], preferred_element_type=jnp.float32)]
    ppermute x82 -> x59, waiting for transfers between devices: 157 us -> 137 us  [swap(): lax.ppermute(block, axis, [(i, i ^ bit) for i in range(lax.axis_size(axis...]
  transfers between devices with their start and end apart: 116 -> 81, of which waited for: 54 -> 29; matrix products, arithmetic and copies ran while one was open for 15% -> 12% of each run, Pallas kernels for 5% -> 13%
where the time goes in v3:
time: 660 us; the launch traced here: 650 us
  waiting for transfers between devices  216 us (33%)
  Pallas kernels  153 us (23%)
  local copies, waits for them, and re-layouts  98.7 us (15%)
  starting transfers between devices  67.4 us (10%)
  matrix products  57.3 us (9%)
  other arithmetic  41.8 us (6%)
  between operations  16.6 us (3%)
    ppermute x59, waiting for transfers between devices, swap(): lax.ppermute(block, axis, [(i, i ^ bit) for i in range(lax.axis_size(axis...  137 us
    unnamed x406, local copies, waits for them, and re-layouts  72.6 us
    pallas_call x4, Pallas kernels, attention_call(): pl.pallas_call(kernel, grid=(pairs,), out_shape=[jax.ShapeDtypeStruct((ro...  52.9 us
    ppermute x59, starting transfers between devices, swap(): lax.ppermute(block, axis, [(i, i ^ bit) for i in range(lax.axis_size(axis...  48.3 us
    ppermute x18, waiting for transfers between devices, turn(): lax.ppermute(block, axis, [((i + step) % size, i) for i in range(size)])  45 us
    dot_general x8, matrix products, times_transpose(): lax.dot_general(left_side, right_side, (((1,), (1,)), ((), ())), preferre...  40.8 us
    pallas_call x21, Pallas kernels, local_call(): pl.pallas_call(kernel, grid=(steps,), out_shape=[jax.ShapeDtypeStruct(sha...  36.7 us
    all_gather x3, waiting for transfers between devices, along(): return ((), [(own, lambda array: lax.all_gather(array, 'shard', axis=0))])  34.3 us
  transfers between devices with their start and end apart: 81, of which 29 were waited for; matrix products, arithmetic and copies ran while one was open for 12% of the time, Pallas kernels for 13%

profile of v3, /device:TPU:0, one launch (start us, length us, event | category | flops | bytes accessed | tf_op | source)
XLA Modules:
  0.0 650.4 jit_solution(66603177301338587)
XLA Ops:
  12.7 32.4 %all-gather.9.cloned.1.call-done = bf16[192,3200]{1,0:T(8,128)(2,1)} async-done(((bf16[48,3200]{1,0:T(8,128)(2,1)}), bf16[192,3200]{1,0:T(8,128)(2,1)}) %all-gather.9.cloned.1.call-update) | async-done | bytes 1228816 | tf_op jit(solution)/shard_map/all_gather | solution.py:452
  49.9 23.7 %collective-permute-done = bf16[4,48,3200]{2,1,0:T(8,128)(2,1)S(1)} collective-permute-done((bf16[4,48,3200]{2,1,0:T(8,128)(2,1)}, bf16[4,48,3200]{2,1,0:T(8,128)(2,1)S(1)}, u32[]{:S(2)}, u32[]{:S(2)}) %collective-permute-start) | collective-permute-done | bytes 1228832 | tf_op jit(solution)/shard_map/ppermute | solution.py:172
  83.9 37.6 %collective-permute-done.2 = bf16[2,48,3200]{2,1,0:T(8,128)(2,1)S(1)} collective-permute-done((bf16[2,48,3200]{2,1,0:T(8,128)(2,1)}, bf16[2,48,3200]{2,1,0:T(8,128)(2,1)S(1)}, u32[]{:S(2)}, u32[]{:S(2)}) %collective-permute-start.2) | collective-permute-done | bytes 614432 | tf_op jit(solution)/shard_map/ppermute | solution.py:172
  141.6 5.7 shard_map.280
  158.1 11.7 %shard_map.281 = (bf16[512,768]{1,0:T(8,128)(2,1)S(1)}, f32[512,768]{1,0:T(8,128)S(1)}) custom-call(s32[512,1]{1,0:T(8,128)S(1)} %copy.38.column_ref, s32[1,512]{1,0:T(1,128)S(1)} %bitcast.115, bf16[512,2304]{1,0:T(8,128)(2,1)S(1)} %fusion.q_ref.k_ref.v_ref, bf16[512,2304]{1,0:T(8,128)(2,1)S(1)} %fusion.q_ref.k_ref.v_ref, ...), custom_call_target="tpu_custom_call" | custom-call | flops 1 | bytes 1 | tf_op jit(solution)/shard_map/pallas_call | solution.py:141
  197.1 5.1 shard_map.282
  204.3 6.8 %shard_map.283 = (bf16[512,3072]{1,0:T(8,128)(2,1)S(1)}, bf16[512,3072]{1,0:T(8,128)(2,1)S(1)}) custom-call(bf16[512,768]{1,0:T(8,128)(2,1)S(1)} %add_convert_fusion.3.normed_ref.refs_0_, bf16[768,3072]{1,0:T(8,128)(2,1)S(1)} %bitcast.104, f32[1,3072]{1,0:T(1,128)S(1)} %bitcast.120), custom_call_target="tpu_custom_call" | custom-call | flops 1 | bytes 1 | tf_op jit(solution)/shard_map/pallas_call | solution.py:421
  218.2 6.5 collective-permute-done.14.theirs
  224.7 5.1 shard_map.284
  237.9 11.9 %shard_map.285 = (bf16[512,768]{1,0:T(8,128)(2,1)S(1)}, f32[512,768]{1,0:T(8,128)S(1)}) custom-call(s32[512,1]{1,0:T(8,128)S(1)} %copy.38.column_ref, s32[1,512]{1,0:T(1,128)S(1)} %bitcast.116, bf16[512,2304]{1,0:T(8,128)(2,1)S(1)} %fusion.1.q_ref.k_ref.v_ref, bf16[512,2304]{1,0:T(8,128)(2,1)S(1)} %fusion.1.q_ref.k_ref.v_ref, ...), custom_call_target="tpu_custom_call" | custom-call | flops 1 | bytes 1 | tf_op jit(solution)/shard_map/pallas_call | solution.py:141
  253.8 6.8 %shard_map.286 = (bf16[512,3072]{1,0:T(8,128)(2,1)S(1)}, bf16[512,3072]{1,0:T(8,128)(2,1)S(1)}) custom-call(bf16[512,768]{1,0:T(8,128)(2,1)S(1)} %add_convert_fusion.2.normed_ref.refs_0_, bf16[768,3072]{1,0:T(8,128)(2,1)S(1)} %bitcast.109, f32[1,3072]{1,0:T(1,128)S(1)} %bitcast.119), custom_call_target="tpu_custom_call" | custom-call | flops 1 | bytes 1 | tf_op jit(solution)/shard_map/pallas_call | solution.py:421
  269.5 5.8 shard_map.287
  277.3 7.3 %multiply_convert_fusion.1.refs_2_ = bf16[512,3072]{1,0:T(8,128)(2,1)} fusion(bf16[512,3072]{1,0:T(8,128)(2,1)} %copy-done.117, bf16[512,768]{1,0:T(8,128)(2,1)S(1)} %get-tuple-element.1274.refs_1_, bf16[3072,768]{1,0:T(8,128)(2,1)} %bitcast.123), kind=kOutput, calls=%fused_computation.1 | convolution fusion | flops 2420637696 | bytes 11796480 | tf_op jit(solution)/shard_map/dot_general | solution.py:48
  287.3 6.8 %multiply_reduce_fusion.3 = (f32[768]{0:T(1024)}, f32[512]{0:T(512)S(1)}, f32[768]{0:T(1024)}, f32[512,768]{1,0:T(8,128)S(1)}) fusion(f32[512,768]{1,0:T(8,128)S(1)} %get-tuple-element.755, f32[512]{0:T(512)S(1)} %fusion.40, f32[512]{0:T(512)S(1)} %broadcast_multiply_fusion.3, f32[768]{0:T(1024)S(1)} %get-tuple-element.722, ...), kind=kOutput, calls=%fused_computation.61 | convolution fusion | flops 2419062784 | bytes 11025408 | tf_op jit(solution)/shard_map/dot_general | solution.py:48
  298.7 6.5 shard_map.288
  314.2 14.6 %shard_map.290 = (bf16[512,768]{1,0:T(8,128)(2,1)S(1)}, bf16[512,768]{1,0:T(8,128)(2,1)S(1)}, bf16[512,768]{1,0:T(8,128)(2,1)S(1)}) custom-call(s32[512,1]{1,0:T(8,128)S(1)} %copy.38.column_ref, s32[1,512]{1,0:T(1,128)S(1)} %bitcast.117, bf16[512,2304]{1,0:T(8,128)(2,1)} %copy-done.3, bf16[512,2304]{1,0:T(8,128)(2,1)} %copy-done.3, ...), custom_call_target="tpu_custom_call" | custom-call | flops 1 | bytes 1 | tf_op jit(solution)/shard_map/pallas_call | solution.py:141
  334.6 4.9 shard_map.293
  341.6 5.8 fusion.57
  353.4 19.7 %collective-permute-done.20.low_got = bf16[2,192,384]{2,1,0:T(8,128)(2,1)S(1)} collective-permute-done((bf16[2,192,384]{2,1,0:T(8,128)(2,1)S(1)}, bf16[2,192,384]{2,1,0:T(8,128)(2,1)S(1)}, u32[]{:S(2)}, u32[]{:S(2)}) %collective-permute-start.20) | collective-permute-done | bytes 294944 | tf_op jit(solution)/shard_map/ppermute | solution.py:172
  383.9 6.6 %multiply_convert_fusion.refs_2_ = bf16[512,3072]{1,0:T(8,128)(2,1)} fusion(bf16[512,3072]{1,0:T(8,128)(2,1)S(1)} %copy-done.116, bf16[512,768]{1,0:T(8,128)(2,1)S(1)} %get-tuple-element.1272.refs_1_, bf16[3072,768]{1,0:T(8,128)(2,1)} %bitcast.122), kind=kOutput, calls=%fused_computation | convolution fusion | flops 2420637696 | bytes 11796480 | tf_op jit(solution)/shard_map/dot_general | solution.py:48
  390.5 5.1 shard_map.296
  413.3 6.4 multiply_reduce_fusion
  424.3 7.3 %shard_map.299 = (bf16[4,96,3840]{2,1,0:T(8,128)(2,1)S(1)}, bf16[4,96,3840]{2,1,0:T(8,128)(2,1)}, f32[1,3840]{1,0:T(1,128)S(1)}) custom-call(s32[4]{0:T(128)S(1)} %pad_add_fusion.where_ref, bf16[512,768]{1,0:T(8,128)(2,1)S(1)} %copy-done.15, bf16[512,768]{1,0:T(8,128)(2,1)S(1)} %copy-done.41, bf16[512,3072]{1,0:T(8,128)(2,1)S(1)} %copy-done.28, ...), custom_call_target="tpu_custom_call" | custom-call | flops 1 | bytes 1 | tf_op jit(solution)/shard_map/pallas_call | solution.py:388
  438.0 9.0 %collective-permute-done.31.refs_14_ = bf16[48,1920]{1,0:T(8,128)(2,1)S(1)} collective-permute-done((bf16[48,1920]{1,0:T(8,128)(2,1)}, bf16[48,1920]{1,0:T(8,128)(2,1)S(1)}, u32[]{:S(2)}, u32[]{:S(2)}) %collective-permute-start.31) | collective-permute-done | bytes 184352 | tf_op jit(solution)/shard_map/ppermute | solution.py:177
  462.9 14.6 %shard_map.302 = (bf16[512,768]{1,0:T(8,128)(2,1)S(1)}, bf16[512,768]{1,0:T(8,128)(2,1)S(1)}, bf16[512,768]{1,0:T(8,128)(2,1)S(1)}) custom-call(s32[512,1]{1,0:T(8,128)S(1)} %copy-done.19, s32[1,512]{1,0:T(1,128)S(1)} %bitcast.118, bf16[512,2304]{1,0:T(8,128)(2,1)} %copy-done.2, bf16[512,2304]{1,0:T(8,128)(2,1)} %copy-done.2, bf16[512,2304]{1,0:T(8,128)(2,1)} %copy-done.2, ...), custom_call_target="tpu_custom_call" | custom-call | flops 1 | bytes 1 | tf_op jit(solution)/shard_map/pallas_call | solution.py:141
  494.9 5.1 collective-permute-done.42.refs_6_
  528.3 9.1 %collective-permute-done.49.refs_2_ = bf16[192,384]{1,0:T(8,128)(2,1)S(1)} collective-permute-done((bf16[192,384]{1,0:T(8,128)(2,1)S(1)}, bf16[192,384]{1,0:T(8,128)(2,1)S(1)}, u32[]{:S(2)}, u32[]{:S(2)}) %collective-permute-start.49) | collective-permute-done | bytes 147488 | tf_op jit(solution)/shard_map/ppermute | solution.py:177
  553.3 6.1 collective-permute-done.54.refs_9_
  559.4 9.0 %collective-permute-done.55.refs_10_ = bf16[48,1920]{1,0:T(8,128)(2,1)S(1)} collective-permute-done((bf16[48,1920]{1,0:T(8,128)(2,1)S(1)}, bf16[48,1920]{1,0:T(8,128)(2,1)S(1)}, u32[]{:S(2)}, u32[]{:S(2)}) %collective-permute-start.55) | collective-permute-done | bytes 184352 | tf_op jit(solution)/shard_map/ppermute | solution.py:177
  572.3 7.1 %collective-permute-done.62 = f32[2,12,768]{2,1,0:T(8,128)S(1)} collective-permute-done((f32[2,12,768]{2,1,0:T(8,128)S(1)}, f32[2,12,768]{2,1,0:T(8,128)S(1)}, u32[]{:S(2)}, u32[]{:S(2)}) %collective-permute-start.62) | collective-permute-done | bytes 73760 | tf_op jit(solution)/shard_map/ppermute | solution.py:172
  606.2 12.0 %collective-permute-done.72.refs_1_ = bf16[2,48,3072]{2,1,0:T(8,128)(2,1)S(1)} collective-permute-done((bf16[2,48,3072]{2,1,0:T(8,128)(2,1)S(1)}, bf16[2,48,3072]{2,1,0:T(8,128)(2,1)S(1)}, u32[]{:S(2)}, u32[]{:S(2)}) %collective-permute-start.72) | collective-permute-done | bytes 589856 | tf_op jit(solution)/shard_map/ppermute | solution.py:172
  622.7 5.6 collective-permute-start.70
  (714 shorter events, 306.4 us)
Async XLA Ops:
  7.2 37.9 %all-gather.9.cloned.1.call-start = ((), (), s32[]{:S(2)}) async-start(), calls=%async_computation | async-start | bytes 1536000 | tf_op jit(solution)/shard_map/all_gather | solution.py:452
  11.0 65.8 %all-gather.11.cloned.1.call-start = ((), (), s32[]{:S(2)}) async-start(), calls=%async_computation.1 | async-start | bytes 1474560 | tf_op jit(solution)/shard_map/all_gather | solution.py:452
  45.1 76.3 %all-gather.13.cloned.1.call-start = ((), (), s32[]{:S(2)}) async-start(), calls=%async_computation.2 | async-start | bytes 1474560 | tf_op jit(solution)/shard_map/all_gather | solution.py:452
  45.2 28.4 %collective-permute-start = (bf16[4,48,3200]{2,1,0:T(8,128)(2,1)}, bf16[4,48,3200]{2,1,0:T(8,128)(2,1)S(1)}, u32[]{:S(2)}, u32[]{:S(2)}) collective-permute-start(bf16[4,48,3200]{2,1,0:T(8,128)(2,1)} %bitcast.135), channel_id=1, source_target_pairs={{0,16},{16,0},{1,17},{17,1},{2,18},{18,2},{3,19},{19,3},{4,20},{20... | collective-permute-start | bytes 3686408 | tf_op jit(solution)/shard_map/ppermute | solution.py:172
  46.7 28.2 %collective-permute-start.1 = (bf16[4,48,3200]{2,1,0:T(8,128)(2,1)}, bf16[4,48,3200]{2,1,0:T(8,128)(2,1)}, u32[]{:S(2)}, u32[]{:S(2)}) collective-permute-start(bf16[4,48,3200]{2,1,0:T(8,128)(2,1)} %bitcast.136), channel_id=1, source_target_pairs={{0,2},{1,3},{2,0},{3,1},{4,6},{5,7},{6,4},{7,5},{8,10},{9,11},{10,... | collective-permute-start | bytes 3686408 | tf_op jit(solution)/shard_map/ppermute | solution.py:172
  79.6 554.2 %all-gather.15.cloned.1.call-start = ((), (), s32[]{:S(2)}) async-start(), calls=%async_computation.3 | async-start | bytes 2359296 | tf_op jit(solution)/shard_map/all_gather | solution.py:529
  79.7 41.8 %collective-permute-start.4 = (bf16[4,48,3072]{2,1,0:T(8,128)(2,1)}, bf16[4,48,3072]{2,1,0:T(8,128)(2,1)}, u32[]{:S(2)}, u32[]{:S(2)}) collective-permute-start(bf16[4,48,3072]{2,1,0:T(8,128)(2,1)} %bitcast.138), channel_id=1, source_target_pairs={{0,16},{16,0},{1,17},{17,1},{2,18},{18,2},{3,19},{19,3},{4,20},{20... | collective-permute-start | bytes 3538952 | tf_op jit(solution)/shard_map/ppermute | solution.py:172
  81.2 40.2 %collective-permute-start.5 = (bf16[4,48,3072]{2,1,0:T(8,128)(2,1)}, bf16[4,48,3072]{2,1,0:T(8,128)(2,1)}, u32[]{:S(2)}, u32[]{:S(2)}) collective-permute-start(bf16[4,48,3072]{2,1,0:T(8,128)(2,1)} %bitcast.139), channel_id=1, source_target_pairs={{0,2},{1,3},{2,0},{3,1},{4,6},{5,7},{6,4},{7,5},{8,10},{9,11},{10,... | collective-permute-start | bytes 3538952 | tf_op jit(solution)/shard_map/ppermute | solution.py:172
  82.7 38.8 %collective-permute-start.2 = (bf16[2,48,3200]{2,1,0:T(8,128)(2,1)}, bf16[2,48,3200]{2,1,0:T(8,128)(2,1)S(1)}, u32[]{:S(2)}, u32[]{:S(2)}) collective-permute-start(bf16[2,48,3200]{2,1,0:T(8,128)(2,1)} %slice.167), channel_id=1, source_target_pairs={{0,2},{1,3},{2,0},{3,1},{4,6},{5,7},{6,4},{7,5},{8,10},{9,11},{10,... | collective-permute-start | bytes 1843208 | tf_op jit(solution)/shard_map/ppermute | solution.py:172
  83.2 38.2 %collective-permute-start.3 = (bf16[2,48,3200]{2,1,0:T(8,128)(2,1)}, bf16[2,48,3200]{2,1,0:T(8,128)(2,1)}, u32[]{:S(2)}, u32[]{:S(2)}) collective-permute-start(bf16[2,48,3200]{2,1,0:T(8,128)(2,1)} %slice.168), channel_id=1, source_target_pairs={{0,16},{16,0},{1,17},{17,1},{2,18},{18,2},{3,19},{19,3},{4,20},{20... | collective-permute-start | bytes 1843208 | tf_op jit(solution)/shard_map/ppermute | solution.py:172
  133.7 42.5 %collective-permute-start.10 = (bf16[4,192,768]{2,1,0:T(8,128)(2,1)}, bf16[4,192,768]{2,1,0:T(8,128)(2,1)}, u32[]{:S(2)}, u32[]{:S(2)}) collective-permute-start(bf16[4,192,768]{2,1,0:T(8,128)(2,1)} %bitcast.10), channel_id=1, source_target_pairs={{0,2},{1,3},{2,0},{3,1},{4,6},{5,7},{6,4},{7,5},{8,10},{9,11},{10,... | collective-permute-start | bytes 3538952 | tf_op jit(solution)/shard_map/ppermute | solution.py:172
  135.2 41.1 %collective-permute-start.9 = (bf16[4,192,768]{2,1,0:T(8,128)(2,1)}, bf16[4,192,768]{2,1,0:T(8,128)(2,1)}, u32[]{:S(2)}, u32[]{:S(2)}) collective-permute-start(bf16[4,192,768]{2,1,0:T(8,128)(2,1)} %bitcast.10), channel_id=1, source_target_pairs={{0,16},{16,0},{1,17},{17,1},{2,18},{18,2},{3,19},{19,3},{4,20},{20... | collective-permute-start | bytes 3538952 | tf_op jit(solution)/shard_map/ppermute | solution.py:172
  135.7 39.2 %collective-permute-start.7 = (bf16[2,48,3072]{2,1,0:T(8,128)(2,1)}, bf16[2,48,3072]{2,1,0:T(8,128)(2,1)S(1)}, u32[]{:S(2)}, u32[]{:S(2)}) collective-permute-start(bf16[2,48,3072]{2,1,0:T(8,128)(2,1)} %slice.169), channel_id=1, source_target_pairs={{0,2},{1,3},{2,0},{3,1},{4,6},{5,7},{6,4},{7,5},{8,10},{9,11},{10,... | collective-permute-start | bytes 1769480 | tf_op jit(solution)/shard_map/ppermute | solution.py:172
  136.3 39.9 %collective-permute-start.8 = (bf16[2,48,3072]{2,1,0:T(8,128)(2,1)}, bf16[2,48,3072]{2,1,0:T(8,128)(2,1)}, u32[]{:S(2)}, u32[]{:S(2)}) collective-permute-start(bf16[2,48,3072]{2,1,0:T(8,128)(2,1)} %slice.170), channel_id=1, source_target_pairs={{0,16},{16,0},{1,17},{17,1},{2,18},{18,2},{3,19},{19,3},{4,20},{20... | collective-permute-start | bytes 1769480 | tf_op jit(solution)/shard_map/ppermute | solution.py:172
  189.0 25.5 %collective-permute-start.12 = (bf16[2,192,768]{2,1,0:T(8,128)(2,1)}, bf16[2,192,768]{2,1,0:T(8,128)(2,1)}, u32[]{:S(2)}, u32[]{:S(2)}) collective-permute-start(bf16[2,192,768]{2,1,0:T(8,128)(2,1)} %slice.192), channel_id=1, source_target_pairs={{0,2},{1,3},{2,0},{3,1},{4,6},{5,7},{6,4},{7,5},{8,10},{9,11},{10,... | collective-permute-start | bytes 1769480 | tf_op jit(solution)/shard_map/ppermute | solution.py:172
  189.8 24.7 %collective-permute-start.13 = (bf16[2,192,768]{2,1,0:T(8,128)(2,1)S(1)}, bf16[2,192,768]{2,1,0:T(8,128)(2,1)}, u32[]{:S(2)}, u32[]{:S(2)}) collective-permute-start(bf16[2,192,768]{2,1,0:T(8,128)(2,1)S(1)} %copy-done.159), channel_id=1, source_target_pairs={{0,16},{16,0},{1,17},{17,1},{2,18},{18,2},{3,19},{19,3},{4,20},{20... | collective-permute-start | bytes 1769480 | tf_op jit(solution)/shard_map/ppermute | solution.py:172
  287.2 22.8 %collective-permute-start.16 = (bf16[4,384,768]{2,1,0:T(8,128)(2,1)}, bf16[4,384,768]{2,1,0:T(8,128)(2,1)}, u32[]{:S(2)}, u32[]{:S(2)}) collective-permute-start(bf16[4,384,768]{2,1,0:T(8,128)(2,1)} %get-tuple-element.759), channel_id=1, source_target_pairs={{0,1},{1,0},{2,3},{3,2},{4,5},{5,4},{6,7},{7,6},{8,9},{9,8},{10,11... | collective-permute-start | bytes 7077896 | tf_op jit(solution)/shard_map/ppermute | solution.py:172
  347.4 25.7 %collective-permute-start.22 = (bf16[2,2,48,1920]{3,2,1,0:T(8,128)(2,1)S(1)}, bf16[2,2,48,1920]{3,2,1,0:T(8,128)(2,1)S(1)}, u32[]{:S(2)}, u32[]{:S(2)}) collective-permute-start(bf16[2,2,48,1920]{3,2,1,0:T(8,128)(2,1)S(1)} %copy-done.128), channel_id=1, source_target_pairs={{0,16},{16,0},{1,17},{17,1},{2,18},{18,2},{3,19},{19,3},{4,20},{20... | collective-permute-start | bytes 2211848 | tf_op jit(solution)/shard_map/ppermute | solution.py:172
  349.2 24.0 %collective-permute-start.23 = (bf16[2,48,3840]{2,1,0:T(8,128)(2,1)S(1)}, bf16[2,48,3840]{2,1,0:T(8,128)(2,1)S(1)}, u32[]{:S(2)}, u32[]{:S(2)}) collective-permute-start(bf16[2,48,3840]{2,1,0:T(8,128)(2,1)S(1)} %copy-done.126), channel_id=1, source_target_pairs={{0,2},{1,3},{2,0},{3,1},{4,6},{5,7},{6,4},{7,5},{8,10},{9,11},{10,... | collective-permute-start | bytes 2211848 | tf_op jit(solution)/shard_map/ppermute | solution.py:172
  350.6 22.5 %collective-permute-start.20 = (bf16[2,192,384]{2,1,0:T(8,128)(2,1)S(1)}, bf16[2,192,384]{2,1,0:T(8,128)(2,1)S(1)}, u32[]{:S(2)}, u32[]{:S(2)}) collective-permute-start(bf16[2,192,384]{2,1,0:T(8,128)(2,1)S(1)} %copy-done.136), channel_id=1, source_target_pairs={{0,2},{1,3},{2,0},{3,1},{4,6},{5,7},{6,4},{7,5},{8,10},{9,11},{10,... | collective-permute-start | bytes 884744 | tf_op jit(solution)/shard_map/ppermute | solution.py:172
  376.3 22.8 %collective-permute-start.29 = (bf16[4,96,2304]{2,1,0:T(8,128)(2,1)}, bf16[4,96,2304]{2,1,0:T(8,128)(2,1)S(1)}, u32[]{:S(2)}, u32[]{:S(2)}) collective-permute-start(bf16[4,96,2304]{2,1,0:T(8,128)(2,1)} %get-tuple-element.866), channel_id=1, source_target_pairs={{0,1},{1,0},{2,3},{3,2},{4,5},{5,4},{6,7},{7,6},{8,9},{9,8},{10,11... | collective-permute-start | bytes 5308424 | tf_op jit(solution)/shard_map/ppermute | solution.py:172
  408.3 39.4 %collective-permute-start.35 = (bf16[4,384,768]{2,1,0:T(8,128)(2,1)}, bf16[4,384,768]{2,1,0:T(8,128)(2,1)}, u32[]{:S(2)}, u32[]{:S(2)}) collective-permute-start(bf16[4,384,768]{2,1,0:T(8,128)(2,1)} %copy-done.120), channel_id=1, source_target_pairs={{0,1},{1,0},{2,3},{3,2},{4,5},{5,4},{6,7},{7,6},{8,9},{9,8},{10,11... | collective-permute-start | bytes 7077896 | tf_op jit(solution)/shard_map/ppermute | solution.py:172
  408.4 39.2 %collective-permute-start.33 = (bf16[2,2,48,1152]{3,2,1,0:T(8,128)(2,1)}, bf16[2,2,48,1152]{3,2,1,0:T(8,128)(2,1)}, u32[]{:S(2)}, u32[]{:S(2)}) collective-permute-start(bf16[2,2,48,1152]{3,2,1,0:T(8,128)(2,1)} %copy-done.132), channel_id=1, source_target_pairs={{0,16},{16,0},{1,17},{17,1},{2,18},{18,2},{3,19},{19,3},{4,20},{20... | collective-permute-start | bytes 1327112 | tf_op jit(solution)/shard_map/ppermute | solution.py:172
  410.1 37.6 %collective-permute-start.34 = (bf16[2,48,2304]{2,1,0:T(8,128)(2,1)}, bf16[2,48,2304]{2,1,0:T(8,128)(2,1)}, u32[]{:S(2)}, u32[]{:S(2)}) collective-permute-start(bf16[2,48,2304]{2,1,0:T(8,128)(2,1)} %copy-done.131), channel_id=1, source_target_pairs={{0,2},{1,3},{2,0},{3,1},{4,6},{5,7},{6,4},{7,5},{8,10},{9,11},{10,... | collective-permute-start | bytes 1327112 | tf_op jit(solution)/shard_map/ppermute | solution.py:172
  410.7 22.1 %collective-permute-start.30 = (bf16[48,1920]{1,0:T(8,128)(2,1)S(1)}, bf16[48,1920]{1,0:T(8,128)(2,1)S(1)}, u32[]{:S(2)}, u32[]{:S(2)}) collective-permute-start(bf16[48,1920]{1,0:T(8,128)(2,1)S(1)} %get-tuple-element.910), channel_id=1, source_target_pairs={{4,0},{8,4},{12,8},{0,12},{5,1},{9,5},{13,9},{1,13},{6,2},{10,6},{... | collective-permute-start | bytes 552968 | tf_op jit(solution)/shard_map/ppermute | solution.py:177
  456.2 23.0 %collective-permute-start.40 = (bf16[4,96,3840]{2,1,0:T(8,128)(2,1)}, bf16[4,96,3840]{2,1,0:T(8,128)(2,1)}, u32[]{:S(2)}, u32[]{:S(2)}) collective-permute-start(bf16[4,96,3840]{2,1,0:T(8,128)(2,1)} %get-tuple-element.954), channel_id=1, source_target_pairs={{0,1},{1,0},{2,3},{3,2},{4,5},{5,4},{6,7},{7,6},{8,9},{9,8},{10,11... | collective-permute-start | bytes 8847368 | tf_op jit(solution)/shard_map/ppermute | solution.py:172
  456.2 22.9 %collective-permute-start.38 = (bf16[2,2,192,384]{3,2,1,0:T(8,128)(2,1)}, bf16[2,2,192,384]{3,2,1,0:T(8,128)(2,1)S(1)}, u32[]{:S(2)}, u32[]{:S(2)}) collective-permute-start(bf16[2,2,192,384]{3,2,1,0:T(8,128)(2,1)} %copy-done.130), channel_id=1, source_target_pairs={{0,16},{16,0},{1,17},{17,1},{2,18},{18,2},{3,19},{19,3},{4,20},{20... | collective-permute-start | bytes 1769480 | tf_op jit(solution)/shard_map/ppermute | solution.py:172
  486.7 25.8 %collective-permute-start.46 = (bf16[2,2,48,1920]{3,2,1,0:T(8,128)(2,1)}, bf16[2,2,48,1920]{3,2,1,0:T(8,128)(2,1)}, u32[]{:S(2)}, u32[]{:S(2)}) collective-permute-start(bf16[2,2,48,1920]{3,2,1,0:T(8,128)(2,1)} %get-tuple-element.1005), channel_id=1, source_target_pairs={{0,16},{16,0},{1,17},{17,1},{2,18},{18,2},{3,19},{19,3},{4,20},{20... | collective-permute-start | bytes 2211848 | tf_op jit(solution)/shard_map/ppermute | solution.py:172
  488.4 24.1 %collective-permute-start.47 = (bf16[2,48,3840]{2,1,0:T(8,128)(2,1)}, bf16[2,48,3840]{2,1,0:T(8,128)(2,1)}, u32[]{:S(2)}, u32[]{:S(2)}) collective-permute-start(bf16[2,48,3840]{2,1,0:T(8,128)(2,1)} %get-tuple-element.1006), channel_id=1, source_target_pairs={{0,2},{1,3},{2,0},{3,1},{4,6},{5,7},{6,4},{7,5},{8,10},{9,11},{10,... | collective-permute-start | bytes 2211848 | tf_op jit(solution)/shard_map/ppermute | solution.py:172
  488.8 23.7 %collective-permute-start.44 = (bf16[2,192,384]{2,1,0:T(8,128)(2,1)}, bf16[2,192,384]{2,1,0:T(8,128)(2,1)}, u32[]{:S(2)}, u32[]{:S(2)}) collective-permute-start(bf16[2,192,384]{2,1,0:T(8,128)(2,1)} %get-tuple-element.1003), channel_id=1, source_target_pairs={{0,2},{1,3},{2,0},{3,1},{4,6},{5,7},{6,4},{7,5},{8,10},{9,11},{10,... | collective-permute-start | bytes 884744 | tf_op jit(solution)/shard_map/ppermute | solution.py:172
  490.6 21.9 %collective-permute-start.45 = (bf16[2,192,384]{2,1,0:T(8,128)(2,1)}, bf16[2,192,384]{2,1,0:T(8,128)(2,1)}, u32[]{:S(2)}, u32[]{:S(2)}) collective-permute-start(bf16[2,192,384]{2,1,0:T(8,128)(2,1)} %get-tuple-element.1004), channel_id=1, source_target_pairs={{0,16},{16,0},{1,17},{17,1},{2,18},{18,2},{3,19},{19,3},{4,20},{20... | collective-permute-start | bytes 884744 | tf_op jit(solution)/shard_map/ppermute | solution.py:172
  606.2 27.6 %collective-permute-start.71 = (bf16[2,48,3072]{2,1,0:T(8,128)(2,1)S(1)}, bf16[2,48,3072]{2,1,0:T(8,128)(2,1)S(1)}, u32[]{:S(2)}, u32[]{:S(2)}) collective-permute-start(bf16[2,48,3072]{2,1,0:T(8,128)(2,1)S(1)} %pad_maximum_fusion.2.refs_0_), channel_id=1, source_target_pairs={{0,1},{1,0},{2,3},{3,2},{4,5},{5,4},{6,7},{7,6},{8,9},{9,8},{10,11... | collective-permute-start | bytes 1769480 | tf_op jit(solution)/shard_map/ppermute | solution.py:172
  (238 other events, 2549.9 us)
Sparse Core Ops, SparseCore 0:
  11.1 33.9 all-gather.8
  47.2 29.5 all-gather.10
  79.7 29.5 all-gather.12
  597.6 25.6 all-gather.14

commit v4 on v3

--- a/solution.py
+++ b/solution.py
@@ -19,9 +19,21 @@
 
 
 def layer_norm(hidden, norm_gain, norm_shift):
-    center = hidden - jnp.mean(hidden, axis=-1, keepdims=True)
+    mean = jnp.mean(hidden, axis=-1, keepdims=True)
+    center = hidden - mean
     spread = jnp.mean(center * center, axis=-1, keepdims=True)
-    return center * lax.rsqrt(spread + EPSILON) * norm_gain + norm_shift
+    scale = lax.rsqrt(spread + EPSILON)
+    return (center * scale * norm_gain + norm_shift, (mean, scale))
+
+
+def layer_norm_back(hidden, stats, norm_gain, grad):
+    mean, scale = stats
+    hat = (hidden - mean) * scale
+    scaled = grad * norm_gain
+    first = jnp.mean(scaled, axis=-1, keepdims=True)
+    second = jnp.mean(scaled * hat, axis=-1, keepdims=True)
+    hidden_grad = scale * (scaled - first - hat * second)
+    return (hidden_grad, jnp.sum(grad * hat, axis=0), jnp.sum(grad, axis=0))
 
 
 def slot_layout(counts, row_count):
@@ -149,7 +161,7 @@
         + [spec(first) for _, first in blocks],
         out_specs=[spec(0) for _ in outs],
         scratch_shapes=[pltpu.VMEM((row_count, row_count), jnp.float32)],
-        compiler_params=pltpu.CompilerParams(vmem_limit_bytes=48 * 1024 * 1024),
+        compiler_params=pltpu.CompilerParams(vmem_limit_bytes=20 * 1024 * 1024),
         cost_estimate=SHORT,
     )(segment[:, None], segment[None, :], *(array for array, _ in blocks))
 
@@ -181,18 +193,20 @@
     return lax.ppermute(block, axis, [(source, target)])
 
 
-def place_kernel(widths, where_ref, mine, theirs, *refs):
-    outs, held, in_sems, out_sems = refs[:-3], refs[-3], refs[-2], refs[-1]
+def place_kernel(widths, where_ref, *refs):
+    mine, theirs, outs = refs[:5], refs[5:10], refs[10:-3]
+    held, in_sems, out_sems = refs[-3:]
     section, core, side = (where_ref[i] for i in range(3))
 
     def run(same, other):
         steps = []
         for rank_core, pieces in ((core, mine), (1 - core, theirs)):
-            for i in range(16):
+            entries = [(piece, i) for piece in pieces for i in range(piece.shape[0])]
+            for i, (piece, entry) in enumerate(entries):
                 block = (same, other, same, other)[i // 4]
                 to_side = (side, side, 1 - side, 1 - side)[i // 4]
                 slot = held.at[len(steps)]
-                load = pltpu.make_async_copy(pieces.at[i], slot, in_sems.at[len(steps)])
+                load = pltpu.make_async_copy(piece.at[entry], slot, in_sems.at[len(steps)])
                 load.start()
                 stores, start = [], 0
                 for index, width in enumerate(widths):
@@ -235,7 +249,7 @@
             pltpu.SemaphoreType.DMA((32,)),
             pltpu.SemaphoreType.DMA((32 * len(widths),)),
         ],
-        compiler_params=pltpu.CompilerParams(vmem_limit_bytes=32 * 1024 * 1024),
+        compiler_params=pltpu.CompilerParams(vmem_limit_bytes=14 * 1024 * 1024),
         cost_estimate=SHORT,
     )(where, *pieces)
 
@@ -248,7 +262,7 @@
     return lax.dynamic_index_in_dim(array, index, axis, keepdims=False)
 
 
-def local_call(kernel, where, arrays, outs, scratch=(), steps=1, kind=jnp.bfloat16):
+def local_call(kernel, where, arrays, outs, scratch=(), steps=1, kind=jnp.bfloat16, limit=16):
     def spec(shape, first):
         if first is None:
             return pl.BlockSpec(shape, lambda i: (0,) * len(shape))
@@ -264,7 +278,7 @@
         + [spec(array.shape, first) for array, first in pairs],
         out_specs=[spec(shape, None if steps == 1 else 0) for shape in outs],
         scratch_shapes=list(scratch),
-        compiler_params=pltpu.CompilerParams(vmem_limit_bytes=48 * 1024 * 1024),
+        compiler_params=pltpu.CompilerParams(vmem_limit_bytes=limit * 1024 * 1024),
         cost_estimate=SHORT,
     )(where, *(array for array, _ in pairs))
 
@@ -312,17 +326,38 @@
         target[...] = both[lax.rem(here + 3 - i, 4)]
 
 
-def back_kernel(where_ref, *refs):
+def pairs_kernel(where_ref, low, high, low_got, high_got, keep, send):
+    def put(own, other):
+        own[...] = add_low(low[...], low_got[...])
+        other[...] = add_low(high[...], high_got[...])
+
+    @pl.when(where_ref[3] < 2)
+    def _():
+        put(keep, send)
+
+    @pl.when(where_ref[3] >= 2)
+    def _():
+        put(send, keep)
+
+
+def single_kernel(where_ref, own, got, keep, send):
+    here = lax.rem(where_ref[3], 2)
+    keep[...] = add_low(own[here], got[here])
+    send[...] = add_low(own[1 - here], got[1 - here])
+
+
+def back_kernel(counts, where_ref, *refs):
     keep, give = refs[-2:]
 
     def put(first, second):
-        start = 0
-        for member in range(len(refs) // 8):
-            width = refs[member * 8].shape[1]
-            for block, target in enumerate((first, second)):
-                terms = refs[member * 8 + block * 4 : member * 8 + block * 4 + 4]
+        start = position = 0
+        for pair in counts:
+            width = refs[position].shape[1]
+            for count, target in zip(pair, (first, second)):
+                terms = refs[position : position + count]
                 total = sum(term[...].astype(jnp.float32) for term in terms)
                 target[:, start : start + width] = total.astype(jnp.bfloat16)
+                position += count
             start += width
 
     @pl.when(where_ref[0] == 0)
@@ -393,7 +428,7 @@
         in_specs=in_specs,
         out_specs=[out_spec, out_spec, sums_spec],
         scratch_shapes=[pltpu.VMEM((width, width), jnp.float32)],
-        compiler_params=pltpu.CompilerParams(vmem_limit_bytes=40 * 1024 * 1024),
+        compiler_params=pltpu.CompilerParams(vmem_limit_bytes=16 * 1024 * 1024),
         cost_estimate=SHORT,
     )(where, *lefts, *rights)
 
@@ -428,7 +463,7 @@
             pl.BlockSpec((1, width), lambda j: (0, j)),
         ],
         out_specs=[out_spec, out_spec],
-        compiler_params=pltpu.CompilerParams(vmem_limit_bytes=40 * 1024 * 1024),
+        compiler_params=pltpu.CompilerParams(vmem_limit_bytes=24 * 1024 * 1024),
         cost_estimate=SHORT,
     )(normed, weight, bias[None])
 
@@ -463,10 +498,10 @@
         return [along, across, beyond]
 
     def laid(self, state, widths=None):
-        mine = jnp.concatenate(state, axis=0)
-        return place((mine, self.to_mate(mine)), self.where, widths)
-
-    def reduce(self):
+        theirs = tuple(self.to_mate(piece) for piece in state)
+        return place((*state, *theirs), self.where, widths)
+
+    def reduce(self, direct):
         def mates(own, send):
             return ((own,), [(send, self.to_mate)])
 
@@ -499,14 +534,26 @@
             turns = [functools.partial(turn, axis="shard", step=i) for i in (1, 2, 3)]
             return ((result[0],), list(zip(result[1:], turns)))
 
-        return [mates, across, along, shards]
+        def pairs(*state):
+            shape = state[0].shape
+            keep, send = local_call(pairs_kernel, self.where, state, (shape, shape))
+            return ((keep,), [(send, lambda array: swap(array, "shard", 2))])
+
+        def single(own, got):
+            shape = own.shape[1:]
+            keep, send = local_call(single_kernel, self.where, (own, got), (shape, shape))
+            return ((keep,), [(send, lambda array: swap(array, "shard", 1))])
+
+        return [mates, across, along] + ([shards] if direct else [pairs, single])
 
     def spread(self):
         def back(*pairs):
             terms = [term for pair in pairs for state in pair for term in state]
             rows = terms[0].shape[0]
             shape = (rows, sum(pair[0][0].shape[1] for pair in pairs))
-            keep, give = local_call(back_kernel, self.where, terms, (shape, shape))
+            counts = [tuple(len(state) for state in pair) for pair in pairs]
+            kernel = functools.partial(back_kernel, counts)
+            keep, give = local_call(kernel, self.where, terms, (shape, shape))
             return ((keep,), [(give, self.over_x)])
 
         def around(keep, got):
@@ -531,17 +578,19 @@
         step.late = late
         return [step]
 
-    @staticmethod
-    def total():
-        def step_of(axis, bit):
-            def step(*terms):
-                array = sum(terms[1:], terms[0])
-                return ((array,), [(array, lambda array: swap(array, axis, bit))])
+    def total(self):
+        def chip(array):
+            return ((array,), [(array, self.to_mate)])
+
+        def step_of(move):
+            def step(own, got):
+                array = own + got
+                return ((array,), [(array, move)])
 
             return step
 
-        pairs = (("replica", 1), ("section", 1), ("replica", 2), ("shard", 1), ("shard", 2))
-        return [step_of(*pair) for pair in pairs]
+        moves = (self.over_x, self.over_y, lambda a: swap(a, "shard", 2), lambda a: swap(a, "shard", 1))
+        return [chip] + [step_of(move) for move in moves]
 
 
 class Flows:
@@ -559,7 +608,9 @@
 
     def stage(self, compute=lambda: (), *inputs):
         names = [name for name in self.left if self.left[name]]
-        steps = [self.left[name].pop(0) for name in names]
+        steps = {name: self.left[name].pop(0) for name in names}
+        names = [name for name in names if steps[name] is not None]
+        steps = [steps[name] for name in names]
         states = [self.states[name] for name in names]
         inputs, states = lax.optimization_barrier((inputs, states))
         ready = [step(*state) for step, state in zip(steps, states)]
@@ -629,14 +680,15 @@
         return (own, over_y, mate, mate_y)
 
     arrays = (*pieces(wide), *pieces(contract))
-    return local_call(close_kernel, where, arrays, shapes, kind=jnp.float32)
+    return local_call(close_kernel, where, arrays, shapes, kind=jnp.float32, limit=32)
 
 VECTORS = ("gain_a", "shift_a", "bias_q", "bias_v", "bias_o", "gain_f", "shift_f", "bias_c")
 
 
 def forward_attention(params, hidden_low, segment):
     hidden = hidden_low.astype(jnp.float32)
-    normed = layer_norm(hidden, params["gain_a"], params["shift_a"]).astype(jnp.bfloat16)
+    normed, stats_a = layer_norm(hidden, params["gain_a"], params["shift_a"])
+    normed = normed.astype(jnp.bfloat16)
     zeros = jnp.zeros_like(params["bias_q"])
     joint_bias = jnp.concatenate([params["bias_q"], zeros, params["bias_v"]])
     joint_low = (
@@ -651,6 +703,7 @@
     return dict(
         hidden_low=hidden_low,
         normed=normed,
+        stats_a=stats_a,
         joint_low=joint_low,
         log_sums=log_sums,
         mixed_low=mixed_low,
@@ -659,9 +712,10 @@
 
 
 def forward_expand(params, middle):
-    normed_two = layer_norm(middle, params["gain_f"], params["shift_f"]).astype(jnp.bfloat16)
+    normed_two, stats_f = layer_norm(middle, params["gain_f"], params["shift_f"])
+    normed_two = normed_two.astype(jnp.bfloat16)
     activated, slope = expand_call(normed_two, params["expand"], params["bias_e"])
-    return dict(normed_two=normed_two, slope=slope, activated=activated)
+    return dict(normed_two=normed_two, stats_f=stats_f, slope=slope, activated=activated)
 
 
 def forward_contract(params, middle, activated, living):
@@ -683,12 +737,15 @@
             "expand": (self.expand, ("upstream", "activated", "slope")),
             "norm": (
                 self.norm,
-                ("expand_low", "normed_two", "out_grad", "middle", "mixed_low"),
+                ("expand_low", "normed_two", "out_grad", "middle", "stats_f", "mixed_low"),
             ),
             "attention": (self.attention, ("joint_low", "log_sums", "mixed_grad")),
             "input": (self.input, ("normed", "joint_grad")),
-            "last": (self.last, ("joint_grad", "middle_grad", "hidden_low")),
-            "both": (self.both, ("normed", "joint_grad", "middle_grad", "hidden_low")),
+            "last": (self.last, ("joint_grad", "middle_grad", "hidden_low", "stats_a")),
+            "both": (
+                self.both,
+                ("normed", "joint_grad", "middle_grad", "hidden_low", "stats_a"),
+            ),
         }[part]
         self.held.update(flow.stage(function, *(self.held[name] for name in names)))
 
@@ -708,10 +765,11 @@
         expand_low = (activated_grad * slope.astype(jnp.float32)).astype(jnp.bfloat16)
         return dict(found, out_grad=out_grad, expand_low=expand_low)
 
-    def norm(self, expand_low, normed_two, out_grad, middle, mixed_low):
+    def norm(self, expand_low, normed_two, out_grad, middle, stats_f, mixed_low):
         normed_grad = times_transpose(expand_low, self.params["expand"])
-        _, pull = jax.vjp(layer_norm, middle, self.params["gain_f"], self.params["shift_f"])
-        norm_grad, gain_grad, shift_grad = pull(normed_grad)
+        norm_grad, gain_grad, shift_grad = layer_norm_back(
+            middle, stats_f, self.params["gain_f"], normed_grad
+        )
         middle_grad = out_grad + norm_grad
         branch_low = middle_grad.astype(jnp.bfloat16)
         mixed_grad = times_transpose(branch_low, self.params["output"]).astype(jnp.bfloat16)
@@ -726,21 +784,17 @@
     def input(self, normed, joint_grad):
         return self.grads("input", (normed, joint_grad))
 
-    def last(self, joint_grad, middle_grad, hidden_low):
+    def last(self, joint_grad, middle_grad, hidden_low, stats_a):
         normed_grad = times_transpose(joint_grad, self.params["input"])
-        _, pull = jax.vjp(
-            layer_norm,
-            hidden_low.astype(jnp.float32),
-            self.params["gain_a"],
-            self.params["shift_a"],
+        norm_grad, gain_grad, shift_grad = layer_norm_back(
+            hidden_low.astype(jnp.float32), stats_a, self.params["gain_a"], normed_grad
         )
-        norm_grad, gain_grad, shift_grad = pull(normed_grad)
         grad = middle_grad + norm_grad
         return dict(grad_low=grad.astype(jnp.bfloat16), gain_a=gain_grad, shift_a=shift_grad)
 
-    def both(self, normed, joint_grad, middle_grad, hidden_low):
+    def both(self, normed, joint_grad, middle_grad, hidden_low, stats_a):
         found = self.input(normed, joint_grad)
-        return dict(found, **self.last(joint_grad, middle_grad, hidden_low))
+        return dict(found, **self.last(joint_grad, middle_grad, hidden_low, stats_a))
 
     def small(self):
         held = self.held
@@ -891,15 +945,17 @@
 
     kept_second, last_out = second_forward(middle_out)
 
-    def begin(block, name):
+    def begin(block, name, direct=False):
         tag = ("first_" if block is first else "second_") + name
         if cube:
-            flow.start(tag, moves.reduce(), block.held[name + "_own"], block.held[name + "_send"])
+            flow.start(tag, moves.reduce(direct), block.held[name + "_own"], block.held[name + "_send"])
 
     def spread(name, *members):
         if cube:
             pairs = [(flow.states["first_" + m], flow.states["second_" + m]) for m in members]
-            flow.start(name, moves.spread(), *pairs)
+            back, around = moves.spread()
+            steps = [back, around] if name == "wide" else [back, None, around]
+            flow.start(name, steps, *pairs)
 
     first = None
     second = Backward(params[1], kept_second, segment, living, where if cube else None, seed)
@@ -919,16 +975,16 @@
     begin(first, "expand")
     first.run(flow, "attention")
     first.run(flow, "input")
-    begin(first, "input")
+    begin(first, "input", direct=True)
     first.run(flow, "last")
     small_both = jnp.stack([first.small(), second.small()])
     flow.start("small", moves.total() if cube else [], small_both)
     flow.start("grad", moves.exchange(4), section, first.held["grad_low"], second.held["grad_low"])
     flow.stage()
+    spread("contract", "contract")
     flow.stage()
     flow.stage()
     spread("wide", "input", "expand")
-    spread("contract", "contract")
     flow.stage()
     flow.stage()
 

time: 660 us -> 639 us (0.968)
  local copies, waits for them, and re-layouts: 98.7 us -> 85.5 us
  other arithmetic: 41.8 us -> 33.8 us
    ppermute x18 -> x3, waiting for transfers between devices: 45 us -> 3.79 us  [turn(): lax.ppermute(block, axis, [((i + step) % size, i) for i in range(size)])]
    ppermute x59 -> x81, waiting for transfers between devices: 137 us -> 175 us  [swap(): lax.ppermute(block, axis, [(i, i ^ bit) for i in range(lax.axis_size(axis...]
    ppermute x18 -> x3, starting transfers between devices: 19 us -> 2.31 us  [turn(): lax.ppermute(block, axis, [((i + step) % size, i) for i in range(size)])]
    ppermute x59 -> x81, starting transfers between devices: 48.3 us -> 64.1 us  [swap(): lax.ppermute(block, axis, [(i, i ^ bit) for i in range(lax.axis_size(axis...]
    unnamed x406 -> x386, local copies, waits for them, and re-layouts: 72.6 us -> 61.7 us
    pallas_call x21 -> x26, Pallas kernels: 36.7 us -> 38.7 us  [local_call(): pl.pallas_call(kernel, grid=(steps,), out_shape=[jax.ShapeDtypeStruct(sha...]
  transfers between devices with their start and end apart: 81 -> 88, of which waited for: 29 -> 28; matrix products, arithmetic and copies ran while one was open for 12% -> 14% of each run, Pallas kernels for 13% -> 14%
where the time goes in v4:
time: 639 us; the launch traced here: 629 us
  waiting for transfers between devices  213 us (33%)
  Pallas kernels  154 us (24%)
  local copies, waits for them, and re-layouts  85.5 us (13%)
  starting transfers between devices  66.6 us (10%)
  matrix products  58.6 us (9%)
  other arithmetic  33.8 us (5%)
  between operations  16.5 us (3%)
    ppermute x81, waiting for transfers between devices, swap(): lax.ppermute(block, axis, [(i, i ^ bit) for i in range(lax.axis_size(axis...  175 us
    ppermute x81, starting transfers between devices, swap(): lax.ppermute(block, axis, [(i, i ^ bit) for i in range(lax.axis_size(axis...  64.1 us
    unnamed x386, local copies, waits for them, and re-layouts  61.7 us
    pallas_call x4, Pallas kernels, attention_call(): pl.pallas_call(kernel, grid=(pairs,), out_shape=[jax.ShapeDtypeStruct((ro...  51.8 us
    dot_general x8, matrix products, times_transpose(): lax.dot_general(left_side, right_side, (((1,), (1,)), ((), ())), preferre...  40.9 us
    pallas_call x26, Pallas kernels, local_call(): pl.pallas_call(kernel, grid=(steps,), out_shape=[jax.ShapeDtypeStruct(sha...  38.7 us
    pallas_call x6, Pallas kernels, grad_call(): pl.pallas_call(functools.partial(grad_kernel, kinds), grid=(steps,), out_...  35.6 us
    all_gather x3, waiting for transfers between devices, along(): return ((), [(own, lambda array: lax.all_gather(array, 'shard', axis=0))])  34.3 us
  transfers between devices with their start and end apart: 88, of which 28 were waited for; matrix products, arithmetic and copies ran while one was open for 14% of the time, Pallas kernels for 14%

profile of v4, /device:TPU:0, one launch (start us, length us, event | category | flops | bytes accessed | tf_op | source)
XLA Modules:
  0.0 628.7 jit_solution(1522663187568553644)
XLA Ops:
  12.7 32.4 %all-gather.9.cloned.1.call-done = bf16[192,3200]{1,0:T(8,128)(2,1)} async-done(((bf16[48,3200]{1,0:T(8,128)(2,1)}), bf16[192,3200]{1,0:T(8,128)(2,1)}) %all-gather.9.cloned.1.call-update) | async-done | bytes 1228816 | tf_op jit(solution)/shard_map/all_gather | solution.py:487
  49.9 23.7 %collective-permute-done.refs_1_ = bf16[4,48,3200]{2,1,0:T(8,128)(2,1)S(1)} collective-permute-done((bf16[4,48,3200]{2,1,0:T(8,128)(2,1)}, bf16[4,48,3200]{2,1,0:T(8,128)(2,1)S(1)}, u32[]{:S(2)}, u32[]{:S(2)}) %collective-permute-start) | collective-permute-done | bytes 1228832 | tf_op jit(solution)/shard_map/ppermute | solution.py:184
  84.7 36.7 %collective-permute-done.2.refs_3_ = bf16[2,48,3200]{2,1,0:T(8,128)(2,1)S(1)} collective-permute-done((bf16[2,48,3200]{2,1,0:T(8,128)(2,1)}, bf16[2,48,3200]{2,1,0:T(8,128)(2,1)S(1)}, u32[]{:S(2)}, u32[]{:S(2)}) %collective-permute-start.2) | collective-permute-done | bytes 614432 | tf_op jit(solution)/shard_map/ppermute | solution.py:184
  136.5 5.3 shard_map.280
  153.3 11.7 %shard_map.281 = (bf16[512,768]{1,0:T(8,128)(2,1)S(1)}, f32[512,768]{1,0:T(8,128)S(1)}) custom-call(s32[512,1]{1,0:T(8,128)S(1)} %copy.38.column_ref, s32[1,512]{1,0:T(1,128)S(1)} %bitcast.133, bf16[512,2304]{1,0:T(8,128)(2,1)S(1)} %fusion.q_ref.k_ref.v_ref, bf16[512,2304]{1,0:T(8,128)(2,1)S(1)} %fusion.q_ref.k_ref.v_ref, ...), custom_call_target="tpu_custom_call" | custom-call | flops 1 | bytes 1 | tf_op jit(solution)/shard_map/pallas_call | solution.py:153
  169.9 5.0 collective-permute-done.11.refs_3_
  190.9 5.0 shard_map.282
  195.9 6.8 %shard_map.283 = (bf16[512,3072]{1,0:T(8,128)(2,1)S(1)}, bf16[512,3072]{1,0:T(8,128)(2,1)S(1)}) custom-call(bf16[512,768]{1,0:T(8,128)(2,1)S(1)} %add_convert_fusion.3.normed_ref.refs_0_, bf16[768,3072]{1,0:T(8,128)(2,1)S(1)} %bitcast.120, f32[1,3072]{1,0:T(1,128)S(1)} %bitcast.138), custom_call_target="tpu_custom_call" | custom-call | flops 1 | bytes 1 | tf_op jit(solution)/shard_map/pallas_call | solution.py:456
  220.7 11.9 %shard_map.285 = (bf16[512,768]{1,0:T(8,128)(2,1)S(1)}, f32[512,768]{1,0:T(8,128)S(1)}) custom-call(s32[512,1]{1,0:T(8,128)S(1)} %copy.38.column_ref, s32[1,512]{1,0:T(1,128)S(1)} %bitcast.134, bf16[512,2304]{1,0:T(8,128)(2,1)S(1)} %fusion.1.q_ref.k_ref.v_ref, bf16[512,2304]{1,0:T(8,128)(2,1)S(1)} %fusion.1.q_ref.k_ref.v_ref, ...), custom_call_target="tpu_custom_call" | custom-call | flops 1 | bytes 1 | tf_op jit(solution)/shard_map/pallas_call | solution.py:153
  234.6 6.8 %shard_map.286 = (bf16[512,3072]{1,0:T(8,128)(2,1)S(1)}, bf16[512,3072]{1,0:T(8,128)(2,1)S(1)}) custom-call(bf16[512,768]{1,0:T(8,128)(2,1)S(1)} %add_convert_fusion.2.normed_ref.refs_0_, bf16[768,3072]{1,0:T(8,128)(2,1)S(1)} %bitcast.122, f32[1,3072]{1,0:T(1,128)S(1)} %bitcast.137), custom_call_target="tpu_custom_call" | custom-call | flops 1 | bytes 1 | tf_op jit(solution)/shard_map/pallas_call | solution.py:456
  250.7 6.3 shard_map.287
  259.0 6.3 %multiply_convert_fusion.1.refs_2_ = bf16[512,3072]{1,0:T(8,128)(2,1)S(1)} fusion(bf16[512,3072]{1,0:T(8,128)(2,1)} %copy-done.118, bf16[512,768]{1,0:T(8,128)(2,1)} %copy-done.26, bf16[3072,768]{1,0:T(8,128)(2,1)} %bitcast.141), kind=kOutput, calls=%fused_computation.1 | convolution fusion | flops 2420637696 | bytes 11796480 | tf_op jit(solution)/shard_map/dot_general | solution.py:60
  267.9 6.1 multiply_reduce_fusion.6
  275.8 6.5 %shard_map.288 = (bf16[4,96,3840]{2,1,0:T(8,128)(2,1)S(1)}, bf16[4,96,3840]{2,1,0:T(8,128)(2,1)S(1)}, f32[1,3840]{1,0:T(1,128)S(1)}) custom-call(s32[4]{0:T(128)S(1)} %pad_add_fusion.where_ref, bf16[512,768]{1,0:T(8,128)(2,1)S(1)} %copy-done.18, bf16[512,768]{1,0:T(8,128)(2,1)S(1)} %copy-done.41, bf16[512,3072]{1,0:T(8,128)(2,1)S(1)} %multiply_convert_fusion.1.refs_2_, ...), custom_call_target="tpu_custom_call" | custom-call | flops 1 | bytes 1 | tf_op jit(solution)/shard_map/pallas_call | solution.py:423
  294.0 14.1 %shard_map.290 = (bf16[512,768]{1,0:T(8,128)(2,1)S(1)}, bf16[512,768]{1,0:T(8,128)(2,1)S(1)}, bf16[512,768]{1,0:T(8,128)(2,1)S(1)}) custom-call(s32[512,1]{1,0:T(8,128)S(1)} %copy.38.column_ref, s32[1,512]{1,0:T(1,128)S(1)} %bitcast.135, bf16[512,2304]{1,0:T(8,128)(2,1)S(1)} %copy-done.3, bf16[512,2304]{1,0:T(8,128)(2,1)S(1)} %copy-done.3, ...), custom_call_target="tpu_custom_call" | custom-call | flops 1 | bytes 1 | tf_op jit(solution)/shard_map/pallas_call | solution.py:153
  325.1 5.4 multiply_reduce_fusion.4
  331.1 14.5 %collective-permute-done.32.low_got = bf16[2,192,384]{2,1,0:T(8,128)(2,1)S(1)} collective-permute-done((bf16[2,192,384]{2,1,0:T(8,128)(2,1)}, bf16[2,192,384]{2,1,0:T(8,128)(2,1)S(1)}, u32[]{:S(2)}, u32[]{:S(2)}) %collective-permute-start.32) | collective-permute-done | bytes 294944 | tf_op jit(solution)/shard_map/ppermute | solution.py:184
  354.3 6.6 %multiply_convert_fusion.refs_2_ = bf16[512,3072]{1,0:T(8,128)(2,1)} fusion(bf16[512,3072]{1,0:T(8,128)(2,1)S(1)} %copy-done.117, bf16[512,768]{1,0:T(8,128)(2,1)S(1)} %get-tuple-element.1294.refs_1_, bf16[3072,768]{1,0:T(8,128)(2,1)} %bitcast.140), kind=kOutput, calls=%fused_computation | convolution fusion | flops 2420637696 | bytes 11796480 | tf_op jit(solution)/shard_map/dot_general | solution.py:60
  360.9 5.9 shard_map.296
  381.4 6.1 multiply_reduce_fusion.2
  389.2 7.3 %shard_map.300 = (bf16[4,96,3840]{2,1,0:T(8,128)(2,1)S(1)}, bf16[4,96,3840]{2,1,0:T(8,128)(2,1)}, f32[1,3840]{1,0:T(1,128)S(1)}) custom-call(s32[4]{0:T(128)S(1)} %pad_add_fusion.where_ref, bf16[512,768]{1,0:T(8,128)(2,1)S(1)} %add_convert_fusion.3.normed_ref.refs_0_, bf16[512,768]{1,0:T(8,128)(2,1)S(1)} %copy-done.39, bf16[512,3072]{1,0:T(8,128)(2,1)S(1)} %copy-done.25, ...), custom_call_target="tpu_custom_call" | custom-call | flops 1 | bytes 1 | tf_op jit(solution)/shard_map/pallas_call | solution.py:423
  425.9 14.1 %shard_map.304 = (bf16[512,768]{1,0:T(8,128)(2,1)S(1)}, bf16[512,768]{1,0:T(8,128)(2,1)S(1)}, bf16[512,768]{1,0:T(8,128)(2,1)S(1)}) custom-call(s32[512,1]{1,0:T(8,128)S(1)} %copy.38.column_ref, s32[1,512]{1,0:T(1,128)S(1)} %bitcast.136, bf16[512,2304]{1,0:T(8,128)(2,1)S(1)} %fusion.q_ref.k_ref.v_ref, bf16[512,2304]{1,0:T(8,128)(2,1)S(1)} %fusion.q_ref.k_ref.v_ref, ...), custom_call_target="tpu_custom_call" | custom-call | flops 1 | bytes 1 | tf_op jit(solution)/shard_map/pallas_call | solution.py:153
  441.5 6.0 collective-permute-done.47.high_got
  470.7 6.4 %collective-permute-done.52.low_got = bf16[2,192,384]{2,1,0:T(8,128)(2,1)} collective-permute-done((bf16[2,192,384]{2,1,0:T(8,128)(2,1)}, bf16[2,192,384]{2,1,0:T(8,128)(2,1)}, u32[]{:S(2)}, u32[]{:S(2)}) %collective-permute-start.52) | collective-permute-done | bytes 294944 | tf_op jit(solution)/shard_map/ppermute | solution.py:184
  503.1 5.9 collective-permute-done.56.refs_5_
  509.7 5.2 collective-permute-done.57.got
  528.7 6.5 %collective-permute-done.61.refs_1_ = bf16[192,384]{1,0:T(8,128)(2,1)S(1)} collective-permute-done((bf16[192,384]{1,0:T(8,128)(2,1)S(1)}, bf16[192,384]{1,0:T(8,128)(2,1)S(1)}, u32[]{:S(2)}, u32[]{:S(2)}) %collective-permute-start.61) | collective-permute-done | bytes 147488 | tf_op jit(solution)/shard_map/ppermute | solution.py:184
  535.2 7.3 %collective-permute-done.62.got = bf16[2,48,1920]{2,1,0:T(8,128)(2,1)S(1)} collective-permute-done((bf16[2,48,1920]{2,1,0:T(8,128)(2,1)S(1)}, bf16[2,48,1920]{2,1,0:T(8,128)(2,1)S(1)}, u32[]{:S(2)}, u32[]{:S(2)}) %collective-permute-start.62) | collective-permute-done | bytes 368672 | tf_op jit(solution)/shard_map/ppermute | solution.py:184
  549.8 9.4 %collective-permute-done.69 = f32[2,12,768]{2,1,0:T(8,128)S(1)} collective-permute-done((f32[2,12,768]{2,1,0:T(8,128)S(1)}, f32[2,12,768]{2,1,0:T(8,128)S(1)}, u32[]{:S(2)}, u32[]{:S(2)}) %collective-permute-start.69) | collective-permute-done | bytes 73760 | tf_op jit(solution)/shard_map/ppermute | solution.py:184
  574.0 5.7 collective-permute-done.77.refs_5_
  581.6 5.7 collective-permute-done.75
  589.1 14.4 %collective-permute-done.82.refs_1_ = bf16[2,48,3072]{2,1,0:T(8,128)(2,1)S(1)} collective-permute-done((bf16[2,48,3072]{2,1,0:T(8,128)(2,1)S(1)}, bf16[2,48,3072]{2,1,0:T(8,128)(2,1)S(1)}, u32[]{:S(2)}, u32[]{:S(2)}) %collective-permute-start.82) | collective-permute-done | bytes 589856 | tf_op jit(solution)/shard_map/ppermute | solution.py:184
  (692 shorter events, 295.1 us)
Async XLA Ops:
  7.2 37.9 %all-gather.9.cloned.1.call-start = ((), (), s32[]{:S(2)}) async-start(), calls=%async_computation | async-start | bytes 1536000 | tf_op jit(solution)/shard_map/all_gather | solution.py:487
  11.0 65.8 %all-gather.11.cloned.1.call-start = ((), (), s32[]{:S(2)}) async-start(), calls=%async_computation.1 | async-start | bytes 1474560 | tf_op jit(solution)/shard_map/all_gather | solution.py:487
  45.1 76.4 %all-gather.13.cloned.1.call-start = ((), (), s32[]{:S(2)}) async-start(), calls=%async_computation.2 | async-start | bytes 1474560 | tf_op jit(solution)/shard_map/all_gather | solution.py:487
  45.2 28.4 %collective-permute-start = (bf16[4,48,3200]{2,1,0:T(8,128)(2,1)}, bf16[4,48,3200]{2,1,0:T(8,128)(2,1)S(1)}, u32[]{:S(2)}, u32[]{:S(2)}) collective-permute-start(bf16[4,48,3200]{2,1,0:T(8,128)(2,1)} %bitcast.124), channel_id=1, source_target_pairs={{0,16},{16,0},{1,17},{17,1},{2,18},{18,2},{3,19},{19,3},{4,20},{20... | collective-permute-start | bytes 3686408 | tf_op jit(solution)/shard_map/ppermute | solution.py:184
  46.7 28.2 %collective-permute-start.1 = (bf16[4,48,3200]{2,1,0:T(8,128)(2,1)}, bf16[4,48,3200]{2,1,0:T(8,128)(2,1)}, u32[]{:S(2)}, u32[]{:S(2)}) collective-permute-start(bf16[4,48,3200]{2,1,0:T(8,128)(2,1)} %bitcast.125), channel_id=1, source_target_pairs={{0,2},{1,3},{2,0},{3,1},{4,6},{5,7},{6,4},{7,5},{8,10},{9,11},{10,... | collective-permute-start | bytes 3686408 | tf_op jit(solution)/shard_map/ppermute | solution.py:184
  79.6 533.1 %all-gather.15.cloned.1.call-start = ((), (), s32[]{:S(2)}) async-start(), calls=%async_computation.3 | async-start | bytes 2359296 | tf_op jit(solution)/shard_map/all_gather | solution.py:576
  79.7 41.8 %collective-permute-start.4 = (bf16[4,48,3072]{2,1,0:T(8,128)(2,1)}, bf16[4,48,3072]{2,1,0:T(8,128)(2,1)}, u32[]{:S(2)}, u32[]{:S(2)}) collective-permute-start(bf16[4,48,3072]{2,1,0:T(8,128)(2,1)} %bitcast.8.refs_0_), channel_id=1, source_target_pairs={{0,16},{16,0},{1,17},{17,1},{2,18},{18,2},{3,19},{19,3},{4,20},{20... | collective-permute-start | bytes 3538952 | tf_op jit(solution)/shard_map/ppermute | solution.py:184
  81.2 40.2 %collective-permute-start.5 = (bf16[4,48,3072]{2,1,0:T(8,128)(2,1)}, bf16[4,48,3072]{2,1,0:T(8,128)(2,1)}, u32[]{:S(2)}, u32[]{:S(2)}) collective-permute-start(bf16[4,48,3072]{2,1,0:T(8,128)(2,1)} %bitcast.8.refs_0_), channel_id=1, source_target_pairs={{0,2},{1,3},{2,0},{3,1},{4,6},{5,7},{6,4},{7,5},{8,10},{9,11},{10,... | collective-permute-start | bytes 3538952 | tf_op jit(solution)/shard_map/ppermute | solution.py:184
  82.7 38.8 %collective-permute-start.2 = (bf16[2,48,3200]{2,1,0:T(8,128)(2,1)}, bf16[2,48,3200]{2,1,0:T(8,128)(2,1)S(1)}, u32[]{:S(2)}, u32[]{:S(2)}) collective-permute-start(bf16[2,48,3200]{2,1,0:T(8,128)(2,1)} %slice.167), channel_id=1, source_target_pairs={{0,2},{1,3},{2,0},{3,1},{4,6},{5,7},{6,4},{7,5},{8,10},{9,11},{10,... | collective-permute-start | bytes 1843208 | tf_op jit(solution)/shard_map/ppermute | solution.py:184
  83.2 38.2 %collective-permute-start.3 = (bf16[2,48,3200]{2,1,0:T(8,128)(2,1)}, bf16[2,48,3200]{2,1,0:T(8,128)(2,1)}, u32[]{:S(2)}, u32[]{:S(2)}) collective-permute-start(bf16[2,48,3200]{2,1,0:T(8,128)(2,1)} %slice.168), channel_id=1, source_target_pairs={{0,16},{16,0},{1,17},{17,1},{2,18},{18,2},{3,19},{19,3},{4,20},{20... | collective-permute-start | bytes 1843208 | tf_op jit(solution)/shard_map/ppermute | solution.py:184
  131.3 43.6 %collective-permute-start.13 = (bf16[4,192,768]{2,1,0:T(8,128)(2,1)}, bf16[4,192,768]{2,1,0:T(8,128)(2,1)}, u32[]{:S(2)}, u32[]{:S(2)}) collective-permute-start(bf16[4,192,768]{2,1,0:T(8,128)(2,1)} %bitcast.10.refs_0_), channel_id=1, source_target_pairs={{0,16},{16,0},{1,17},{17,1},{2,18},{18,2},{3,19},{19,3},{4,20},{20... | collective-permute-start | bytes 3538952 | tf_op jit(solution)/shard_map/ppermute | solution.py:184
  133.9 41.0 %collective-permute-start.14 = (bf16[4,192,768]{2,1,0:T(8,128)(2,1)}, bf16[4,192,768]{2,1,0:T(8,128)(2,1)}, u32[]{:S(2)}, u32[]{:S(2)}) collective-permute-start(bf16[4,192,768]{2,1,0:T(8,128)(2,1)} %bitcast.10.refs_0_), channel_id=1, source_target_pairs={{0,2},{1,3},{2,0},{3,1},{4,6},{5,7},{6,4},{7,5},{8,10},{9,11},{10,... | collective-permute-start | bytes 3538952 | tf_op jit(solution)/shard_map/ppermute | solution.py:184
  135.4 39.5 %collective-permute-start.11 = (bf16[2,48,3072]{2,1,0:T(8,128)(2,1)}, bf16[2,48,3072]{2,1,0:T(8,128)(2,1)}, u32[]{:S(2)}, u32[]{:S(2)}) collective-permute-start(bf16[2,48,3072]{2,1,0:T(8,128)(2,1)} %slice.169), channel_id=1, source_target_pairs={{0,2},{1,3},{2,0},{3,1},{4,6},{5,7},{6,4},{7,5},{8,10},{9,11},{10,... | collective-permute-start | bytes 1769480 | tf_op jit(solution)/shard_map/ppermute | solution.py:184
  135.9 38.9 %collective-permute-start.12 = (bf16[2,48,3072]{2,1,0:T(8,128)(2,1)}, bf16[2,48,3072]{2,1,0:T(8,128)(2,1)}, u32[]{:S(2)}, u32[]{:S(2)}) collective-permute-start(bf16[2,48,3072]{2,1,0:T(8,128)(2,1)} %slice.170), channel_id=1, source_target_pairs={{0,16},{16,0},{1,17},{17,1},{2,18},{18,2},{3,19},{19,3},{4,20},{20... | collective-permute-start | bytes 1769480 | tf_op jit(solution)/shard_map/ppermute | solution.py:184
  320.9 24.7 %collective-permute-start.34 = (bf16[2,2,48,1920]{3,2,1,0:T(8,128)(2,1)}, bf16[2,2,48,1920]{3,2,1,0:T(8,128)(2,1)S(1)}, u32[]{:S(2)}, u32[]{:S(2)}) collective-permute-start(bf16[2,2,48,1920]{3,2,1,0:T(8,128)(2,1)} %copy-done.125), channel_id=1, source_target_pairs={{0,16},{16,0},{1,17},{17,1},{2,18},{18,2},{3,19},{19,3},{4,20},{20... | collective-permute-start | bytes 2211848 | tf_op jit(solution)/shard_map/ppermute | solution.py:184
  321.5 24.1 %collective-permute-start.35 = (bf16[2,48,3840]{2,1,0:T(8,128)(2,1)}, bf16[2,48,3840]{2,1,0:T(8,128)(2,1)S(1)}, u32[]{:S(2)}, u32[]{:S(2)}) collective-permute-start(bf16[2,48,3840]{2,1,0:T(8,128)(2,1)} %copy-done.124), channel_id=1, source_target_pairs={{0,2},{1,3},{2,0},{3,1},{4,6},{5,7},{6,4},{7,5},{8,10},{9,11},{10,... | collective-permute-start | bytes 2211848 | tf_op jit(solution)/shard_map/ppermute | solution.py:184
  322.1 23.5 %collective-permute-start.32 = (bf16[2,192,384]{2,1,0:T(8,128)(2,1)}, bf16[2,192,384]{2,1,0:T(8,128)(2,1)S(1)}, u32[]{:S(2)}, u32[]{:S(2)}) collective-permute-start(bf16[2,192,384]{2,1,0:T(8,128)(2,1)} %copy-done.136), channel_id=1, source_target_pairs={{0,2},{1,3},{2,0},{3,1},{4,6},{5,7},{6,4},{7,5},{8,10},{9,11},{10,... | collective-permute-start | bytes 884744 | tf_op jit(solution)/shard_map/ppermute | solution.py:184
  323.6 22.1 %collective-permute-start.33 = (bf16[2,192,384]{2,1,0:T(8,128)(2,1)}, bf16[2,192,384]{2,1,0:T(8,128)(2,1)S(1)}, u32[]{:S(2)}, u32[]{:S(2)}) collective-permute-start(bf16[2,192,384]{2,1,0:T(8,128)(2,1)} %copy-done.135), channel_id=1, source_target_pairs={{0,16},{16,0},{1,17},{17,1},{2,18},{18,2},{3,19},{19,3},{4,20},{20... | collective-permute-start | bytes 884744 | tf_op jit(solution)/shard_map/ppermute | solution.py:184
  378.5 26.0 %collective-permute-start.44 = (bf16[4,384,768]{2,1,0:T(8,128)(2,1)}, bf16[4,384,768]{2,1,0:T(8,128)(2,1)}, u32[]{:S(2)}, u32[]{:S(2)}) collective-permute-start(bf16[4,384,768]{2,1,0:T(8,128)(2,1)} %get-tuple-element.939), channel_id=1, source_target_pairs={{0,1},{1,0},{2,3},{3,2},{4,5},{5,4},{6,7},{7,6},{8,9},{9,8},{10,11... | collective-permute-start | bytes 7077896 | tf_op jit(solution)/shard_map/ppermute | solution.py:184
  378.5 26.0 %collective-permute-start.42 = (bf16[2,2,48,1152]{3,2,1,0:T(8,128)(2,1)}, bf16[2,2,48,1152]{3,2,1,0:T(8,128)(2,1)}, u32[]{:S(2)}, u32[]{:S(2)}) collective-permute-start(bf16[2,2,48,1152]{3,2,1,0:T(8,128)(2,1)} %get-tuple-element.937), channel_id=1, source_target_pairs={{0,16},{16,0},{1,17},{17,1},{2,18},{18,2},{3,19},{19,3},{4,20},{20... | collective-permute-start | bytes 1327112 | tf_op jit(solution)/shard_map/ppermute | solution.py:184
  379.7 24.8 %collective-permute-start.43 = (bf16[2,48,2304]{2,1,0:T(8,128)(2,1)}, bf16[2,48,2304]{2,1,0:T(8,128)(2,1)}, u32[]{:S(2)}, u32[]{:S(2)}) collective-permute-start(bf16[2,48,2304]{2,1,0:T(8,128)(2,1)} %get-tuple-element.938), channel_id=1, source_target_pairs={{0,2},{1,3},{2,0},{3,1},{4,6},{5,7},{6,4},{7,5},{8,10},{9,11},{10,... | collective-permute-start | bytes 1327112 | tf_op jit(solution)/shard_map/ppermute | solution.py:184
  380.5 24.0 %collective-permute-start.41 = (bf16[2,48,1920]{2,1,0:T(8,128)(2,1)}, bf16[2,48,1920]{2,1,0:T(8,128)(2,1)}, u32[]{:S(2)}, u32[]{:S(2)}) collective-permute-start(bf16[2,48,1920]{2,1,0:T(8,128)(2,1)} %get-tuple-element.936), channel_id=1, source_target_pairs={{0,8},{4,12},{8,0},{12,4},{1,9},{5,13},{9,1},{13,5},{2,10},{6,14},... | collective-permute-start | bytes 1105928 | tf_op jit(solution)/shard_map/ppermute | solution.py:184
  415.9 31.5 %collective-permute-start.50 = (bf16[4,96,3840]{2,1,0:T(8,128)(2,1)}, bf16[4,96,3840]{2,1,0:T(8,128)(2,1)}, u32[]{:S(2)}, u32[]{:S(2)}) collective-permute-start(bf16[4,96,3840]{2,1,0:T(8,128)(2,1)} %get-tuple-element.985), channel_id=1, source_target_pairs={{0,1},{1,0},{2,3},{3,2},{4,5},{5,4},{6,7},{7,6},{8,9},{9,8},{10,11... | collective-permute-start | bytes 8847368 | tf_op jit(solution)/shard_map/ppermute | solution.py:184
  415.9 31.5 %collective-permute-start.48 = (bf16[2,2,192,384]{3,2,1,0:T(8,128)(2,1)}, bf16[2,2,192,384]{3,2,1,0:T(8,128)(2,1)S(1)}, u32[]{:S(2)}, u32[]{:S(2)}) collective-permute-start(bf16[2,2,192,384]{3,2,1,0:T(8,128)(2,1)} %copy-done.127), channel_id=1, source_target_pairs={{0,16},{16,0},{1,17},{17,1},{2,18},{18,2},{3,19},{19,3},{4,20},{20... | collective-permute-start | bytes 1769480 | tf_op jit(solution)/shard_map/ppermute | solution.py:184
  417.4 30.0 %collective-permute-start.49 = (bf16[2,192,768]{2,1,0:T(8,128)(2,1)}, bf16[2,192,768]{2,1,0:T(8,128)(2,1)S(1)}, u32[]{:S(2)}, u32[]{:S(2)}) collective-permute-start(bf16[2,192,768]{2,1,0:T(8,128)(2,1)} %copy-done.126), channel_id=1, source_target_pairs={{0,2},{1,3},{2,0},{3,1},{4,6},{5,7},{6,4},{7,5},{8,10},{9,11},{10,... | collective-permute-start | bytes 1769480 | tf_op jit(solution)/shard_map/ppermute | solution.py:184
  418.0 22.1 %collective-permute-start.45 = (bf16[48,1920]{1,0:T(8,128)(2,1)}, bf16[48,1920]{1,0:T(8,128)(2,1)S(1)}, u32[]{:S(2)}, u32[]{:S(2)}) collective-permute-start(bf16[48,1920]{1,0:T(8,128)(2,1)} %copy-done.140), channel_id=1, source_target_pairs={{0,4},{4,0},{8,12},{12,8},{1,5},{5,1},{9,13},{13,9},{2,6},{6,2},{1... | collective-permute-start | bytes 552968 | tf_op jit(solution)/shard_map/ppermute | solution.py:184
  453.4 23.8 %collective-permute-start.54 = (bf16[2,2,48,1920]{3,2,1,0:T(8,128)(2,1)}, bf16[2,2,48,1920]{3,2,1,0:T(8,128)(2,1)}, u32[]{:S(2)}, u32[]{:S(2)}) collective-permute-start(bf16[2,2,48,1920]{3,2,1,0:T(8,128)(2,1)} %get-tuple-element.1033), channel_id=1, source_target_pairs={{0,16},{16,0},{1,17},{17,1},{2,18},{18,2},{3,19},{19,3},{4,20},{20... | collective-permute-start | bytes 2211848 | tf_op jit(solution)/shard_map/ppermute | solution.py:184
  453.9 23.2 %collective-permute-start.55 = (bf16[2,48,3840]{2,1,0:T(8,128)(2,1)}, bf16[2,48,3840]{2,1,0:T(8,128)(2,1)}, u32[]{:S(2)}, u32[]{:S(2)}) collective-permute-start(bf16[2,48,3840]{2,1,0:T(8,128)(2,1)} %get-tuple-element.1034), channel_id=1, source_target_pairs={{0,2},{1,3},{2,0},{3,1},{4,6},{5,7},{6,4},{7,5},{8,10},{9,11},{10,... | collective-permute-start | bytes 2211848 | tf_op jit(solution)/shard_map/ppermute | solution.py:184
  487.2 29.1 %collective-permute-start.60 = (bf16[4,96,2304]{2,1,0:T(8,128)(2,1)}, bf16[4,96,2304]{2,1,0:T(8,128)(2,1)}, u32[]{:S(2)}, u32[]{:S(2)}) collective-permute-start(bf16[4,96,2304]{2,1,0:T(8,128)(2,1)} %get-tuple-element.1082), channel_id=1, source_target_pairs={{0,1},{1,0},{2,3},{3,2},{4,5},{5,4},{6,7},{7,6},{8,9},{9,8},{10,11... | collective-permute-start | bytes 5308424 | tf_op jit(solution)/shard_map/ppermute | solution.py:184
  491.8 23.7 %collective-permute-start.58 = (bf16[2,48,1920]{2,1,0:T(8,128)(2,1)}, bf16[2,48,1920]{2,1,0:T(8,128)(2,1)S(1)}, u32[]{:S(2)}, u32[]{:S(2)}) collective-permute-start(bf16[2,48,1920]{2,1,0:T(8,128)(2,1)} %copy-done.132), channel_id=1, source_target_pairs={{0,2},{1,3},{2,0},{3,1},{4,6},{5,7},{6,4},{7,5},{8,10},{9,11},{10,... | collective-permute-start | bytes 1105928 | tf_op jit(solution)/shard_map/ppermute | solution.py:184
  493.0 22.6 %collective-permute-start.59 = (bf16[2,48,1920]{2,1,0:T(8,128)(2,1)}, bf16[2,48,1920]{2,1,0:T(8,128)(2,1)S(1)}, u32[]{:S(2)}, u32[]{:S(2)}) collective-permute-start(bf16[2,48,1920]{2,1,0:T(8,128)(2,1)} %copy-done.131), channel_id=1, source_target_pairs={{0,16},{16,0},{1,17},{17,1},{2,18},{18,2},{3,19},{19,3},{4,20},{20... | collective-permute-start | bytes 1105928 | tf_op jit(solution)/shard_map/ppermute | solution.py:184
  589.1 23.6 %collective-permute-start.81 = (bf16[2,48,3072]{2,1,0:T(8,128)(2,1)S(1)}, bf16[2,48,3072]{2,1,0:T(8,128)(2,1)S(1)}, u32[]{:S(2)}, u32[]{:S(2)}) collective-permute-start(bf16[2,48,3072]{2,1,0:T(8,128)(2,1)S(1)} %pad_maximum_fusion.2.refs_0_), channel_id=1, source_target_pairs={{0,1},{1,0},{2,3},{3,2},{4,5},{5,4},{6,7},{7,6},{8,9},{9,8},{10,11... | collective-permute-start | bytes 1769480 | tf_op jit(solution)/shard_map/ppermute | solution.py:184
  (241 other events, 2262.5 us)
Sparse Core Ops, SparseCore 0:
  11.1 33.9 all-gather.8
  47.2 29.5 all-gather.10
  79.7 29.5 all-gather.12
  581.8 25.1 all-gather.14

commit v5 on v4

--- a/solution.py
+++ b/solution.py
@@ -468,12 +468,41 @@
     )(normed, weight, bias[None])
 
 
+def slope_kernel(low_ref, weight_ref, slope_ref, out_ref):
+    product = times_transpose(low_ref[...], weight_ref[...])
+    out_ref[...] = (product * slope_ref[...].astype(jnp.float32)).astype(jnp.bfloat16)
+
+
+def slope_call(low, weight, slope):
+    row_count, width = low.shape
+    columns = slope.shape[1]
+    block = pl.BlockSpec((row_count, width), lambda j: (0, j))
+    return pl.pallas_call(
+        slope_kernel,
+        grid=(columns // width,),
+        out_shape=jax.ShapeDtypeStruct((row_count, columns), jnp.bfloat16),
+        in_specs=[
+            pl.BlockSpec((row_count, width), lambda j: (0, 0)),
+            pl.BlockSpec((width, width), lambda j: (j, 0)),
+            block,
+        ],
+        out_specs=block,
+        compiler_params=pltpu.CompilerParams(vmem_limit_bytes=20 * 1024 * 1024),
+        cost_estimate=SHORT,
+    )(low, weight, slope)
+
+
 def ordered(own, other, index, axis):
     first = jnp.where(index == 0, own, other)
     second = jnp.where(index == 0, other, own)
     return jnp.concatenate([first, second], axis=axis)
 
 
+def far_kernel(where_ref, over_x, over_y, low, high):
+    low[...] = over_x[...]
+    high[...] = over_y[...]
+
+
 class Moves:
     def __init__(self, where):
         self.where = where
@@ -493,7 +522,11 @@
 
         def beyond(*arrays):
             _, over_x, over_y = arrays
-            return (arrays, [(over_x[:2], self.over_y), (over_y[2:], self.over_x)])
+            shape = (2, *over_x.shape[1:])
+            low, high = local_call(
+                far_kernel, self.where, ((over_x, 0), (over_y, 2)), (shape, shape), steps=2
+            )
+            return (arrays, [(low, self.over_y), (high, self.over_x)])
 
         return [along, across, beyond]
 
@@ -616,7 +649,6 @@
         ready = [step(*state) for step, state in zip(steps, states)]
         kept = [keep for keep, _ in ready]
         sent = [[array for array, _ in sends] for _, sends in ready]
-        inputs, kept, sent = lax.optimization_barrier((inputs, kept, sent))
         got = [
             [move(array) for array, (_, move) in zip(arrays, sends)]
             for arrays, (_, sends) in zip(sent, ready)
@@ -761,8 +793,7 @@
         out_grad = upstream.astype(jnp.float32) * self.living[:, None]
         low = out_grad.astype(jnp.bfloat16)
         found = self.grads("contract", (activated, low), deep=True)
-        activated_grad = times_transpose(low, self.params["contract"])
-        expand_low = (activated_grad * slope.astype(jnp.float32)).astype(jnp.bfloat16)
+        expand_low = slope_call(low, self.params["contract"], slope)
         return dict(found, out_grad=out_grad, expand_low=expand_low)
 
     def norm(self, expand_low, normed_two, out_grad, middle, stats_f, mixed_low):

time: 639 us -> 610 us (0.955)
  Pallas kernels: 154 us -> 167 us
  waiting for transfers between devices: 213 us -> 200 us
  local copies, waits for them, and re-layouts: 85.5 us -> 73 us
  matrix products: 58.6 us -> 46.2 us
    ppermute x81, waiting for transfers between devices: 175 us -> 162 us  [swap(): lax.ppermute(block, axis, [(i, i ^ bit) for i in range(lax.axis_size(axis...]
    dot_general x8 -> x6, matrix products: 40.9 us -> 28.6 us  [times_transpose(): lax.dot_general(left_side, right_side, (((1,), (1,)), ((), ())), preferre...]
    slice x6 -> x0, local copies, waits for them, and re-layouts: 10.7 us -> none  [beyond(): return (arrays, [(over_x[:2], self.over_y), (over_y[2:], self.over_x)])]
    pallas_call x26 -> x29, Pallas kernels: 38.7 us -> 46.9 us  [local_call(): pl.pallas_call(kernel, grid=(steps,), out_shape=[jax.ShapeDtypeStruct(sha...]
    pallas_call x0 -> x2, Pallas kernels: none -> 7.39 us  [slope_call(): pl.pallas_call(slope_kernel, grid=(columns // width,), out_shape=jax.Shap...]
    unnamed x386 -> x310, local copies, waits for them, and re-layouts: 61.7 us -> 59.9 us
  transfers between devices with their start and end apart: 88 -> 88, of which waited for: 28 -> 27; matrix products, arithmetic and copies ran while one was open for 14% -> 11% of each run, Pallas kernels for 14% -> 22%
where the time goes in v5:
time: 610 us; the launch traced here: 600 us
  waiting for transfers between devices  200 us (33%)
  Pallas kernels  167 us (27%)
  local copies, waits for them, and re-layouts  73 us (12%)
  starting transfers between devices  65.2 us (11%)
  matrix products  46.2 us (8%)
  other arithmetic  31.9 us (5%)
  between operations  16.2 us (3%)
    ppermute x81, waiting for transfers between devices, swap(): lax.ppermute(block, axis, [(i, i ^ bit) for i in range(lax.axis_size(axis...  162 us
    ppermute x81, starting transfers between devices, swap(): lax.ppermute(block, axis, [(i, i ^ bit) for i in range(lax.axis_size(axis...  63 us
    unnamed x310, local copies, waits for them, and re-layouts  59.9 us
    pallas_call x4, Pallas kernels, attention_call(): pl.pallas_call(kernel, grid=(pairs,), out_shape=[jax.ShapeDtypeStruct((ro...  52.1 us
    pallas_call x29, Pallas kernels, local_call(): pl.pallas_call(kernel, grid=(steps,), out_shape=[jax.ShapeDtypeStruct(sha...  46.9 us
    all_gather x3, waiting for transfers between devices, along(): return ((), [(own, lambda array: lax.all_gather(array, 'shard', axis=0))])  34.3 us
    pallas_call x6, Pallas kernels, grad_call(): pl.pallas_call(functools.partial(grad_kernel, kinds), grid=(steps,), out_...  32.6 us
    dot_general x6, matrix products, times_transpose(): lax.dot_general(left_side, right_side, (((1,), (1,)), ((), ())), preferre...  28.6 us
  transfers between devices with their start and end apart: 88, of which 27 were waited for; matrix products, arithmetic and copies ran while one was open for 11% of the time, Pallas kernels for 22%

profile of v5, /device:TPU:0, one launch (start us, length us, event | category | flops | bytes accessed | tf_op | source)
XLA Modules:
  0.0 600.2 jit_solution(5325158370730968112)
XLA Ops:
  12.7 32.4 %all-gather.9.cloned.1.call-done = bf16[192,3200]{1,0:T(8,128)(2,1)} async-done(((bf16[48,3200]{1,0:T(8,128)(2,1)}), bf16[192,3200]{1,0:T(8,128)(2,1)}) %all-gather.9.cloned.1.call-update) | async-done | bytes 1228816 | tf_op jit(solution)/shard_map/all_gather | solution.py:516
  49.9 23.7 %collective-permute-done.over_x.refs_1_ = bf16[4,48,3200]{2,1,0:T(8,128)(2,1)S(1)} collective-permute-done((bf16[4,48,3200]{2,1,0:T(8,128)(2,1)}, bf16[4,48,3200]{2,1,0:T(8,128)(2,1)S(1)}, u32[]{:S(2)}, u32[]{:S(2)}) %collective-permute-start) | collective-permute-done | bytes 1228832 | tf_op jit(solution)/shard_map/ppermute | solution.py:184
  84.1 34.7 %collective-permute-done.2.refs_3_ = bf16[2,48,3200]{2,1,0:T(8,128)(2,1)} collective-permute-done((bf16[2,48,3200]{2,1,0:T(8,128)(2,1)}, bf16[2,48,3200]{2,1,0:T(8,128)(2,1)}, u32[]{:S(2)}, u32[]{:S(2)}) %collective-permute-start.2) | collective-permute-done | bytes 614432 | tf_op jit(solution)/shard_map/ppermute | solution.py:184
  129.8 5.3 shard_map.281
  146.5 11.7 %shard_map.282 = (bf16[512,768]{1,0:T(8,128)(2,1)S(1)}, f32[512,768]{1,0:T(8,128)S(1)}) custom-call(s32[512,1]{1,0:T(8,128)S(1)} %copy.38.column_ref, s32[1,512]{1,0:T(1,128)S(1)} %bitcast.133, bf16[512,2304]{1,0:T(8,128)(2,1)S(1)} %fusion.q_ref.k_ref.v_ref, bf16[512,2304]{1,0:T(8,128)(2,1)S(1)} %fusion.q_ref.k_ref.v_ref, ...), custom_call_target="tpu_custom_call" | custom-call | flops 1 | bytes 1 | tf_op jit(solution)/shard_map/pallas_call | solution.py:153
  163.2 5.0 collective-permute-done.11.refs_3_
  182.4 5.0 shard_map.284
  187.4 6.8 %shard_map.285 = (bf16[512,3072]{1,0:T(8,128)(2,1)S(1)}, bf16[512,3072]{1,0:T(8,128)(2,1)S(1)}) custom-call(bf16[512,768]{1,0:T(8,128)(2,1)S(1)} %add_convert_fusion.3.normed_ref.refs_0_, bf16[768,3072]{1,0:T(8,128)(2,1)S(1)} %bitcast.116, f32[1,3072]{1,0:T(1,128)S(1)} %bitcast.138), custom_call_target="tpu_custom_call" | custom-call | flops 1 | bytes 1 | tf_op jit(solution)/shard_map/pallas_call | solution.py:456
  211.0 12.1 %shard_map.288 = (bf16[512,768]{1,0:T(8,128)(2,1)S(1)}, f32[512,768]{1,0:T(8,128)S(1)}) custom-call(s32[512,1]{1,0:T(8,128)S(1)} %copy.38.column_ref, s32[1,512]{1,0:T(1,128)S(1)} %bitcast.134, bf16[512,2304]{1,0:T(8,128)(2,1)S(1)} %fusion.1.q_ref.k_ref.v_ref, bf16[512,2304]{1,0:T(8,128)(2,1)S(1)} %fusion.1.q_ref.k_ref.v_ref, ...), custom_call_target="tpu_custom_call" | custom-call | flops 1 | bytes 1 | tf_op jit(solution)/shard_map/pallas_call | solution.py:153
  225.2 6.8 %shard_map.289 = (bf16[512,3072]{1,0:T(8,128)(2,1)S(1)}, bf16[512,3072]{1,0:T(8,128)(2,1)S(1)}) custom-call(bf16[512,768]{1,0:T(8,128)(2,1)S(1)} %add_convert_fusion.2.normed_ref.refs_0_, bf16[768,3072]{1,0:T(8,128)(2,1)S(1)} %bitcast.118, f32[1,3072]{1,0:T(1,128)S(1)} %bitcast.137), custom_call_target="tpu_custom_call" | custom-call | flops 1 | bytes 1 | tf_op jit(solution)/shard_map/pallas_call | solution.py:456
  249.6 4.9 shard_map.290
  258.5 6.9 %multiply_reduce_fusion.6 = (f32[768]{0:T(1024)S(1)}, f32[512]{0:T(512)S(1)}, f32[512]{0:T(512)S(1)}, f32[768]{0:T(1024)S(1)}, f32[512,768]{1,0:T(8,128)S(1)}) fusion(f32[512,768]{1,0:T(8,128)} %copy-done.115, f32[512]{0:T(512)S(1)} %broadcast_multiply_fusion.8, f32[512]{0:T(512)S(1)} %add_rsqrt_fusion, f32[768]{0:T(1024)S(1)} %get-tuple-element.535, ...), kind=kOutput, calls=%fused_computation.41 | convolution fusion | flops 2419455488 | bytes 11027456 | tf_op jit(solution)/shard_map/dot_general | solution.py:60
  268.5 6.6 %shard_map.292 = (bf16[4,96,3840]{2,1,0:T(8,128)(2,1)S(1)}, bf16[4,96,3840]{2,1,0:T(8,128)(2,1)S(1)}, f32[1,3840]{1,0:T(1,128)S(1)}) custom-call(s32[4]{0:T(128)S(1)} %pad_add_fusion.where_ref, bf16[512,768]{1,0:T(8,128)(2,1)S(1)} %copy-done.22, bf16[512,768]{1,0:T(8,128)(2,1)S(1)} %copy-done.51, bf16[512,3072]{1,0:T(8,128)(2,1)S(1)} %copy-done.7, ...), custom_call_target="tpu_custom_call" | custom-call | flops 1 | bytes 1 | tf_op jit(solution)/shard_map/pallas_call | solution.py:423
  285.8 14.1 %shard_map.293 = (bf16[512,768]{1,0:T(8,128)(2,1)S(1)}, bf16[512,768]{1,0:T(8,128)(2,1)S(1)}, bf16[512,768]{1,0:T(8,128)(2,1)S(1)}) custom-call(s32[512,1]{1,0:T(8,128)S(1)} %copy.38.column_ref, s32[1,512]{1,0:T(1,128)S(1)} %bitcast.135, bf16[512,2304]{1,0:T(8,128)(2,1)S(1)} %copy-done.3, bf16[512,2304]{1,0:T(8,128)(2,1)S(1)} %copy-done.3, ...), custom_call_target="tpu_custom_call" | custom-call | flops 1 | bytes 1 | tf_op jit(solution)/shard_map/pallas_call | solution.py:153
  310.2 4.8 shard_map.295
  316.4 5.4 multiply_reduce_fusion.4
  322.4 7.1 %collective-permute-done.32.low_got = bf16[2,192,384]{2,1,0:T(8,128)(2,1)} collective-permute-done((bf16[2,192,384]{2,1,0:T(8,128)(2,1)}, bf16[2,192,384]{2,1,0:T(8,128)(2,1)}, u32[]{:S(2)}, u32[]{:S(2)}) %collective-permute-start.32) | collective-permute-done | bytes 294944 | tf_op jit(solution)/shard_map/ppermute | solution.py:184
  346.3 4.9 shard_map.298
  368.7 6.1 %multiply_reduce_fusion.2 = (f32[768]{0:T(1024)}, f32[512]{0:T(512)S(1)}, f32[512]{0:T(512)S(1)}, f32[768]{0:T(1024)}, f32[512,768]{1,0:T(8,128)S(1)}) fusion(f32[512,768]{1,0:T(8,128)S(1)} %copy-done.118, f32[512]{0:T(512)S(1)} %broadcast_multiply_fusion.10, f32[512]{0:T(512)S(1)} %add_rsqrt_fusion.2, f32[768]{0:T(1024)S(1)} %get-tuple-element.512, ...), kind=kOutput, calls=%fused_computation.32 | convolution fusion | flops 2419455488 | bytes 11027456 | tf_op jit(solution)/shard_map/dot_general | solution.py:60
  376.6 7.3 %shard_map.302 = (bf16[4,96,3840]{2,1,0:T(8,128)(2,1)S(1)}, bf16[4,96,3840]{2,1,0:T(8,128)(2,1)}, f32[1,3840]{1,0:T(1,128)S(1)}) custom-call(s32[4]{0:T(128)S(1)} %pad_add_fusion.where_ref, bf16[512,768]{1,0:T(8,128)(2,1)S(1)} %add_convert_fusion.3.normed_ref.refs_0_, bf16[512,768]{1,0:T(8,128)(2,1)S(1)} %copy-done.49, bf16[512,3072]{1,0:T(8,128)(2,1)S(1)} %copy-done.5, ...), custom_call_target="tpu_custom_call" | custom-call | flops 1 | bytes 1 | tf_op jit(solution)/shard_map/pallas_call | solution.py:423
  400.4 14.1 %shard_map.306 = (bf16[512,768]{1,0:T(8,128)(2,1)S(1)}, bf16[512,768]{1,0:T(8,128)(2,1)S(1)}, bf16[512,768]{1,0:T(8,128)(2,1)S(1)}) custom-call(s32[512,1]{1,0:T(8,128)S(1)} %copy.38.column_ref, s32[1,512]{1,0:T(1,128)S(1)} %bitcast.136, bf16[512,2304]{1,0:T(8,128)(2,1)S(1)} %fusion.q_ref.k_ref.v_ref, bf16[512,2304]{1,0:T(8,128)(2,1)S(1)} %fusion.q_ref.k_ref.v_ref, ...), custom_call_target="tpu_custom_call" | custom-call | flops 1 | bytes 1 | tf_op jit(solution)/shard_map/pallas_call | solution.py:153
  415.9 5.9 collective-permute-done.47.high_got
  442.4 6.3 %collective-permute-done.52.low_got = bf16[2,192,384]{2,1,0:T(8,128)(2,1)} collective-permute-done((bf16[2,192,384]{2,1,0:T(8,128)(2,1)}, bf16[2,192,384]{2,1,0:T(8,128)(2,1)}, u32[]{:S(2)}, u32[]{:S(2)}) %collective-permute-start.52) | collective-permute-done | bytes 294944 | tf_op jit(solution)/shard_map/ppermute | solution.py:184
  458.7 4.6 multiply_reduce_fusion
  468.5 12.2 %collective-permute-done.57.got = bf16[2,192,384]{2,1,0:T(8,128)(2,1)S(1)} collective-permute-done((bf16[2,192,384]{2,1,0:T(8,128)(2,1)S(1)}, bf16[2,192,384]{2,1,0:T(8,128)(2,1)S(1)}, u32[]{:S(2)}, u32[]{:S(2)}) %collective-permute-start.57) | collective-permute-done | bytes 294944 | tf_op jit(solution)/shard_map/ppermute | solution.py:184
  501.9 5.7 collective-permute-done.61.refs_1_
  507.6 7.7 %collective-permute-done.62.got = bf16[2,48,1920]{2,1,0:T(8,128)(2,1)S(1)} collective-permute-done((bf16[2,48,1920]{2,1,0:T(8,128)(2,1)S(1)}, bf16[2,48,1920]{2,1,0:T(8,128)(2,1)S(1)}, u32[]{:S(2)}, u32[]{:S(2)}) %collective-permute-start.62) | collective-permute-done | bytes 368672 | tf_op jit(solution)/shard_map/ppermute | solution.py:184
  522.9 6.9 %collective-permute-done.69 = f32[2,12,768]{2,1,0:T(8,128)S(1)} collective-permute-done((f32[2,12,768]{2,1,0:T(8,128)S(1)}, f32[2,12,768]{2,1,0:T(8,128)S(1)}, u32[]{:S(2)}, u32[]{:S(2)}) %collective-permute-start.69) | collective-permute-done | bytes 73760 | tf_op jit(solution)/shard_map/ppermute | solution.py:184
  537.3 4.6 collective-permute-done.72.refs_2_
  544.1 6.0 %collective-permute-done.77.refs_5_ = bf16[2,192,384]{2,1,0:T(8,128)(2,1)S(1)} collective-permute-done((bf16[2,192,384]{2,1,0:T(8,128)(2,1)S(1)}, bf16[2,192,384]{2,1,0:T(8,128)(2,1)S(1)}, u32[]{:S(2)}, u32[]{:S(2)}) %collective-permute-start.77) | collective-permute-done | bytes 294944 | tf_op jit(solution)/shard_map/ppermute | solution.py:184
  552.3 4.7 collective-permute-done.75
  560.4 14.6 %collective-permute-done.82.refs_1_ = bf16[2,48,3072]{2,1,0:T(8,128)(2,1)S(1)} collective-permute-done((bf16[2,48,3072]{2,1,0:T(8,128)(2,1)S(1)}, bf16[2,48,3072]{2,1,0:T(8,128)(2,1)S(1)}, u32[]{:S(2)}, u32[]{:S(2)}) %collective-permute-start.82) | collective-permute-done | bytes 589856 | tf_op jit(solution)/shard_map/ppermute | solution.py:184
  (612 shorter events, 279.2 us)
Async XLA Ops:
  7.2 37.9 %all-gather.9.cloned.1.call-start = ((), (), s32[]{:S(2)}) async-start(), calls=%async_computation | async-start | bytes 1536000 | tf_op jit(solution)/shard_map/all_gather | solution.py:516
  11.0 65.8 %all-gather.11.cloned.1.call-start = ((), (), s32[]{:S(2)}) async-start(), calls=%async_computation.1 | async-start | bytes 1474560 | tf_op jit(solution)/shard_map/all_gather | solution.py:516
  45.1 73.6 %all-gather.13.cloned.1.call-start = ((), (), s32[]{:S(2)}) async-start(), calls=%async_computation.2 | async-start | bytes 1474560 | tf_op jit(solution)/shard_map/all_gather | solution.py:516
  45.2 28.4 %collective-permute-start = (bf16[4,48,3200]{2,1,0:T(8,128)(2,1)}, bf16[4,48,3200]{2,1,0:T(8,128)(2,1)S(1)}, u32[]{:S(2)}, u32[]{:S(2)}) collective-permute-start(bf16[4,48,3200]{2,1,0:T(8,128)(2,1)} %bitcast.124), channel_id=1, source_target_pairs={{0,16},{16,0},{1,17},{17,1},{2,18},{18,2},{3,19},{19,3},{4,20},{20... | collective-permute-start | bytes 3686408 | tf_op jit(solution)/shard_map/ppermute | solution.py:184
  46.7 28.2 %collective-permute-start.1 = (bf16[4,48,3200]{2,1,0:T(8,128)(2,1)}, bf16[4,48,3200]{2,1,0:T(8,128)(2,1)}, u32[]{:S(2)}, u32[]{:S(2)}) collective-permute-start(bf16[4,48,3200]{2,1,0:T(8,128)(2,1)} %bitcast.125), channel_id=1, source_target_pairs={{0,2},{1,3},{2,0},{3,1},{4,6},{5,7},{6,4},{7,5},{8,10},{9,11},{10,... | collective-permute-start | bytes 3686408 | tf_op jit(solution)/shard_map/ppermute | solution.py:184
  76.8 507.4 %all-gather.15.cloned.1.call-start = ((), (), s32[]{:S(2)}) async-start(), calls=%async_computation.3 | async-start | bytes 2359296 | tf_op jit(solution)/shard_map/all_gather | solution.py:609
  76.9 41.9 %collective-permute-start.4 = (bf16[4,48,3072]{2,1,0:T(8,128)(2,1)}, bf16[4,48,3072]{2,1,0:T(8,128)(2,1)}, u32[]{:S(2)}, u32[]{:S(2)}) collective-permute-start(bf16[4,48,3072]{2,1,0:T(8,128)(2,1)} %bitcast.8.refs_0_), channel_id=1, source_target_pairs={{0,16},{16,0},{1,17},{17,1},{2,18},{18,2},{3,19},{19,3},{4,20},{20... | collective-permute-start | bytes 3538952 | tf_op jit(solution)/shard_map/ppermute | solution.py:184
  78.4 40.3 %collective-permute-start.5 = (bf16[4,48,3072]{2,1,0:T(8,128)(2,1)}, bf16[4,48,3072]{2,1,0:T(8,128)(2,1)}, u32[]{:S(2)}, u32[]{:S(2)}) collective-permute-start(bf16[4,48,3072]{2,1,0:T(8,128)(2,1)} %bitcast.8.refs_0_), channel_id=1, source_target_pairs={{0,2},{1,3},{2,0},{3,1},{4,6},{5,7},{6,4},{7,5},{8,10},{9,11},{10,... | collective-permute-start | bytes 3538952 | tf_op jit(solution)/shard_map/ppermute | solution.py:184
  82.0 36.7 %collective-permute-start.2 = (bf16[2,48,3200]{2,1,0:T(8,128)(2,1)}, bf16[2,48,3200]{2,1,0:T(8,128)(2,1)}, u32[]{:S(2)}, u32[]{:S(2)}) collective-permute-start(bf16[2,48,3200]{2,1,0:T(8,128)(2,1)} %get-tuple-element.471), channel_id=1, source_target_pairs={{0,2},{1,3},{2,0},{3,1},{4,6},{5,7},{6,4},{7,5},{8,10},{9,11},{10,... | collective-permute-start | bytes 1843208 | tf_op jit(solution)/shard_map/ppermute | solution.py:184
  82.6 36.2 %collective-permute-start.3 = (bf16[2,48,3200]{2,1,0:T(8,128)(2,1)}, bf16[2,48,3200]{2,1,0:T(8,128)(2,1)}, u32[]{:S(2)}, u32[]{:S(2)}) collective-permute-start(bf16[2,48,3200]{2,1,0:T(8,128)(2,1)} %get-tuple-element.472), channel_id=1, source_target_pairs={{0,16},{16,0},{1,17},{17,1},{2,18},{18,2},{3,19},{19,3},{4,20},{20... | collective-permute-start | bytes 1843208 | tf_op jit(solution)/shard_map/ppermute | solution.py:184
  125.5 42.7 %collective-permute-start.13 = (bf16[4,192,768]{2,1,0:T(8,128)(2,1)}, bf16[4,192,768]{2,1,0:T(8,128)(2,1)}, u32[]{:S(2)}, u32[]{:S(2)}) collective-permute-start(bf16[4,192,768]{2,1,0:T(8,128)(2,1)} %bitcast.10.refs_0_), channel_id=1, source_target_pairs={{0,16},{16,0},{1,17},{17,1},{2,18},{18,2},{3,19},{19,3},{4,20},{20... | collective-permute-start | bytes 3538952 | tf_op jit(solution)/shard_map/ppermute | solution.py:184
  127.2 41.0 %collective-permute-start.14 = (bf16[4,192,768]{2,1,0:T(8,128)(2,1)}, bf16[4,192,768]{2,1,0:T(8,128)(2,1)}, u32[]{:S(2)}, u32[]{:S(2)}) collective-permute-start(bf16[4,192,768]{2,1,0:T(8,128)(2,1)} %bitcast.10.refs_0_), channel_id=1, source_target_pairs={{0,2},{1,3},{2,0},{3,1},{4,6},{5,7},{6,4},{7,5},{8,10},{9,11},{10,... | collective-permute-start | bytes 3538952 | tf_op jit(solution)/shard_map/ppermute | solution.py:184
  128.7 39.5 %collective-permute-start.11 = (bf16[2,48,3072]{2,1,0:T(8,128)(2,1)}, bf16[2,48,3072]{2,1,0:T(8,128)(2,1)}, u32[]{:S(2)}, u32[]{:S(2)}) collective-permute-start(bf16[2,48,3072]{2,1,0:T(8,128)(2,1)} %get-tuple-element.495), channel_id=1, source_target_pairs={{0,2},{1,3},{2,0},{3,1},{4,6},{5,7},{6,4},{7,5},{8,10},{9,11},{10,... | collective-permute-start | bytes 1769480 | tf_op jit(solution)/shard_map/ppermute | solution.py:184
  129.3 38.9 %collective-permute-start.12 = (bf16[2,48,3072]{2,1,0:T(8,128)(2,1)}, bf16[2,48,3072]{2,1,0:T(8,128)(2,1)}, u32[]{:S(2)}, u32[]{:S(2)}) collective-permute-start(bf16[2,48,3072]{2,1,0:T(8,128)(2,1)} %get-tuple-element.496), channel_id=1, source_target_pairs={{0,16},{16,0},{1,17},{17,1},{2,18},{18,2},{3,19},{19,3},{4,20},{20... | collective-permute-start | bytes 1769480 | tf_op jit(solution)/shard_map/ppermute | solution.py:184
  173.9 24.1 %collective-permute-start.23 = (bf16[4,192,768]{2,1,0:T(8,128)(2,1)}, bf16[4,192,768]{2,1,0:T(8,128)(2,1)S(1)}, u32[]{:S(2)}, u32[]{:S(2)}) collective-permute-start(bf16[4,192,768]{2,1,0:T(8,128)(2,1)} %collective-permute-done.13.over_x.refs_1_), channel_id=1, source_target_pairs={{0,1},{1,0},{2,3},{3,2},{4,5},{5,4},{6,7},{7,6},{8,9},{9,8},{10,11... | collective-permute-start | bytes 3538952 | tf_op jit(solution)/shard_map/ppermute | solution.py:184
  304.6 24.9 %collective-permute-start.34 = (bf16[2,2,48,1920]{3,2,1,0:T(8,128)(2,1)}, bf16[2,2,48,1920]{3,2,1,0:T(8,128)(2,1)}, u32[]{:S(2)}, u32[]{:S(2)}) collective-permute-start(bf16[2,2,48,1920]{3,2,1,0:T(8,128)(2,1)} %get-tuple-element.612), channel_id=1, source_target_pairs={{0,16},{16,0},{1,17},{17,1},{2,18},{18,2},{3,19},{19,3},{4,20},{20... | collective-permute-start | bytes 2211848 | tf_op jit(solution)/shard_map/ppermute | solution.py:184
  305.2 24.3 %collective-permute-start.35 = (bf16[2,48,3840]{2,1,0:T(8,128)(2,1)}, bf16[2,48,3840]{2,1,0:T(8,128)(2,1)}, u32[]{:S(2)}, u32[]{:S(2)}) collective-permute-start(bf16[2,48,3840]{2,1,0:T(8,128)(2,1)} %get-tuple-element.613), channel_id=1, source_target_pairs={{0,2},{1,3},{2,0},{3,1},{4,6},{5,7},{6,4},{7,5},{8,10},{9,11},{10,... | collective-permute-start | bytes 2211848 | tf_op jit(solution)/shard_map/ppermute | solution.py:184
  329.5 25.2 %collective-permute-start.39 = (bf16[4,96,2304]{2,1,0:T(8,128)(2,1)}, bf16[4,96,2304]{2,1,0:T(8,128)(2,1)}, u32[]{:S(2)}, u32[]{:S(2)}) collective-permute-start(bf16[4,96,2304]{2,1,0:T(8,128)(2,1)} %get-tuple-element.643), channel_id=1, source_target_pairs={{0,1},{1,0},{2,3},{3,2},{4,5},{5,4},{6,7},{7,6},{8,9},{9,8},{10,11... | collective-permute-start | bytes 5308424 | tf_op jit(solution)/shard_map/ppermute | solution.py:184
  331.8 22.8 %collective-permute-start.37 = (bf16[2,48,1920]{2,1,0:T(8,128)(2,1)}, bf16[2,48,1920]{2,1,0:T(8,128)(2,1)}, u32[]{:S(2)}, u32[]{:S(2)}) collective-permute-start(bf16[2,48,1920]{2,1,0:T(8,128)(2,1)} %get-tuple-element.641), channel_id=1, source_target_pairs={{0,2},{1,3},{2,0},{3,1},{4,6},{5,7},{6,4},{7,5},{8,10},{9,11},{10,... | collective-permute-start | bytes 1105928 | tf_op jit(solution)/shard_map/ppermute | solution.py:184
  354.7 34.1 %collective-permute-start.44 = (bf16[4,384,768]{2,1,0:T(8,128)(2,1)}, bf16[4,384,768]{2,1,0:T(8,128)(2,1)}, u32[]{:S(2)}, u32[]{:S(2)}) collective-permute-start(bf16[4,384,768]{2,1,0:T(8,128)(2,1)} %copy-done.107), channel_id=1, source_target_pairs={{0,1},{1,0},{2,3},{3,2},{4,5},{5,4},{6,7},{7,6},{8,9},{9,8},{10,11... | collective-permute-start | bytes 7077896 | tf_op jit(solution)/shard_map/ppermute | solution.py:184
  360.3 28.4 %collective-permute-start.42 = (bf16[2,2,48,1152]{3,2,1,0:T(8,128)(2,1)}, bf16[2,2,48,1152]{3,2,1,0:T(8,128)(2,1)}, u32[]{:S(2)}, u32[]{:S(2)}) collective-permute-start(bf16[2,2,48,1152]{3,2,1,0:T(8,128)(2,1)} %get-tuple-element.682), channel_id=1, source_target_pairs={{0,16},{16,0},{1,17},{17,1},{2,18},{18,2},{3,19},{19,3},{4,20},{20... | collective-permute-start | bytes 1327112 | tf_op jit(solution)/shard_map/ppermute | solution.py:184
  360.8 27.9 %collective-permute-start.43 = (bf16[2,48,2304]{2,1,0:T(8,128)(2,1)}, bf16[2,48,2304]{2,1,0:T(8,128)(2,1)}, u32[]{:S(2)}, u32[]{:S(2)}) collective-permute-start(bf16[2,48,2304]{2,1,0:T(8,128)(2,1)} %get-tuple-element.683), channel_id=1, source_target_pairs={{0,2},{1,3},{2,0},{3,1},{4,6},{5,7},{6,4},{7,5},{8,10},{9,11},{10,... | collective-permute-start | bytes 1327112 | tf_op jit(solution)/shard_map/ppermute | solution.py:184
  364.3 24.5 %collective-permute-start.41 = (bf16[2,48,1920]{2,1,0:T(8,128)(2,1)}, bf16[2,48,1920]{2,1,0:T(8,128)(2,1)}, u32[]{:S(2)}, u32[]{:S(2)}) collective-permute-start(bf16[2,48,1920]{2,1,0:T(8,128)(2,1)} %get-tuple-element.679), channel_id=1, source_target_pairs={{0,8},{4,12},{8,0},{12,4},{1,9},{5,13},{9,1},{13,5},{2,10},{6,14},... | collective-permute-start | bytes 1105928 | tf_op jit(solution)/shard_map/ppermute | solution.py:184
  388.8 33.1 %collective-permute-start.50 = (bf16[4,96,3840]{2,1,0:T(8,128)(2,1)}, bf16[4,96,3840]{2,1,0:T(8,128)(2,1)}, u32[]{:S(2)}, u32[]{:S(2)}) collective-permute-start(bf16[4,96,3840]{2,1,0:T(8,128)(2,1)} %get-tuple-element.715), channel_id=1, source_target_pairs={{0,1},{1,0},{2,3},{3,2},{4,5},{5,4},{6,7},{7,6},{8,9},{9,8},{10,11... | collective-permute-start | bytes 8847368 | tf_op jit(solution)/shard_map/ppermute | solution.py:184
  392.6 29.3 %collective-permute-start.48 = (bf16[2,2,192,384]{3,2,1,0:T(8,128)(2,1)S(1)}, bf16[2,2,192,384]{3,2,1,0:T(8,128)(2,1)S(1)}, u32[]{:S(2)}, u32[]{:S(2)}) collective-permute-start(bf16[2,2,192,384]{3,2,1,0:T(8,128)(2,1)S(1)} %get-tuple-element.713), channel_id=1, source_target_pairs={{0,16},{16,0},{1,17},{17,1},{2,18},{18,2},{3,19},{19,3},{4,20},{20... | collective-permute-start | bytes 1769480 | tf_op jit(solution)/shard_map/ppermute | solution.py:184
  394.1 27.8 %collective-permute-start.49 = (bf16[2,192,768]{2,1,0:T(8,128)(2,1)S(1)}, bf16[2,192,768]{2,1,0:T(8,128)(2,1)S(1)}, u32[]{:S(2)}, u32[]{:S(2)}) collective-permute-start(bf16[2,192,768]{2,1,0:T(8,128)(2,1)S(1)} %get-tuple-element.714), channel_id=1, source_target_pairs={{0,2},{1,3},{2,0},{3,1},{4,6},{5,7},{6,4},{7,5},{8,10},{9,11},{10,... | collective-permute-start | bytes 1769480 | tf_op jit(solution)/shard_map/ppermute | solution.py:184
  424.8 23.9 %collective-permute-start.54 = (bf16[2,2,48,1920]{3,2,1,0:T(8,128)(2,1)}, bf16[2,2,48,1920]{3,2,1,0:T(8,128)(2,1)}, u32[]{:S(2)}, u32[]{:S(2)}) collective-permute-start(bf16[2,2,48,1920]{3,2,1,0:T(8,128)(2,1)} %get-tuple-element.751), channel_id=1, source_target_pairs={{0,16},{16,0},{1,17},{17,1},{2,18},{18,2},{3,19},{19,3},{4,20},{20... | collective-permute-start | bytes 2211848 | tf_op jit(solution)/shard_map/ppermute | solution.py:184
  425.5 23.2 %collective-permute-start.55 = (bf16[2,48,3840]{2,1,0:T(8,128)(2,1)}, bf16[2,48,3840]{2,1,0:T(8,128)(2,1)}, u32[]{:S(2)}, u32[]{:S(2)}) collective-permute-start(bf16[2,48,3840]{2,1,0:T(8,128)(2,1)} %get-tuple-element.752), channel_id=1, source_target_pairs={{0,2},{1,3},{2,0},{3,1},{4,6},{5,7},{6,4},{7,5},{8,10},{9,11},{10,... | collective-permute-start | bytes 2211848 | tf_op jit(solution)/shard_map/ppermute | solution.py:184
  448.7 31.9 %collective-permute-start.60 = (bf16[4,96,2304]{2,1,0:T(8,128)(2,1)}, bf16[4,96,2304]{2,1,0:T(8,128)(2,1)}, u32[]{:S(2)}, u32[]{:S(2)}) collective-permute-start(bf16[4,96,2304]{2,1,0:T(8,128)(2,1)} %copy-done.109), channel_id=1, source_target_pairs={{0,1},{1,0},{2,3},{3,2},{4,5},{5,4},{6,7},{7,6},{8,9},{9,8},{10,11... | collective-permute-start | bytes 5308424 | tf_op jit(solution)/shard_map/ppermute | solution.py:184
  453.7 26.9 %collective-permute-start.58 = (bf16[2,48,1920]{2,1,0:T(8,128)(2,1)S(1)}, bf16[2,48,1920]{2,1,0:T(8,128)(2,1)S(1)}, u32[]{:S(2)}, u32[]{:S(2)}) collective-permute-start(bf16[2,48,1920]{2,1,0:T(8,128)(2,1)S(1)} %get-tuple-element.783), channel_id=1, source_target_pairs={{0,2},{1,3},{2,0},{3,1},{4,6},{5,7},{6,4},{7,5},{8,10},{9,11},{10,... | collective-permute-start | bytes 1105928 | tf_op jit(solution)/shard_map/ppermute | solution.py:184
  455.0 25.6 %collective-permute-start.59 = (bf16[2,48,1920]{2,1,0:T(8,128)(2,1)S(1)}, bf16[2,48,1920]{2,1,0:T(8,128)(2,1)S(1)}, u32[]{:S(2)}, u32[]{:S(2)}) collective-permute-start(bf16[2,48,1920]{2,1,0:T(8,128)(2,1)S(1)} %get-tuple-element.784), channel_id=1, source_target_pairs={{0,16},{16,0},{1,17},{17,1},{2,18},{18,2},{3,19},{19,3},{4,20},{20... | collective-permute-start | bytes 1105928 | tf_op jit(solution)/shard_map/ppermute | solution.py:184
  560.4 23.8 %collective-permute-start.81 = (bf16[2,48,3072]{2,1,0:T(8,128)(2,1)S(1)}, bf16[2,48,3072]{2,1,0:T(8,128)(2,1)S(1)}, u32[]{:S(2)}, u32[]{:S(2)}) collective-permute-start(bf16[2,48,3072]{2,1,0:T(8,128)(2,1)S(1)} %pad_maximum_fusion.2.refs_0_), channel_id=1, source_target_pairs={{0,1},{1,0},{2,3},{3,2},{4,5},{5,4},{6,7},{7,6},{8,9},{9,8},{10,11... | collective-permute-start | bytes 1769480 | tf_op jit(solution)/shard_map/ppermute | solution.py:184
  (203 other events, 2059.4 us)
Sparse Core Ops, SparseCore 0:
  11.1 33.9 all-gather.8
  47.2 29.5 all-gather.10
  78.9 29.5 all-gather.12
  552.4 26.2 all-gather.14
